TPU v7x, 32 devices: a whole 2x2x4 slice. The times are simulated.
32 devices in a mesh: dp: 16 (over z, x, core), seq: 2 (over y).
Axes of the slice: x: 2, y: 2, z: 4, core: 2. Of those that a mesh axis runs over, the one named last changes fastest.
Arguments:
- tokens: bfloat16 [16, 1024, 1024], P('dp', 'seq'), may hold values from -6 to 6
- time_index: int32 [16], P('dp'), may hold values from 0 to 999
- lengths: int32 [16], P('dp'), may hold values from 32 to 1024, as said below
- time_weight: bfloat16 [1024, 4096], replicated, may hold values from -0.09375 to 0.09375
- time_bias: float32 [4096], replicated, may hold values from -3 to 3
- attend_gain: float32 [1024], replicated, may hold values from 0.25 to 1.75
- query_key_value_weight: bfloat16 [1024, 3072], replicated, may hold values from -0.1875 to 0.1875
- attention_output_weight: bfloat16 [1024, 1024], replicated, may hold values from -1 to 1
- attend_bias: float32 [1024], replicated, may hold values from -3 to 3
- dense_gain: float32 [1024], replicated, may hold values from 0.25 to 1.75
- feedforward_up_matrix: bfloat16 [1024, 4096], replicated, may hold values from -0.1875 to 0.1875
- up_bias: float32 [4096], replicated, may hold values from -3 to 3
- feedforward_down_matrix: bfloat16 [4096, 1024], replicated, may hold values from -0.09375 to 0.09375
- down_bias: float32 [1024], replicated, may hold values from -3 to 3
- cotangent: bfloat16 [16, 1024, 1024], P('dp', 'seq'), may hold values from -6 to 6
Outputs:
- result: bfloat16 [16, 1024, 1024], P('dp', 'seq')
- gradient_tokens: bfloat16 [16, 1024, 1024], P('dp', 'seq')
- gradient_time_weight: float32 [1024, 4096], P('dp')
- gradient_time_bias: float32 [4096], P('dp')
- gradient_attend_gain: float32 [1024], P('dp')
- gradient_attend_in: float32 [1024, 3072], P('dp')
- gradient_attend_out: float32 [1024, 1024], P('dp')
- gradient_attend_bias: float32 [1024], P('dp')
- gradient_dense_gain: float32 [1024], P('dp')
- gradient_up_weight: float32 [1024, 4096], P('dp')
- gradient_up_bias: float32 [4096], P('dp')
- gradient_down_weight: float32 [4096, 1024], P('dp')
- gradient_down_bias: float32 [1024], P('dp')
Inputs may be any that keep to these rules, and one draw needn't show every extreme that they name: A sequence's live tokens are its first lengths slots; in every draw some sequence has all 1024 slots live.
All inputs are finite; a program needn't handle non-finite values.
Results may differ from a plain program's by a relative error of at most 0.024.
Values may be sent and summed in bfloat16 or wider, within the bound.
No kernel may reach another device: no remote copies, remote signals or barrier semaphores. Data moves between devices by JAX's collectives and lax.ppermute only.
A program may use at most 256 MiB of HBM per device.

v0:
```python
import math

import jax
import jax.numpy as jnp
from jax import lax
from jax.sharding import PartitionSpec as P

HD = 64


epsilon = 1e-05
masked_score = -1e30


def sinus_table(time_index, width):
    halfway = width // 2
    rates = jnp.exp(-math.log(10000.0) * jnp.arange(halfway, dtype=jnp.float32) / halfway)
    angles = time_index.astype(jnp.float32)[:, None] * rates[None, :]
    return jnp.concatenate([jnp.sin(angles), jnp.cos(angles)], axis=-1)


def normalize(values):
    centre = values - jnp.mean(values, axis=-1, keepdims=True)
    inverse = lax.rsqrt(jnp.mean(centre * centre, axis=-1, keepdims=True) + epsilon)
    return (centre * inverse, inverse)


def split_condition(condition):
    width = condition.shape[-1] // 4
    first = condition[:, None, 0:width]
    second = condition[:, None, width : 2 * width]
    third = condition[:, None, 2 * width : 3 * width]
    fourth = condition[:, None, 3 * width : 4 * width]
    return (first, second, third, fourth)


def score_block(queries, keyset, length):
    scores = jnp.einsum(
        "qhd,khd->hqk", queries, keyset, preferred_element_type=jnp.float32
    ) * HD ** (-0.5)
    usable = jnp.arange(queries.shape[0]) < length
    return jnp.where(usable[None, None, :], scores, masked_score)


def attend_forward(packet):
    heads_block, length = packet
    seq_rows = heads_block.shape[0]
    queries = heads_block[:, 0].reshape(seq_rows, -1, HD)
    keyset = heads_block[:, 1].reshape(seq_rows, -1, HD)
    valueset = heads_block[:, 2].reshape(seq_rows, -1, HD)
    scores = score_block(queries, keyset, length)
    highest = jnp.max(scores, axis=-1, keepdims=True)
    weights = jnp.exp(scores - highest)
    totals = jnp.sum(weights, axis=-1, keepdims=True)
    probability = weights / totals
    attention_mixture = jnp.einsum(
        "hqk,khd->qhd",
        probability.astype(jnp.bfloat16),
        valueset,
        preferred_element_type=jnp.float32,
    )
    return (
        attention_mixture.astype(jnp.bfloat16).reshape(seq_rows, -1),
        (highest + jnp.log(totals))[..., 0],
    )


def attend_backward(packet):
    heads_block, grad_heads, logsum, length = packet
    seq_rows = heads_block.shape[0]
    queries = heads_block[:, 0].reshape(seq_rows, -1, HD)
    keyset = heads_block[:, 1].reshape(seq_rows, -1, HD)
    valueset = heads_block[:, 2].reshape(seq_rows, -1, HD)
    scores = score_block(queries, keyset, length)
    probability = jnp.exp(scores - logsum[..., None])
    prob_low = probability.astype(jnp.bfloat16)
    upstream = grad_heads.reshape(seq_rows, -1, HD)
    grad_prob = jnp.einsum("qhd,khd->hqk", upstream, valueset, preferred_element_type=jnp.float32)
    inner_sum = jnp.sum(grad_prob * probability, axis=-1, keepdims=True)
    grad_score = (probability * (grad_prob - inner_sum)).astype(jnp.bfloat16)
    factor = HD ** (-0.5)
    grad_query = (
        jnp.einsum("hqk,khd->qhd", grad_score, keyset, preferred_element_type=jnp.float32) * factor
    )
    grad_keyset = (
        jnp.einsum("hqk,qhd->khd", grad_score, queries, preferred_element_type=jnp.float32) * factor
    )
    grad_valueset = jnp.einsum(
        "hqk,qhd->khd", prob_low, upstream, preferred_element_type=jnp.float32
    )
    stacked = jnp.stack([grad_query, grad_keyset, grad_valueset], axis=1).astype(jnp.bfloat16)
    return stacked.reshape(seq_rows, 3, -1)


def norm_back(incoming, normal, inverse, gain, scaling):
    lifted = 1.0 + scaling
    grad_gain = jnp.sum(incoming * normal * lifted, axis=(0, 1))
    grad_scaling = jnp.sum(incoming * normal * gain, axis=1)
    grad_shift = jnp.sum(incoming, axis=1)
    weighted = incoming * gain * lifted
    grad_input = inverse * (
        weighted
        - jnp.mean(weighted, axis=-1, keepdims=True)
        - normal * jnp.mean(weighted * normal, axis=-1, keepdims=True)
    )
    return (grad_input, grad_gain, grad_scaling, grad_shift)


def forward_pass(
    features,
    condition,
    live_rows,
    lengths,
    attend_gain,
    query_key_value_weight,
    attention_output_weight,
    attend_bias,
    dense_gain,
    feedforward_up_matrix,
    up_bias,
    feedforward_down_matrix,
    down_bias,
):
    scale_attend, shift_attend, scale_dense, shift_dense = split_condition(condition)
    normal_one, inverse_one = normalize(features)
    attention_activation = (normal_one * attend_gain * (1.0 + scale_attend) + shift_attend).astype(
        jnp.bfloat16
    )
    projected = jnp.einsum(
        "oxj,jb->oxb",
        attention_activation,
        query_key_value_weight,
        preferred_element_type=jnp.float32,
    ).astype(jnp.bfloat16)
    packed = projected.reshape(projected.shape[0], projected.shape[1], 3, -1)
    by_heads = lax.all_to_all(packed, "seq", split_axis=3, concat_axis=1, tiled=True)
    mixture_heads, logsum = lax.map(attend_forward, (by_heads, lengths))
    attention_mixture = lax.all_to_all(
        mixture_heads, "seq", split_axis=1, concat_axis=2, tiled=True
    )
    attended = (
        jnp.einsum(
            "oxj,jb->oxb",
            attention_mixture,
            attention_output_weight,
            preferred_element_type=jnp.float32,
        )
        + attend_bias
    )
    residual = features + live_rows * attended
    normal_two, inverse_two = normalize(residual)
    dense_activation = (normal_two * dense_gain * (1.0 + scale_dense) + shift_dense).astype(
        jnp.bfloat16
    )
    raised = (
        jnp.einsum(
            "pov,vj->poj",
            dense_activation,
            feedforward_up_matrix,
            preferred_element_type=jnp.float32,
        )
        + up_bias
    )
    hidden_state = jax.nn.gelu(raised, approximate=False).astype(jnp.bfloat16)
    branch = (
        jnp.einsum(
            "hgw,wr->hgr", hidden_state, feedforward_down_matrix, preferred_element_type=jnp.float32
        )
        + down_bias
    )
    output = residual + live_rows * branch
    return (
        normal_one,
        inverse_one,
        attention_activation,
        by_heads,
        logsum,
        attention_mixture,
        normal_two,
        inverse_two,
        dense_activation,
        raised,
        hidden_state,
        output,
    )


def gelu_exact(values):
    return jax.nn.gelu(values, approximate=False)


def body(
    tokens,
    time_index,
    lengths,
    time_weight,
    time_bias,
    attend_gain,
    query_key_value_weight,
    attention_output_weight,
    attend_bias,
    dense_gain,
    feedforward_up_matrix,
    up_bias,
    feedforward_down_matrix,
    down_bias,
    cotangent,
):
    features = tokens.astype(jnp.float32)
    seq_count = tokens.shape[0]
    local_rows = tokens.shape[1]
    table_low = sinus_table(time_index, time_weight.shape[0]).astype(jnp.bfloat16)
    condition = jnp.dot(table_low, time_weight, preferred_element_type=jnp.float32) + time_bias
    positions = lax.axis_index("seq") * local_rows + jnp.arange(local_rows)
    live_rows = (positions[None, :] < lengths[:, None]).astype(jnp.float32)[:, :, None]
    saved = forward_pass(
        features,
        condition,
        live_rows,
        lengths,
        attend_gain,
        query_key_value_weight,
        attention_output_weight,
        attend_bias,
        dense_gain,
        feedforward_up_matrix,
        up_bias,
        feedforward_down_matrix,
        down_bias,
    )
    result = saved[11].astype(jnp.bfloat16)
    barrier_out = lax.optimization_barrier((features, result))
    saved = forward_pass(
        barrier_out[0],
        condition,
        live_rows,
        lengths,
        attend_gain,
        query_key_value_weight,
        attention_output_weight,
        attend_bias,
        dense_gain,
        feedforward_up_matrix,
        up_bias,
        feedforward_down_matrix,
        down_bias,
    )
    (
        normal_one,
        inverse_one,
        attention_activation,
        by_heads,
        logsum,
        attention_mixture,
        normal_two,
        inverse_two,
        dense_activation,
        raised,
        hidden_state,
        output,
    ) = saved
    scale_attend, shift_attend, scale_dense, shift_dense = split_condition(condition)
    incoming = cotangent.astype(jnp.float32)
    gradient_dense_output = (live_rows * incoming).astype(jnp.bfloat16)
    grad_down_weight = jnp.einsum(
        "thx,thp->xp", hidden_state, gradient_dense_output, preferred_element_type=jnp.float32
    )
    grad_down_bias = jnp.sum(gradient_dense_output.astype(jnp.float32), axis=(0, 1))
    grad_hidden = jnp.einsum(
        "okn,qn->okq",
        gradient_dense_output,
        feedforward_down_matrix,
        preferred_element_type=jnp.float32,
    )
    activated, gelu_pull = jax.vjp(gelu_exact, raised)
    gradient_expanded_hidden = gelu_pull(grad_hidden)[0].astype(jnp.bfloat16)
    grad_up_weight = jnp.einsum(
        "twm,twu->mu",
        dense_activation,
        gradient_expanded_hidden,
        preferred_element_type=jnp.float32,
    )
    grad_up_bias = jnp.sum(gradient_expanded_hidden.astype(jnp.float32), axis=(0, 1))
    grad_act_dense = jnp.einsum(
        "qoy,by->qob",
        gradient_expanded_hidden,
        feedforward_up_matrix,
        preferred_element_type=jnp.float32,
    )
    grad_from_two, grad_dense_gain, grad_scale_dense, grad_shift_dense = norm_back(
        grad_act_dense, normal_two, inverse_two, dense_gain, scale_dense
    )
    grad_residual = incoming + grad_from_two
    gradient_attention_output = (live_rows * grad_residual).astype(jnp.bfloat16)
    grad_attend_out = jnp.einsum(
        "hym,hyb->mb",
        attention_mixture,
        gradient_attention_output,
        preferred_element_type=jnp.float32,
    )
    grad_attend_bias = jnp.sum(gradient_attention_output.astype(jnp.float32), axis=(0, 1))
    grad_mixture = jnp.einsum(
        "ocg,wg->ocw",
        gradient_attention_output,
        attention_output_weight,
        preferred_element_type=jnp.float32,
    ).astype(jnp.bfloat16)
    grad_heads = lax.all_to_all(grad_mixture, "seq", split_axis=2, concat_axis=1, tiled=True)
    grad_qkv_heads = lax.map(attend_backward, (by_heads, grad_heads, logsum, lengths))
    grad_qkv = lax.all_to_all(grad_qkv_heads, "seq", split_axis=1, concat_axis=3, tiled=True)
    gradient_projection_input = grad_qkv.reshape(seq_count, local_rows, -1)
    grad_attend_in = jnp.einsum(
        "hym,hyb->mb",
        attention_activation,
        gradient_projection_input,
        preferred_element_type=jnp.float32,
    )
    grad_act_attend = jnp.einsum(
        "ocg,wg->ocw",
        gradient_projection_input,
        query_key_value_weight,
        preferred_element_type=jnp.float32,
    )
    grad_from_one, grad_attend_gain, grad_scale_attend, grad_shift_attend = norm_back(
        grad_act_attend, normal_one, inverse_one, attend_gain, scale_attend
    )
    gradient_tokens = (grad_residual + grad_from_one).astype(jnp.bfloat16)
    grad_condition = jnp.concatenate(
        [grad_scale_attend, grad_shift_attend, grad_scale_dense, grad_shift_dense], axis=-1
    )
    grad_time_weight = jnp.dot(
        table_low.astype(jnp.float32).T, grad_condition, precision=lax.Precision.HIGHEST
    )
    grad_time_bias = jnp.sum(grad_condition, axis=0)
    all_parts = (
        lax.psum_scatter(
            grad_time_weight.astype(jnp.bfloat16), "dp", scatter_dimension=0, tiled=True
        ).astype(jnp.float32),
        lax.psum_scatter(
            grad_attend_in.astype(jnp.bfloat16), "dp", scatter_dimension=0, tiled=True
        ).astype(jnp.float32),
        lax.psum_scatter(
            grad_attend_out.astype(jnp.bfloat16), "dp", scatter_dimension=0, tiled=True
        ).astype(jnp.float32),
        lax.psum_scatter(
            grad_up_weight.astype(jnp.bfloat16), "dp", scatter_dimension=0, tiled=True
        ).astype(jnp.float32),
        lax.psum_scatter(
            grad_down_weight.astype(jnp.bfloat16), "dp", scatter_dimension=0, tiled=True
        ).astype(jnp.float32),
        lax.psum_scatter(
            grad_time_bias.astype(jnp.bfloat16), "dp", scatter_dimension=0, tiled=True
        ).astype(jnp.float32),
        lax.psum_scatter(
            grad_attend_gain.astype(jnp.bfloat16), "dp", scatter_dimension=0, tiled=True
        ).astype(jnp.float32),
        lax.psum_scatter(
            grad_attend_bias.astype(jnp.bfloat16), "dp", scatter_dimension=0, tiled=True
        ).astype(jnp.float32),
        lax.psum_scatter(
            grad_dense_gain.astype(jnp.bfloat16), "dp", scatter_dimension=0, tiled=True
        ).astype(jnp.float32),
        lax.psum_scatter(
            grad_up_bias.astype(jnp.bfloat16), "dp", scatter_dimension=0, tiled=True
        ).astype(jnp.float32),
        lax.psum_scatter(
            grad_down_bias.astype(jnp.bfloat16), "dp", scatter_dimension=0, tiled=True
        ).astype(jnp.float32),
    )
    all_sums = (
        lax.psum(all_parts[0].astype(jnp.bfloat16), "seq").astype(jnp.float32),
        lax.psum(all_parts[1].astype(jnp.bfloat16), "seq").astype(jnp.float32),
        lax.psum(all_parts[2].astype(jnp.bfloat16), "seq").astype(jnp.float32),
        lax.psum(all_parts[3].astype(jnp.bfloat16), "seq").astype(jnp.float32),
        lax.psum(all_parts[4].astype(jnp.bfloat16), "seq").astype(jnp.float32),
        lax.psum(all_parts[5].astype(jnp.bfloat16), "seq").astype(jnp.float32),
        lax.psum(all_parts[6].astype(jnp.bfloat16), "seq").astype(jnp.float32),
        lax.psum(all_parts[7].astype(jnp.bfloat16), "seq").astype(jnp.float32),
        lax.psum(all_parts[8].astype(jnp.bfloat16), "seq").astype(jnp.float32),
        lax.psum(all_parts[9].astype(jnp.bfloat16), "seq").astype(jnp.float32),
        lax.psum(all_parts[10].astype(jnp.bfloat16), "seq").astype(jnp.float32),
    )
    joined = all_sums[0:5]
    vector_sums = all_sums[5:11]
    return (
        result,
        gradient_tokens,
        joined[0],
        vector_sums[0],
        vector_sums[1],
        joined[1],
        joined[2],
        vector_sums[2],
        vector_sums[3],
        joined[3],
        vector_sums[4],
        joined[4],
        vector_sums[5],
    )


def solution(mesh):
    placed = (
        P("dp", "seq", None),
        P("dp"),
        P("dp"),
        P(),
        P(),
        P(),
        P(),
        P(),
        P(),
        P(),
        P(),
        P(),
        P(),
        P(),
        P("dp", "seq", None),
    )
    return jax.shard_map(
        body,
        mesh=mesh,
        in_specs=placed,
        out_specs=(
            P("dp", "seq", None),
            P("dp", "seq", None),
            P("dp", None),
            P("dp"),
            P("dp"),
            P("dp", None),
            P("dp", None),
            P("dp"),
            P("dp"),
            P("dp", None),
            P("dp"),
            P("dp", None),
            P("dp"),
        ),
        check_vma=False,
    )
```

profile of v0, /device:TPU:0, one launch (start us, length us, event | category | flops | bytes accessed | tf_op | source)
XLA Modules:
  0.0 1160.1 jit_solution(13196064970354953051)
XLA Ops:
  12.2 4.7 fusion.162
  17.5 5.2 convolution_convert_fusion.4
  27.4 6.6 copy.99
  33.9 5.8 all-to-all-start
  40.4 48.2 %all-to-all-done = bf16[1,512,3,1024]{1,2,0,3:T(4,128)(2,1)} async-done(((bf16[1,512,3,1024]{1,2,0,3:T(4,128)(2,1)}), bf16[1,512,3,1024]{1,2,0,3:T(4,128)(2,1)}, u32[]{:S(2)}, u32[]{:S(2)}) %all-to-all-start) | async-done | bytes 3145760 | tf_op jit(solution)/shard_map/all_to_all | solution.py:136
  93.2 4.7 copy.101
  108.3 19.0 %fusion.157 = (f32[8,1024]{1,0:T(8,128)S(1)}, f32[8,1024,1024]{1,2,0:T(8,128)}) fusion(pred[1024]{0:T(1024)(128)(4,1)S(1)} %iota_compare_fusion, bf16[1024,8,64]{0,2,1:T(8,128)(2,1)} %bitcast.214, bf16[1024,8,64]{0,2,1:T(8,128)(2,1)} %bitcast.213), kind=kOutput, calls=%fused_computation.228 | convolution fusion | flops 1107297280 | bytes 35685376 | tf_op jit(solution)/shard_map/while/body/eval_jaxpr/sub | solution.py:53
  127.3 13.4 %fusion.78 = bf16[8,64,1024]{2,1,0:T(8,128)(2,1)} fusion(bf16[1024,8,64]{0,2,1:T(8,128)(2,1)} %bitcast.215, f32[8,1024,1024]{1,2,0:T(8,128)} %get-tuple-element.104, f32[8,1024]{1,0:T(8,128)S(1)} %get-tuple-element.103), kind=kOutput, calls=%fused_computation.143 | convolution fusion | flops 1091043328 | bytes 35684352 | tf_op jit(solution)/shard_map/while/body/eval_jaxpr/hqk,khd->qhd/dot_general | solution.py:56
  140.8 6.3 copy.106
  147.6 9.0 reduce.24
  165.3 11.8 %all-to-all-done.1 = bf16[2,2,131072]{2,1,0:T(2,128)(2,1)} async-done(((bf16[2,2,131072]{2,1,0:T(2,128)(2,1)}), bf16[2,2,131072]{2,1,0:T(2,128)(2,1)}, u32[]{:S(2)}, u32[]{:S(2)}) %all-to-all-start.1) | async-done | bytes 1048608 | tf_op jit(solution)/shard_map/all_to_all | solution.py:138
  189.6 33.3 %fusion.71 = bf16[1,512,1024]{2,1,0:T(8,128)(2,1)} fusion(f32[1,512,1024]{2,1,0:T(8,128)} %copy-done.5, bf16[4096,1024]{1,0:T(8,128)(2,1)} %param.27, bf16[1024,4096]{1,0:T(8,128)(2,1)} %param.25, f32[4096]{0:T(1024)S(1)} %copy-done.31, f32[1024]{0:T(1024)S(1)} %copy-done.32, f32[1024]{0:T(1024)S(1)} %bitcast.234, f32[1024]{0:T(1024)S(1)} %bitcast.226, ...), kind=kOutput, calls=%fused_computation.115 | convolution fusion | flops 8733589504 | bytes 19961856 | tf_op jit(solution)/shard_map/hgw,wr->hgr/dot_general | solution.py:166
  226.7 8.7 convolution_convert_fusion.3
  235.4 4.7 copy.108
  244.7 49.1 %all_to_all.90 = bf16[1,512,3,1024]{1,2,0,3:T(4,128)(2,1)S(1)} all-to-all(bf16[1,512,3,1024]{1,2,0,3:T(4,128)(2,1)S(1)} %copy.109), channel_id=1, replica_groups=mesh['dp'=16,'seq'=2] {'seq'}, dimensions={3} | all-to-all | bytes 6291456 | tf_op jit(solution)/shard_map/all_to_all | solution.py:136
  296.2 4.8 copy.111
  311.0 14.9 %fusion.159 = (f32[8,1024]{1,0:T(8,128)S(1)}, f32[8,1024,1024]{1,2,0:T(8,128)}) fusion(bf16[1024,8,64]{0,2,1:T(8,128)(2,1)} %bitcast.183, bf16[1024,8,64]{0,2,1:T(8,128)(2,1)S(1)} %bitcast.181, pred[1024]{0:T(1024)(128)(4,1)S(1)} %copy-done.27), kind=kOutput, calls=%fused_computation.230 | convolution fusion | flops 1098899456 | bytes 35685376 | tf_op jit(solution)/shard_map/while/body/eval_jaxpr/qhd,khd->hqk/dot_general | solution.py:38
  325.9 13.1 %fusion.1 = f32[8,1024]{1,0:T(8,128)S(1)} fusion(f32[8,1024,1024]{1,2,0:T(8,128)} %get-tuple-element.108, f32[8,1024]{1,0:T(8,128)S(1)} %get-tuple-element.107), kind=kLoop, calls=%fused_computation.10 | loop fusion | flops 16769024 | bytes 33619968 | tf_op jit(solution)/shard_map/while/body/eval_jaxpr/reduce_sum | solution.py:54
  339.0 13.6 %fusion.77 = bf16[8,64,1024]{2,1,0:T(8,128)(2,1)S(1)} fusion(bf16[1024,8,64]{0,2,1:T(8,128)(2,1)S(1)} %bitcast.199, f32[8,1024,1024]{1,2,0:T(8,128)} %get-tuple-element.108, f32[8,1024]{1,0:T(8,128)S(1)} %fusion.1, f32[8,1024]{1,0:T(8,128)S(1)} %get-tuple-element.107), kind=kOutput, calls=%fused_computation.142 | convolution fusion | flops 1099431936 | bytes 35717120 | tf_op jit(solution)/shard_map/while/body/eval_jaxpr/hqk,khd->qhd/dot_general | solution.py:56
  357.1 8.0 reduce.25
  366.7 15.2 %all_to_all.91 = bf16[2,2,131072]{2,1,0:T(2,128)(2,1)S(1)} all-to-all(bf16[2,2,131072]{2,1,0:T(2,128)(2,1)} %reshape.579), channel_id=1, replica_groups=mesh['dp'=16,'seq'=2] {'seq'}, dimensions={0} | all-to-all | bytes 2097152 | tf_op jit(solution)/shard_map/all_to_all | solution.py:138
  390.7 27.1 %fusion.15 = (f32[512,4096]{1,0:T(8,128)}, f32[512,4096]{1,0:T(8,128)}) fusion(f32[4096]{0:T(1024)S(1)} %copy-done.31, bf16[1024,4096]{1,0:T(8,128)(2,1)} %param.25, f32[1,512,1024]{2,1,0:T(8,128)S(1)} %get-tuple-element.110, f32[512]{0:T(512)S(1)} %add_rsqrt_fusion, f32[512]{0:T(512)S(1)} %broadcast_multiply_fusion.4, f32[1024]{0:T(1024)S(1)} %bitcast.235, ...), kind=kOutput, calls=%fused_computation.26 | convolution fusion | flops 4430233600 | bytes 27295744 | tf_op jit(solution)/shard_map/pov,vj->poj/dot_general | solution.py:156
  417.8 13.6 %fusion.161 = (bf16[4096]{0:T(1024)(128)(2,1)S(1)}, bf16[512,4096]{1,0:T(8,128)(2,1)S(1)}) fusion(f32[512,4096]{1,0:T(8,128)} %get-tuple-element.111, bf16[4096,1024]{1,0:T(8,128)(2,1)} %param.27, bf16[1,512,1024]{2,1,0:T(8,128)(2,1)S(1)} %copy-done.8, f32[512]{0:T(512)S(1)} %fusion.109, f32[512,4096]{1,0:T(8,128)} %get-tuple-element.112, ...), kind=kOutput, calls=%fused_computation.232 | convolution fusion | flops 4330090496 | bytes 30435328 | tf_op jit(solution)/shard_map/okn,qn->okq/dot_general | solution.py:269
  431.4 9.3 multiply_reduce_fusion.1
  449.8 8.0 reduce.26
  467.7 5.9 all-to-all-done.4
  481.2 14.8 %fusion.74 = bf16[8,64,1024]{2,1,0:T(8,128)(2,1)} fusion(bf16[1024,8,64]{0,2,1:T(8,128)(2,1)S(1)} %reshape.566, f32[8,1024,1024]{1,2,0:T(8,128)} %get-tuple-element.108, f32[8,1024]{1,0:T(8,128)S(1)} %log_add_fusion), kind=kOutput, calls=%fused_computation.140 | convolution fusion | flops 1091043328 | bytes 35684352 | tf_op jit(solution)/shard_map/while/body/eval_jaxpr/hqk,qhd->khd/dot_general | solution.py:88
  496.1 22.5 %multiply_reduce_fusion = (f32[8,1024]{1,0:T(8,128)S(1)}, f32[8,1024,1024]{1,2,0:T(8,128)}) fusion(f32[8,1024,1024]{1,2,0:T(8,128)} %get-tuple-element.108, f32[8,1024]{1,0:T(8,128)S(1)} %log_add_fusion, bf16[1024,8,64]{0,2,1:T(8,128)(2,1)S(1)} %reshape.566, bf16[1024,8,64]{0,2,1:T(8,128)(2,1)} %bitcast.198), kind=kOutput, calls=%fused_computation.2 | convolution fusion | flops 1098899456 | bytes 69271552 | tf_op jit(solution)/shard_map/while/body/eval_jaxpr/qhd,khd->hqk/dot_general | solution.py:78
  518.6 28.4 %multiply_convert_fusion = bf16[8,1024,1024]{1,2,0:T(8,128)(2,1)} fusion(f32[8,1024,1024]{1,2,0:T(8,128)} %get-tuple-element.115, f32[8,1024,1024]{1,2,0:T(8,128)} %get-tuple-element.108, f32[8,1024]{1,0:T(8,128)S(1)} %get-tuple-element.114, f32[8,1024]{1,0:T(8,128)S(1)} %log_add_fusion), kind=kLoop, calls=%fused_computation.1 | loop fusion | flops 33554432 | bytes 83951616 | tf_op jit(solution)/shard_map/while/body/eval_jaxpr/convert_element_type | solution.py:80
  547.0 12.3 %multiply_convert_fusion.4 = bf16[8,64,1024]{2,1,0:T(8,128)(2,1)} fusion(bf16[1024,8,64]{0,2,1:T(8,128)(2,1)} %bitcast.184, bf16[8,1024,1024]{1,2,0:T(8,128)(2,1)} %multiply_convert_fusion), kind=kOutput, calls=%fused_computation.122 | convolution fusion | flops 1074790400 | bytes 18874368 | tf_op jit(solution)/shard_map/while/body/eval_jaxpr/hqk,qhd->khd/dot_general | solution.py:86
  559.3 9.8 multiply_convert_fusion.5
  569.1 5.9 copy.125
  575.0 6.0 copy.124
  581.0 5.9 copy.123
  587.0 8.6 pad_maximum_fusion
  595.6 46.6 %all_to_all.92 = bf16[1,1024,3,512]{3,2,0,1:T(4,128)(2,1)S(1)} all-to-all(bf16[1,1024,3,512]{3,2,0,1:T(4,128)(2,1)S(1)} %pad_maximum_fusion), channel_id=1, replica_groups=mesh['dp'=16,'seq'=2] {'seq'}, dimensions={1} | all-to-all | bytes 6291456 | tf_op jit(solution)/shard_map/all_to_all | solution.py:310
  644.7 4.7 copy.127
  649.5 9.1 convolution_convert_fusion.2
  658.7 14.4 %convolution_convert_fusion = bf16[4096,1024]{1,0:T(8,128)(2,1)} fusion(f32[512,4096]{1,0:T(8,128)} %get-tuple-element.111, f32[512,4096]{1,0:T(8,128)} %get-tuple-element.112, f32[4096]{0:T(1024)S(1)} %copy-done.31, bf16[1,512,1024]{2,1,0:T(8,128)(2,1)S(1)} %copy-done.9, f32[512]{0:T(512)S(1)} %fusion.109), kind=kOutput, calls=%fused_computation.57 | convolution fusion | flops 4309123072 | bytes 26232832 | tf_op jit(solution)/shard_map/thx,thp->xp/dot_general | solution.py:265
  673.4 11.2 convolution_convert_fusion.1
  684.7 9.3 multiply_reduce_fusion.2
  695.8 5.2 multiply_convert_fusion.1
  701.1 41.9 %reduce-scatter.8.cloned.1.call-done = bf16[64,3072]{1,0:T(8,128)(2,1)} async-done(((bf16[1024,3072]{1,0:T(8,128)(2,1)}), bf16[64,3072]{1,0:T(8,128)(2,1)}) %reduce-scatter.8.cloned.1.call-update) | async-done | bytes 393232 | tf_op jit(solution)/shard_map/reduce_scatter | solution.py:339
  743.0 108.0 %reduce-scatter.14.cloned.1.call-done = bf16[256,1024]{1,0:T(8,128)(2,1)} async-done(((bf16[4096,1024]{1,0:T(8,128)(2,1)}), bf16[256,1024]{1,0:T(8,128)(2,1)}) %reduce-scatter.14.cloned.1.call-update) | async-done | bytes 524304 | tf_op jit(solution)/shard_map/reduce_scatter | solution.py:348
  851.0 108.4 %reduce-scatter.12.cloned.1.call-done = bf16[64,4096]{1,0:T(8,128)(2,1)} async-done(((bf16[1024,4096]{1,0:T(8,128)(2,1)}), bf16[64,4096]{1,0:T(8,128)(2,1)}) %reduce-scatter.12.cloned.1.call-update) | async-done | bytes 524304 | tf_op jit(solution)/shard_map/reduce_scatter | solution.py:345
  959.3 108.4 %reduce-scatter.6.cloned.1.call-done = bf16[64,4096]{1,0:T(8,128)(2,1)} async-done(((bf16[1024,4096]{1,0:T(8,128)(2,1)}), bf16[64,4096]{1,0:T(8,128)(2,1)}) %reduce-scatter.6.cloned.1.call-update) | async-done | bytes 524304 | tf_op jit(solution)/shard_map/reduce_scatter | solution.py:336
  1069.6 60.2 %all-reduce.6 = (bf16[4096]{0:T(1024)(128)(2,1)S(1)}, bf16[1024]{0:T(1024)(128)(2,1)S(1)}, bf16[1024]{0:T(1024)(128)(2,1)S(1)}, bf16[1024]{0:T(1024)(128)(2,1)S(...) all-reduce(bf16[4096]{0:T(1024)(128)(2,1)S(1)} %convert_element_typ, ...), channel_id=3, replica_groups=mesh['dp'=16,'seq'=2] {'dp'}, use_global_device_ids=true, to_apply=%region_23.24.clone | all-reduce | flops 12288 | bytes 49152
  1130.3 4.9 all-reduce.7
  (175 shorter events, 131.4 us)
Async XLA Ops:
  7.2 178.0 %copy-start = (bf16[1024,1024]{1,0:T(8,128)(2,1)S(1)}, bf16[1024,1024]{1,0:T(8,128)(2,1)}, u32[]{:S(2)}) copy-start(bf16[1024,1024]{1,0:T(8,128)(2,1)} %param.22) | copy-start | bytes 6291460
  8.0 8.9 copy-start.23
  8.1 9.5 copy-start.1
  8.1 9.5 copy-start.18
  8.1 9.5 slice-start
  12.2 5.4 slice-start.1
  16.9 0.6 copy-start.13
  16.9 5.8 copy-start.28
  33.9 54.7 %all-to-all-start = ((bf16[1,512,3,1024]{1,2,0,3:T(4,128)(2,1)}), bf16[1,512,3,1024]{1,2,0,3:T(4,128)(2,1)}, u32[]{:S(2)}, u32[]{:S(2)}) async-start(bf16[1,512,3,1024]{1,2,0,3:T(4,128)(2,1)} %copy.99), calls=%async_computation | async-start | bytes 8388608 | tf_op jit(solution)/shard_map/all_to_all | solution.py:136
  40.4 67.9 %copy-start.26 = (pred[1024]{0:T(1024)(128)(4,1)}, pred[1024]{0:T(1024)(128)(4,1)S(1)}, u32[]{:S(2)}) copy-start(pred[1024]{0:T(1024)(128)(4,1)S(1)} %iota_compare_fusion) | copy-start | bytes 3076
  156.6 28.6 %copy-start.11 = (f32[1024]{0:T(1024)S(1)}, f32[1024]{0:T(1024)}, u32[]{:S(2)}) copy-start(f32[1024]{0:T(1024)} %param.23) | copy-start | bytes 12292
  159.3 17.8 %all-to-all-start.1 = ((bf16[2,2,131072]{2,1,0:T(2,128)(2,1)}), bf16[2,2,131072]{2,1,0:T(2,128)(2,1)}, u32[]{:S(2)}, u32[]{:S(2)}) async-start(bf16[2,2,131072]{2,1,0:T(2,128)(2,1)} %reshape.577), calls=%async_computation.1 | async-start | bytes 2097152 | tf_op jit(solution)/shard_map/all_to_all | solution.py:138
  165.3 24.3 %copy-start.21 = (f32[1024]{0:T(1024)S(1)}, f32[1024]{0:T(1024)}, u32[]{:S(2)}) copy-start(f32[1024]{0:T(1024)} %param.24) | copy-start | bytes 12292
  165.3 24.3 %copy-start.31 = (f32[4096]{0:T(1024)S(1)}, f32[4096]{0:T(1024)}, u32[]{:S(2)}) copy-start(f32[4096]{0:T(1024)} %param.26) | copy-start | bytes 49156
  165.3 24.3 %copy-start.32 = (f32[1024]{0:T(1024)S(1)}, f32[1024]{0:T(1024)}, u32[]{:S(2)}) copy-start(f32[1024]{0:T(1024)} %param.28) | copy-start | bytes 12292
  187.8 1.4 copy-start.5
  189.6 37.1 %copy-start.14 = (f32[1,1024]{1,0:T(1,128)S(1)}, f32[1,1024]{1,0:T(1,128)}, u32[]{:S(2)}) copy-start(f32[1,1024]{1,0:T(1,128)} %copy-done.13) | copy-start | bytes 12292
  189.6 37.1 %copy-start.19 = (f32[1024]{0:T(1024)S(1)}, f32[1024]{0:T(1024)}, u32[]{:S(2)}) copy-start(f32[1024]{0:T(1024)} %param.20) | copy-start | bytes 12292
  189.6 37.1 %copy-start.29 = (f32[1,1024]{1,0:T(1,128)S(1)}, f32[1,1024]{1,0:T(1,128)}, u32[]{:S(2)}) copy-start(f32[1,1024]{1,0:T(1,128)} %copy-done.28) | copy-start | bytes 12292
  224.7 10.7 copy-start.16
  226.7 8.7 copy-start.24
  296.2 14.8 %copy-start.27 = (pred[1024]{0:T(1024)(128)(4,1)S(1)}, pred[1024]{0:T(1024)(128)(4,1)}, u32[]{:S(2)}) copy-start(pred[1024]{0:T(1024)(128)(4,1)} %copy-done.26) | copy-start | bytes 3076
  306.0 19.9 %copy-start.2 = (bf16[1024,1,512]{0,2,1:T(8,128)(2,1)}, bf16[1024,1,512]{0,2,1:T(8,128)(2,1)S(1)}, u32[]{:S(2)}) copy-start(bf16[1024,1,512]{0,2,1:T(8,128)(2,1)S(1)} %copy.114) | copy-start | bytes 3145732
  325.9 13.1 %copy-start.7 = (bf16[1024,1,512]{0,2,1:T(8,128)(2,1)S(1)}, bf16[1024,1,512]{0,2,1:T(8,128)(2,1)}, u32[]{:S(2)}) copy-start(bf16[1024,1,512]{0,2,1:T(8,128)(2,1)} %copy.112) | copy-start | bytes 3145732
  357.0 29.9 %copy-start.12 = (f32[1024]{0:T(1024)S(1)}, f32[1024]{0:T(1024)}, u32[]{:S(2)}) copy-start(f32[1024]{0:T(1024)} %param.23) | copy-start | bytes 12292
  390.3 50.9 %copy-start.6 = (f32[1,512,1024]{2,1,0:T(8,128)}, f32[1,512,1024]{2,1,0:T(8,128)S(1)}, u32[]{:S(2)}) copy-start(f32[1,512,1024]{2,1,0:T(8,128)S(1)} %get-tuple-element.110) | copy-start | bytes 6291460
  390.7 27.1 %copy-start.8 = (bf16[1,512,1024]{2,1,0:T(8,128)(2,1)S(1)}, bf16[1,512,1024]{2,1,0:T(8,128)(2,1)}, u32[]{:S(2)}) copy-start(bf16[1,512,1024]{2,1,0:T(8,128)(2,1)} %param.29) | copy-start | bytes 3145732
  431.4 9.4 copy-start.34
  443.6 1.0 copy-start.10
  459.4 14.1 %all-to-all-start.4 = ((bf16[2,2,131072]{2,1,0:T(2,128)(2,1)}), bf16[2,2,131072]{2,1,0:T(2,128)(2,1)S(1)}, u32[]{:S(2)}, u32[]{:S(2)}) async-start(bf16[2,2,131072]{2,1,0:T(2,128)(2,1)} %reshape.581), calls=%async_computation.4 | async-start | bytes 2097152 | tf_op jit(solution)/shard_map/all_to_all | solution.py:308
  463.0 238.1 %reduce-scatter.10.cloned.1.call-start = ((), (), s32[]{:S(2)}) async-start(), calls=%async_computation.13 | async-start | bytes 2228224 | tf_op jit(solution)/shard_map/reduce_scatter | solution.py:342
  467.6 275.4 %reduce-scatter.8.cloned.1.call-start = ((), (), s32[]{:S(2)}) async-start(), calls=%async_computation.12 | async-start | bytes 6684672 | tf_op jit(solution)/shard_map/reduce_scatter | solution.py:339
  547.0 12.4 %copy-start.3 = (bf16[1024,1,512]{0,2,1:T(8,128)(2,1)S(1)}, bf16[1024,1,512]{0,2,1:T(8,128)(2,1)}, u32[]{:S(2)}) copy-start(bf16[1024,1,512]{0,2,1:T(8,128)(2,1)} %copy-done.2) | copy-start | bytes 3145732
  642.2 7.2 copy-start.15
  642.2 7.2 copy-start.17
  642.2 7.2 copy-start.20
  642.2 7.2 copy-start.25
  642.2 7.2 copy-start.30
  649.4 9.2 copy-start.9
  658.6 192.3 %reduce-scatter.14.cloned.1.call-start = ((), (), s32[]{:S(2)}) async-start(), calls=%async_computation.15 | async-start | bytes 8912896 | tf_op jit(solution)/shard_map/reduce_scatter | solution.py:348
  673.1 286.2 %reduce-scatter.12.cloned.1.call-start = ((), (), s32[]{:S(2)}) async-start(), calls=%async_computation.14 | async-start | bytes 8912896 | tf_op jit(solution)/shard_map/reduce_scatter | solution.py:345
  684.6 11.1 copy-start.22
  684.6 383.1 %reduce-scatter.6.cloned.1.call-start = ((), (), s32[]{:S(2)}) async-start(), calls=%async_computation.11 | async-start | bytes 8912896 | tf_op jit(solution)/shard_map/reduce_scatter | solution.py:336
  694.0 1.4 copy-start.4
  695.8 372.0 %copy-start.33 = (u32[32]{0:T(128)S(1)}, u32[32]{0:T(128)}, u32[]{:S(2)}) copy-start(u32[32]{0:T(128)} %constant.159) | copy-start | bytes 388
  701.0 442.0 %all-reduce.11.cloned.1.call-start = ((), (), s32[]{:S(2)}) async-start(), calls=%async_computation.16 | async-start | bytes 4194304 | tf_op jit(solution)/shard_map/psum | solution.py:371
Sparse Core Ops, SparseCore 0:
  467.7 62.5 reduce-scatter.9
  658.7 84.2 reduce-scatter.7
  747.1 103.8 reduce-scatter.13
  854.9 104.4 reduce-scatter.11
  963.2 104.4 reduce-scatter.5
  1070.1 63.4 all-reduce.10
where the time goes:
time: 1170 us; the launch traced here: 1160 us
  waiting for transfers between devices  433 us (37%)
  matrix products  278 us (24%)
  blocking collectives  176 us (15%)
  local copies, waits for them, and re-layouts  130 us (11%)
  other arithmetic  111 us (9%)
  between operations  17.9 us (2%)
  starting transfers between devices  14.7 us (1%)
    reduce_scatter x1, waiting for transfers between devices, body(): lax.psum_scatter(grad_time_weight.astype(jnp.bfloat16), 'dp', scatter_dim...  108 us
    reduce_scatter x1, waiting for transfers between devices, body(): lax.psum_scatter(grad_up_weight.astype(jnp.bfloat16), 'dp', scatter_dimen...  108 us
    reduce_scatter x1, waiting for transfers between devices, body(): lax.psum_scatter(grad_down_weight.astype(jnp.bfloat16), 'dp', scatter_dim...  108 us
    unnamed x1, blocking collectives  60.2 us
    all_to_all x1, blocking collectives, forward_pass(): lax.all_to_all(packed, 'seq', split_axis=3, concat_axis=1, tiled=True)  49.1 us
    all_to_all x1, waiting for transfers between devices, forward_pass(): lax.all_to_all(packed, 'seq', split_axis=3, concat_axis=1, tiled=True)  48.2 us
    all_to_all x1, blocking collectives, body(): lax.all_to_all(grad_qkv_heads, 'seq', split_axis=1, concat_axis=3, tiled=...  46.6 us
    reduce_scatter x1, waiting for transfers between devices, body(): lax.psum_scatter(grad_attend_in.astype(jnp.bfloat16), 'dp', scatter_dimen...  41.9 us
  transfers between devices with their start and end apart: 9, of which 7 were waited for; matrix products, arithmetic and copies ran while one was open for 17% of the time, Pallas kernels for 0%

commit v1 on v0

v1 whole, which is shorter than its diff:
```python
import functools
import math

import jax
import jax.numpy as jnp
from jax import lax
from jax.experimental import pallas as pl
from jax.experimental.pallas import tpu as pltpu
from jax.sharding import PartitionSpec as P

HD = 64
EPS = 1e-05
MASKED = -1e30
EXP2_SCALE = math.log2(math.e) * HD ** (-0.5)
BF = jnp.bfloat16
F32 = jnp.float32
VMEM = 56 * 1024 * 1024


def sds(shape, dtype):
    return jax.ShapeDtypeStruct(shape, dtype)


def nt(a, b):
    return lax.dot_general(a, b, (((1,), (1,)), ((), ())), preferred_element_type=F32)


def nn(a, b):
    return jnp.dot(a, b, preferred_element_type=F32)


def tn_dot(a, b):
    return lax.dot_general(a, b, (((0,), (0,)), ((), ())), preferred_element_type=F32)


def call(kernel, name, scalars, grid, ins, in_specs, outs, out_specs, scratch=(), flops=0, aliases=None):
    size = lambda a: math.prod(a.shape) * a.dtype.itemsize
    return pl.pallas_call(
        kernel,
        name=name,
        grid_spec=pltpu.PrefetchScalarGridSpec(
            num_scalar_prefetch=len(scalars),
            grid=grid,
            in_specs=in_specs,
            out_specs=out_specs,
            scratch_shapes=list(scratch),
        ),
        out_shape=outs,
        input_output_aliases=aliases or {},
        compiler_params=pltpu.CompilerParams(
            vmem_limit_bytes=VMEM, dimension_semantics=("arbitrary",) * len(grid)
        ),
        cost_estimate=pl.CostEstimate(
            flops=int(flops),
            bytes_accessed=int(sum(map(size, ins)) + sum(map(size, jax.tree.leaves(outs)))),
            transcendentals=0,
        ),
    )(*scalars, *ins)


def norm_rows(v):
    centre = v - jnp.mean(v, axis=-1, keepdims=True)
    inverse = lax.rsqrt(jnp.mean(centre * centre, axis=-1, keepdims=True) + EPS)
    return centre * inverse, inverse


def live_column(rows, first, info_ref, local, total):
    r = first + lax.broadcasted_iota(jnp.int32, (rows, 1), 0)
    low = lax.rem(r, local)
    start = info_ref[1] - (r - low)
    slot = jnp.where(start < 0, start + total, start) + low
    return slot < info_ref[2]


def project_kernel(info_ref, x_ref, gain_ref, cond_ref, wq_ref, wk_ref, wv_ref, *rest):
    act_ref, qkv_ref = rest[-2:]
    normal, _ = norm_rows(x_ref[...].astype(F32))
    act = (normal * (gain_ref[...] * (1.0 + cond_ref[0:1, :])) + cond_ref[1:2, :]).astype(BF)
    act_ref[...] = act
    w = wq_ref.shape[1]
    for n, ref in enumerate((wq_ref, wk_ref, wv_ref)):
        qkv_ref[:, n * w : (n + 1) * w] = nn(act, ref[...]).astype(BF)


def project(info, x, first, total, gain, cond, weight, before=None):
    rows, width = x.shape
    block = min(256, rows)
    half = weight.shape[1] // 6
    skip = first // block
    weights = [pl.BlockSpec((width, half), lambda i, s, n=n: (0, 2 * n + s[0])) for n in range(3)]
    ins = [x, gain, cond, weight, weight, weight]
    specs = [
        pl.BlockSpec((block, width), lambda i, s: (i, 0)),
        pl.BlockSpec((1, width), lambda i, s: (0, 0)),
        pl.BlockSpec(cond.shape, lambda i, s: (0, 0)),
        *weights,
    ]
    aliases = {}
    if before is not None:
        ins += list(before)
        specs += [pl.BlockSpec(memory_space=pl.ANY)] * 2
        aliases = {7: 0, 8: 1}
    return call(
        project_kernel, "project", (info,), (rows // block,), ins, specs,
        (sds((total, width), BF), sds((total, 3 * half), BF)),
        (
            pl.BlockSpec((block, width), lambda i, s: (i + skip, 0)),
            pl.BlockSpec((block, 3 * half), lambda i, s: (i + skip, 0)),
        ),
        flops=2 * rows * width * 3 * half, aliases=aliases,
    )


def lanes_of(head, lane):
    return (lane < HD) if head == 0 else (lane >= HD), (HD if head == 0 else 0)


def put(lane, spare, inside, values, base):
    out = jnp.where(inside, base, jnp.zeros_like(base))
    for n, value in enumerate(values):
        out = jnp.where(lane == spare + n, value, out)
    return out


def attend_forward_kernel(local, info_ref, q_ref, k_ref, v_ref, o_ref, l_ref, ka, va):
    total = k_ref.shape[0]
    lane = lax.broadcasted_iota(jnp.int32, (1, 2 * HD), 1)

    @pl.when(pl.program_id(1) == 0)
    def _():
        live = live_column(total, 0, info_ref, local, total)
        bias = jnp.where(live, 0.0, MASKED)
        k = k_ref[...].astype(F32)
        v = v_ref[...].astype(F32)
        for head in range(2):
            inside, spare = lanes_of(head, lane)
            ka[head] = put(lane, spare, inside, (bias,), k).astype(BF)
            va[head] = put(lane, spare, inside, (1.0,), v).astype(BF)

    q = q_ref[...].astype(F32)
    results = []
    for head in range(2):
        inside, spare = lanes_of(head, lane)
        qa = put(lane, spare, inside, (1.0,), q).astype(BF)
        scores = nt(qa, ka[head])
        top = jnp.max(scores, axis=-1, keepdims=True)
        weights = jnp.exp2((scores - top) * EXP2_SCALE).astype(BF)
        mixed = nn(weights, va[head])
        sums = mixed[:, spare : spare + 1]
        results.append((mixed / sums, top + jnp.log(sums) * HD**0.5))
    (mixed0, log0), (mixed1, log1) = results
    first = lane < HD
    o_ref[...] = jnp.where(first, mixed0, mixed1).astype(BF)
    l_ref[...] = jnp.where(first, log1, log0)


def attend_forward(info, qkv, local):
    total = qkv.shape[0]
    half = qkv.shape[1] // 3
    pairs = half // (2 * HD)
    block = 256
    return call(
        functools.partial(attend_forward_kernel, local), "attend_forward", (info,), (pairs, total // block),
        [qkv, qkv, qkv],
        [
            pl.BlockSpec((block, 2 * HD), lambda j, i, s: (i, j)),
            pl.BlockSpec((total, 2 * HD), lambda j, i, s: (0, pairs + j)),
            pl.BlockSpec((total, 2 * HD), lambda j, i, s: (0, 2 * pairs + j)),
        ],
        (sds((total, half), BF), sds((total, half), F32)),
        (
            pl.BlockSpec((block, 2 * HD), lambda j, i, s: (i, j)),
            pl.BlockSpec((block, 2 * HD), lambda j, i, s: (i, j)),
        ),
        scratch=[pltpu.VMEM((2, total, 2 * HD), BF), pltpu.VMEM((2, total, 2 * HD), BF)],
        flops=16 * total * total * half,
    )


def attend_backward_kernel(
    local, info_ref, q_ref, g_ref, o_ref, l_ref, k_ref, v_ref, gq_ref, gk_ref, gv_ref, ka, va, kt, acck, accv
):
    total = k_ref.shape[0]
    lane = lax.broadcasted_iota(jnp.int32, (1, 2 * HD), 1)

    @pl.when(pl.program_id(1) == 0)
    def _():
        live = live_column(total, 0, info_ref, local, total)
        bias = jnp.where(live, 0.0, MASKED)
        k = k_ref[...].astype(F32)
        v = v_ref[...].astype(F32)
        for head in range(2):
            inside, spare = lanes_of(head, lane)
            ka[head] = put(lane, spare, inside, (bias, 1.0, 1.0, 1.0), k).astype(BF)
            va[head] = put(lane, spare, inside, (1.0, 1.0), v).astype(BF)
            kt[head] = jnp.where(inside, k, 0.0).astype(BF).T
        acck[...] = jnp.zeros_like(acck)
        accv[...] = jnp.zeros_like(accv)

    q = q_ref[...].astype(F32)
    g = g_ref[...].astype(F32)
    og = o_ref[...].astype(F32) * g
    logs = l_ref[...]
    log_hi = logs.astype(BF).astype(F32)
    log_mid = (logs - log_hi).astype(BF).astype(F32)
    log_low = logs - log_hi - log_mid
    gq_t = None
    for head in range(2):
        inside, spare = lanes_of(head, lane)
        qa = put(lane, spare, inside, (1.0, -log_hi, -log_mid, -log_low), q).astype(BF)
        inner = jnp.sum(jnp.where(inside, og, 0.0), axis=-1, keepdims=True)
        inner_hi = inner.astype(BF).astype(F32)
        ga = put(lane, spare, inside, (-inner_hi, inner_hi - inner), g).astype(BF)
        probability = jnp.exp2(nt(ka[head], qa) * EXP2_SCALE)
        g_scores = (probability * nt(va[head], ga)).astype(BF)
        qm = jnp.where(inside, q, 0.0).astype(BF)
        gm = jnp.where(inside, g, 0.0).astype(BF)
        acck[...] += nn(g_scores, qm)
        accv[...] += nn(probability.astype(BF), gm)
        term = nn(kt[head], g_scores)
        gq_t = term if gq_t is None else gq_t + term
    gq_ref[...] = (gq_t * HD**-0.5).T.astype(BF)

    @pl.when(pl.program_id(1) == pl.num_programs(1) - 1)
    def _():
        gk_ref[...] = (acck[...] * HD**-0.5).astype(BF)
        gv_ref[...] = accv[...].astype(BF)


def attend_backward(info, qkv, g, o, logs, local, first, count):
    total = qkv.shape[0]
    half = qkv.shape[1] // 3
    pairs = half // (2 * HD)
    block = 256
    part = lambda j, i, s: (i, first + j)
    return call(
        functools.partial(attend_backward_kernel, local), "attend_backward", (info,), (count, total // block),
        [qkv, g, o, logs, qkv, qkv],
        [
            pl.BlockSpec((block, 2 * HD), part),
            pl.BlockSpec((block, 2 * HD), part),
            pl.BlockSpec((block, 2 * HD), part),
            pl.BlockSpec((block, 2 * HD), part),
            pl.BlockSpec((total, 2 * HD), lambda j, i, s: (0, pairs + first + j)),
            pl.BlockSpec((total, 2 * HD), lambda j, i, s: (0, 2 * pairs + first + j)),
        ],
        (sds((total, count * 2 * HD), BF),) * 3,
        (
            pl.BlockSpec((block, 2 * HD), lambda j, i, s: (i, j)),
            pl.BlockSpec((total, 2 * HD), lambda j, i, s: (0, j)),
            pl.BlockSpec((total, 2 * HD), lambda j, i, s: (0, j)),
        ),
        scratch=[
            pltpu.VMEM((2, total, 2 * HD), BF),
            pltpu.VMEM((2, total, 2 * HD), BF),
            pltpu.VMEM((2, 2 * HD, total), BF),
            pltpu.VMEM((total, 2 * HD), F32),
            pltpu.VMEM((total, 2 * HD), F32),
        ],
        flops=40 * total * total * count * 2 * HD,
    )


def mix_out_kernel(local, total, info_ref, mine_ref, other_ref, w1_ref, w2_ref, bias_ref, x_ref, gain_ref, cond_ref, res_ref, act_ref):
    rows = x_ref.shape[0]
    live = live_column(rows, pl.program_id(0) * rows, info_ref, local, total).astype(F32)
    attended = nn(mine_ref[...], w1_ref[...]) + nn(other_ref[...], w2_ref[...]) + bias_ref[...]
    residual = x_ref[...].astype(F32) + live * attended
    res_ref[...] = residual
    normal, _ = norm_rows(residual)
    act_ref[...] = (normal * (gain_ref[...] * (1.0 + cond_ref[2:3, :])) + cond_ref[3:4, :]).astype(BF)


def mix_out(info, mine, other, weight, bias, x, gain, cond, local):
    total, width = x.shape
    half = mine.shape[1]
    block = 256
    row = lambda w: pl.BlockSpec((block, w), lambda i, s: (i, 0))
    vec = pl.BlockSpec((1, width), lambda i, s: (0, 0))
    return call(
        functools.partial(mix_out_kernel, local, total), "mix_out", (info,), (total // block,),
        [mine, other, weight, weight, bias, x, gain, cond],
        [
            row(half), row(half),
            pl.BlockSpec((half, width), lambda i, s: (s[0], 0)),
            pl.BlockSpec((half, width), lambda i, s: (1 - s[0], 0)),
            vec, row(width), vec, pl.BlockSpec(cond.shape, lambda i, s: (0, 0)),
        ],
        (sds((total, width), F32), sds((total, width), BF)),
        (row(width), row(width)),
        flops=4 * total * width * half,
    )


def raise_kernel(info_ref, act_ref, w_ref, bias_ref, hid_ref, der_ref):
    raised = nn(act_ref[...], w_ref[...]) + bias_ref[...]
    half = 0.5 * (1.0 + lax.erf(raised * (0.5**0.5)))
    hid_ref[...] = (raised * half).astype(BF)
    der_ref[...] = (half + raised * (jnp.exp(-0.5 * raised * raised) * (2.0 * math.pi) ** -0.5)).astype(BF)


def raise_up(info, act, weight, bias, fb, nb):
    total, width = act.shape
    col = pl.BlockSpec((total, fb), lambda j, s: (0, j))
    return call(
        raise_kernel, "raise_up", (info,), (nb,),
        [act, weight, bias],
        [
            pl.BlockSpec((total, width), lambda j, s: (0, 0)),
            pl.BlockSpec((width, fb), lambda j, s: (0, 2 * j + s[0])),
            pl.BlockSpec((1, fb), lambda j, s: (0, 2 * j + s[0])),
        ],
        (sds((total, fb * nb), BF),) * 2, (col, col),
        flops=2 * total * width * fb * nb,
    )


def weight_gradient_kernel(count, index_ref, lhs_ref, *refs):
    rhs, out_ref = refs[:count], refs[count]
    w = rhs[0].shape[1]
    lhs = lhs_ref[...]
    for n, ref in enumerate(rhs):
        out_ref[:, n * w : (n + 1) * w] = tn_dot(lhs, ref[...]).astype(BF)


def weight_gradient(lhs, rhss, rows, mb, col, w, name="weight_gradient"):
    total, height = lhs.shape
    if mb % 128:
        every = height // 128
        whole = weight_gradient(lhs, rhss, jnp.arange(every), 128, col, w, name)
        return whole.reshape(height // mb, mb, -1)[rows].reshape(rows.shape[0] * mb, -1)
    if w % 128:
        rhss = [lax.dynamic_slice_in_dim(r, col * w, w, 1) for r in rhss]
        col = 0
    n = rows.shape[0]
    index = jnp.concatenate([rows.astype(jnp.int32), jnp.full((1,), col, jnp.int32)])
    return call(
        functools.partial(weight_gradient_kernel, len(rhss)), name, (index,), (n,),
        [lhs, *rhss],
        [pl.BlockSpec((total, mb), lambda i, s: (0, s[i]))]
        + [pl.BlockSpec((total, w), lambda i, s: (0, s[n]))] * len(rhss),
        sds((n * mb, len(rhss) * w), BF),
        pl.BlockSpec((mb, len(rhss) * w), lambda i, s: (i, 0)),
        flops=2 * total * n * mb * len(rhss) * w,
    )


def raise_back_kernel(info_ref, g_ref, w_ref, der_ref, out_ref, sum_ref):
    back = (nt(g_ref[...], w_ref[...]) * der_ref[...].astype(F32)).astype(BF)
    out_ref[...] = back
    sum_ref[...] = jnp.sum(back.astype(F32), axis=0, keepdims=True)


def raise_back(info, g, weight, der, fb, nb):
    total, width = g.shape
    return call(
        raise_back_kernel, "raise_back", (info,), (nb,),
        [g, weight, der],
        [
            pl.BlockSpec((total, width), lambda j, s: (0, 0)),
            pl.BlockSpec((fb, width), lambda j, s: (2 * j + s[0], 0)),
            pl.BlockSpec((total, fb), lambda j, s: (0, j)),
        ],
        (sds((total, fb * nb), BF), sds((1, fb * nb), F32)),
        (pl.BlockSpec((total, fb), lambda j, s: (0, j)), pl.BlockSpec((1, fb), lambda j, s: (0, j))),
        flops=2 * total * width * fb * nb,
    )


def rows_product_kernel(count, transposed, index_ref, *refs):
    lhs, rhs, out_ref = refs[0], refs[1 : 1 + count], refs[1 + count]
    w = rhs[0].shape[1] if transposed else rhs[0].shape[0]
    total = None
    for n, ref in enumerate(rhs):
        term = (nt if transposed else nn)(lhs[:, n * w : (n + 1) * w], ref[...])
        total = term if total is None else total + term
    out_ref[...] = total.astype(BF)


def rows_product(lhs, weight, rows, block, core, fb, nb, transposed, name):
    depth = lhs.shape[1]
    width = weight.shape[0] if transposed else weight.shape[1]
    n = rows.shape[0]
    index = jnp.concatenate([rows.astype(jnp.int32), jnp.full((1,), core, jnp.int32)])
    if transposed:
        specs = [pl.BlockSpec((width, fb), lambda i, s, j=j: (0, 2 * j + s[n])) for j in range(nb)]
    else:
        specs = [pl.BlockSpec((fb, width), lambda i, s, j=j: (2 * j + s[n], 0)) for j in range(nb)]
    return call(
        functools.partial(rows_product_kernel, nb, transposed), name, (index,), (n,),
        [lhs] + [weight] * nb,
        [pl.BlockSpec((block, depth), lambda i, s: (s[i], 0)), *specs],
        sds((n * block, width), BF),
        pl.BlockSpec((block, width), lambda i, s: (i, 0)),
        flops=2 * n * block * depth * width,
    )


def norm_back(g, v, gain, scale):
    normal, inverse = norm_rows(v)
    e = g * (gain * (1.0 + scale))
    grad = inverse * (
        e - jnp.mean(e, axis=-1, keepdims=True) - normal * jnp.mean(e * normal, axis=-1, keepdims=True)
    )
    return grad, jnp.sum(g * normal, axis=0, keepdims=True), jnp.sum(g, axis=0, keepdims=True)


def accumulate(sum_ref, parts):
    block = jnp.concatenate(parts, axis=0)

    @pl.when(pl.program_id(0) == 0)
    def _():
        sum_ref[...] = block

    @pl.when(pl.program_id(0) > 0)
    def _():
        sum_ref[...] += block


def dense_norm_back_kernel(local, total, info_ref, a_ref, b_ref, res_ref, cot_ref, gain_ref, cond_ref, w_ref, gres_ref, gatt_ref, gmix_ref, sum_ref):
    rows = res_ref.shape[0]
    live = live_column(rows, pl.program_id(0) * rows, info_ref, local, total).astype(F32)
    g = a_ref[...].astype(F32) + b_ref[...].astype(F32)
    grad, by_normal, plain = norm_back(g, res_ref[...], gain_ref[...], cond_ref[2:3, :])
    g_residual = cot_ref[...].astype(F32) + grad
    gres_ref[...] = g_residual
    g_attend = (live * g_residual).astype(BF)
    gatt_ref[...] = g_attend
    gmix_ref[...] = nt(g_attend, w_ref[...]).astype(BF)
    bias = jnp.sum(g_attend.astype(F32), axis=0, keepdims=True)
    accumulate(sum_ref, [by_normal, plain, bias, jnp.zeros((5, bias.shape[1]), F32)])


def dense_norm_back(info, a, b, residual, cot, gain, cond, weight, local):
    total, width = residual.shape
    half = weight.shape[0] // 2
    block = 256
    row = lambda w: pl.BlockSpec((block, w), lambda i, s: (i, 0))
    return call(
        functools.partial(dense_norm_back_kernel, local, total), "dense_norm_back", (info,), (total // block,),
        [a, b, residual, cot, gain, cond, weight],
        [
            row(width), row(width), row(width), row(width),
            pl.BlockSpec((1, width), lambda i, s: (0, 0)),
            pl.BlockSpec(cond.shape, lambda i, s: (0, 0)),
            pl.BlockSpec((half, width), lambda i, s: (s[0], 0)),
        ],
        (sds((total, width), F32), sds((total, width), BF), sds((total, half), BF), sds((8, width), F32)),
        (row(width), row(width), row(half), pl.BlockSpec((8, width), lambda i, s: (0, 0))),
        flops=2 * total * width * half,
    )


def project_back_kernel(count, index_ref, *refs):
    lhs, rhs, out_ref = refs[: 3 * count], refs[3 * count : 3 * count + 3], refs[-1]
    total = None
    for n in range(3):
        for m in range(count):
            ref = lhs[n * count + m]
            w = ref.shape[1]
            term = nt(ref[...], rhs[n][:, m * w : (m + 1) * w])
            total = term if total is None else total + term
    out_ref[...] = total.astype(BF)


def project_back(parts, weight, rows, block, core):
    width = weight.shape[0]
    half = weight.shape[1] // 6
    count = len(parts)
    n = rows.shape[0]
    index = jnp.concatenate([rows.astype(jnp.int32), jnp.full((1,), core, jnp.int32)])
    lhs = [part[m] for m in range(3) for part in parts]
    return call(
        functools.partial(project_back_kernel, count), "project_back", (index,), (n,),
        lhs + [weight] * 3,
        [pl.BlockSpec((block, a.shape[1]), lambda i, s: (s[i], 0)) for a in lhs]
        + [pl.BlockSpec((width, half), lambda i, s, m=m: (0, 2 * m + s[n])) for m in range(3)],
        sds((n * block, width), BF),
        pl.BlockSpec((block, width), lambda i, s: (i, 0)),
        flops=6 * n * block * half * width,
    )


def attend_norm_back_kernel(index_ref, a_ref, b_ref, x_ref, gres_ref, gain_ref, cond_ref, out_ref, sum_ref):
    g = a_ref[...].astype(F32) + b_ref[...].astype(F32)
    grad, by_normal, plain = norm_back(g, x_ref[...].astype(F32), gain_ref[...], cond_ref[0:1, :])
    out_ref[...] = (gres_ref[...] + grad).astype(BF)
    accumulate(sum_ref, [by_normal, plain, jnp.zeros((6, plain.shape[1]), F32)])


def attend_norm_back(rows, a, b, x, g_residual, gain, cond, block):
    width = x.shape[1]
    n = rows.shape[0]
    plain = pl.BlockSpec((block, width), lambda i, s: (i, 0))
    picked = pl.BlockSpec((block, width), lambda i, s: (s[i], 0))
    return call(
        attend_norm_back_kernel, "attend_norm_back", (rows.astype(jnp.int32),), (n,),
        [a, b, x, g_residual, gain, cond],
        [
            plain, plain, picked, picked,
            pl.BlockSpec((1, width), lambda i, s: (0, 0)),
            pl.BlockSpec(cond.shape, lambda i, s: (0, 0)),
        ],
        (sds((n * block, width), BF), sds((8, width), F32)),
        (plain, pl.BlockSpec((8, width), lambda i, s: (0, 0))),
        flops=0,
    )


def sinus_angles(time, features, width):
    halfway = width // 2
    rates = jnp.exp(-math.log(10000.0) * (features % halfway).astype(F32) / halfway)
    angles = time[:, None] * rates[None, :]
    return jnp.where((features < halfway)[None, :], jnp.sin(angles), jnp.cos(angles))


def body(
    dp, seq,
    tokens, time_index, lengths, time_weight, time_bias, attend_gain, query_key_value_weight,
    attention_output_weight, attend_bias, dense_gain, feedforward_up_matrix, up_bias,
    feedforward_down_matrix, down_bias, cotangent,
):
    nl, tl, d = tokens.shape
    ff = feedforward_up_matrix.shape[1]
    total = tl * seq
    chips = dp // 2
    nz = dp // 4
    i = lax.axis_index("dp")
    y = lax.axis_index("seq")
    core = i % 2
    x = (i // 2) % 2
    z = i // 4
    h = tl // 2
    half = d // 2
    fb, nb = ff // dp, dp // 2


    core_swap = lambda a: lax.ppermute(a, "dp", [(n, n ^ 1) for n in range(dp)])
    x_swap = lambda a: lax.ppermute(a, "dp", [(n, n ^ 2) for n in range(dp)])

    def z_shift(a, k):
        return lax.ppermute(a, "dp", [(n, (n // 4 + k) % nz * 4 + n % 4) for n in range(dp)])

    def y_shift(a, k):
        return lax.ppermute(a, "seq", [(n, (n + k) % seq) for n in range(seq)])

    def travel(k, q):
        pairs = []
        for chip in range(chips):
            for s in range(seq):
                target = (s + k) % seq
                pairs.append(((chip * 2 + target // nl) * seq + s, (chip * 2 + q) * seq + target))
        return pairs

    def pick(a, index):
        return lax.dynamic_index_in_dim(a, index, 0, keepdims=False)

    def in_core_order(mine, other):
        return jnp.where(core == 0, mine, other), jnp.where(core == 0, other, mine)

    def fetch(a):
        mine = pick(a, y % nl)
        local = jnp.where(core == y // nl, mine, core_swap(mine))
        far = []
        for k in range(1, seq):
            piece = pick(a, (y + k) % seq % nl)
            got = [
                lax.ppermute(piece[q * h : (q + 1) * h], ("dp", "seq"), travel(k, q)) for q in range(2)
            ]
            own = jnp.where(core == 0, got[0], got[1])
            far += in_core_order(own, core_swap(own))
        return local, jnp.concatenate(far, axis=0)

    def give_back(a):
        got = [jnp.concatenate(in_core_order(a[0], core_swap(a[0])), axis=0)]
        for k in range(1, seq):
            halves = [
                lax.ppermute(a[k], ("dp", "seq"), [(t, s) for s, t in travel(k, q)]) for q in range(2)
            ]
            got.append(jnp.concatenate(halves, axis=0))
        got = jnp.stack(got)
        return jnp.stack([pick(got, (core * nl + j - y) % seq) for j in range(nl)])

    def add(*terms):
        return sum(t.astype(F32) for t in terms).astype(BF)

    def z_sum(a):
        return add(pick(a, z), *[z_shift(pick(a, (z + k) % nz), k) for k in range(1, nz)])

    def y_sum(a):
        got = [y_shift(a, k).astype(F32) for k in range(1, seq)]
        return sum(got, a.astype(F32))

    def y_gather(a):
        got = jnp.stack([a] + [y_shift(a, k) for k in range(1, seq)])
        return jnp.stack([pick(got, (y - n) % seq) for n in range(seq)])

    def reduce_x_first(send, keep, rows):
        mine = add(keep, x_swap(send)).reshape(nz, rows, -1)
        return y_sum(z_sum(mine))

    def reduce_y_first(sends, keep, rows):
        mine = add(keep, *[y_shift(s, k + 1) for k, s in enumerate(sends)])
        mine = mine.reshape(nz, 2, rows, -1)
        mine = add(
            lax.dynamic_index_in_dim(mine, x, 1, keepdims=False),
            x_swap(lax.dynamic_index_in_dim(mine, 1 - x, 1, keepdims=False)),
        )
        return y_gather(z_sum(mine))

    zs = jnp.arange(nz)

    def reduced(lhs, early, late, rows, name):
        w_early = early[0].shape[1]
        first = reduce_x_first(
            weight_gradient(lhs, early, zs * 2 + 1 - x, rows, 0, w_early, name),
            weight_gradient(lhs, early, zs * 2 + x, rows, 0, w_early, name),
            rows,
        )
        w = late[0].shape[1] // seq
        every = jnp.arange(chips)
        parts = [weight_gradient(lhs, late, every, rows, (y + k) % seq, w, name) for k in range(1, seq)]
        kept = weight_gradient(lhs, late, every, rows, y, w, name)
        second = reduce_y_first(parts, kept, rows)
        second = second.reshape(seq, rows, len(late), w).transpose(1, 2, 0, 3)
        return first, second.reshape(rows, -1).astype(F32)


    both = jnp.stack([time_index, lengths])
    every = jnp.stack(in_core_order(both, core_swap(both)), axis=1).reshape(2, 2 * nl)
    time = lax.dynamic_slice_in_dim(every[0], y, 1).astype(F32)
    length = lax.dynamic_slice_in_dim(every[1], y, 1)
    info = jnp.concatenate([core[None], (y * tl)[None], length]).astype(jnp.int32)
    slot_of = (y * tl - jnp.arange(total) // tl * tl) % total + jnp.arange(total) % tl
    live = slot_of < length[0]

    near, far = fetch(tokens)
    near_cot, far_cot = fetch(cotangent)
    table = sinus_angles(time, jnp.arange(d), d).astype(BF)
    cond = (jnp.dot(table, time_weight, preferred_element_type=F32) + time_bias).reshape(4, d)
    gain1, gain2 = attend_gain[None, :], dense_gain[None, :]

    act1, qkv = project(info, near, 0, total, gain1, cond, query_key_value_weight)
    act1, qkv = project(info, far, tl, total, gain1, cond, query_key_value_weight, (act1, qkv))
    full = jnp.concatenate([near, far], axis=0)
    mixture, logs = attend_forward(info, qkv, tl)
    other_mixture = core_swap(mixture)
    residual, act2 = mix_out(
        info, mixture, other_mixture, attention_output_weight, attend_bias[None, :], full, gain2, cond, tl
    )
    hidden, slope = raise_up(info, act2, feedforward_up_matrix, up_bias[None, :], fb, nb)

    cot = jnp.concatenate([near_cot, far_cot], axis=0)
    g_dense = jnp.where(live[:, None], cot, jnp.zeros_like(cot))
    g_down_bias = jnp.sum(g_dense.astype(F32), axis=0)
    down_early, down_late = reduced(hidden, [g_dense[:, :half]], [g_dense[:, half:]], fb, "down_gradient")
    gradient_down = jnp.concatenate([down_early, down_late], axis=1)

    g_raised, g_up_bias = raise_back(info, g_dense, feedforward_down_matrix, slope, fb, nb)
    g_act2 = rows_product(
        g_raised, feedforward_up_matrix, jnp.arange(total // 256), 256, core, fb, nb, True, "raise_input_back"
    )
    up_half = fb * nb // 2
    up_early, up_late = reduced(act2, [g_raised[:, :up_half]], [g_raised[:, up_half:]], d // chips, "up_gradient")

    g_residual, g_attend, g_mixture, sums2 = dense_norm_back(
        info, g_act2, core_swap(g_act2), residual, cot, gain2, cond, attention_output_weight, tl
    )

    rb = d // dp
    g_out = weight_gradient(mixture, [g_attend], jnp.arange(half // 128), 128, 0, d, "out_gradient")
    g_out = g_out.reshape(chips // 2, 2, rb, d)
    mine = lax.dynamic_index_in_dim(g_out, core, 1, keepdims=False)
    yours = core_swap(lax.dynamic_index_in_dim(g_out, 1 - core, 1, keepdims=False))
    g_out = jnp.concatenate(in_core_order(mine, yours), axis=0).reshape(nz, 2, rb, d)
    gradient_out = reduce_x_first(
        lax.dynamic_index_in_dim(g_out, 1 - x, 1, keepdims=False).reshape(nz * rb, d),
        lax.dynamic_index_in_dim(g_out, x, 1, keepdims=False).reshape(nz * rb, d),
        rb,
    )

    pairs = half // (2 * HD)
    parts = [
        attend_backward(info, qkv, g_mixture, mixture, logs, tl, n * pairs // 2, pairs // 2) for n in range(2)
    ]
    in_early, in_late = reduced(act1, list(parts[0]), list(parts[1]), d // chips, "in_gradient")

    own_rows, their_rows = jnp.arange(seq) * 2 + core, jnp.arange(seq) * 2 + 1 - core
    g_act1_theirs = core_swap(project_back(parts, query_key_value_weight, their_rows, h, core))
    g_act1 = project_back(parts, query_key_value_weight, own_rows, h, core)
    g_tokens, sums1 = attend_norm_back(own_rows, g_act1, g_act1_theirs, full, g_residual, gain1, cond, h)
    gradient_tokens = give_back(g_tokens.reshape(seq, h, d))

    down_args = (h, core, fb, nb, False, "lower")
    branch_theirs = core_swap(rows_product(hidden, feedforward_down_matrix, their_rows, *down_args))
    branch = rows_product(hidden, feedforward_down_matrix, own_rows, *down_args)
    pieces = lambda a: lax.dynamic_index_in_dim(a.reshape(seq, 2, h, -1), core, 1, keepdims=False)
    live_half = pieces(live[:, None])
    branch = (branch.astype(F32) + branch_theirs.astype(F32)).reshape(seq, h, d) + down_bias
    result = give_back((pieces(residual) + jnp.where(live_half, branch, 0.0)).astype(BF))

    def finish(early, late, blocks, inner):
        whole = jnp.concatenate(
            [a.astype(BF).reshape(2, d // dp, blocks, inner) for a in (early, late)], axis=3
        )
        got = core_swap(lax.dynamic_index_in_dim(whole, 1 - core, 0, keepdims=False))
        mine = lax.dynamic_index_in_dim(whole, core, 0, keepdims=False)
        return in_core_order(mine.astype(F32), got.astype(F32))

    first, second = finish(up_early, up_late, 1, up_half)
    gradient_up = jnp.stack([a.reshape(d // dp, nb, fb) for a in (first, second)], axis=2).reshape(d // dp, ff)
    first, second = finish(in_early, in_late, 3, half // 2)
    gradient_in = jnp.stack([first, second], axis=2).reshape(d // dp, 3 * d)

    once = jnp.where(core == 0, 1.0, 0.0)
    scales = 1.0 + cond
    up_sum = g_up_bias.reshape(nb, 1, fb)
    up_sum = jnp.concatenate(in_core_order(up_sum, jnp.zeros_like(up_sum)), axis=1).reshape(ff // d, d)
    pack = jnp.concatenate(
        [
            sums1[0:1] * gain1,
            sums1[1:2],
            once * sums2[0:1] * gain2,
            once * sums2[1:2],
            sums1[0:1] * scales[0:1],
            once * sums2[0:1] * scales[2:3],
            once * sums2[2:3],
            once * g_down_bias[None, :],
            once * jnp.broadcast_to(time[:, None], (1, d)),
            up_sum,
        ]
    )
    pack = pack + core_swap(pack)
    all_packs = jnp.stack([pack, x_swap(pack)])
    all_packs = jnp.concatenate([all_packs] + [y_shift(all_packs, k) for k in range(1, seq)])
    all_packs = jnp.concatenate([all_packs] + [z_shift(all_packs, k) for k in range(1, nz)])
    g_cond = all_packs[:, 0:4].reshape(-1, 4 * d)
    own_features = i * (d // dp) + jnp.arange(d // dp)
    features = sinus_angles(all_packs[:, 8, 0], own_features, d).astype(BF)
    gradient_time = lax.dot_general(
        features.astype(F32), g_cond, (((0,), (0,)), ((), ())), precision=lax.Precision.HIGHEST
    )
    sums = jnp.sum(all_packs, axis=0)
    part = lambda v: lax.dynamic_index_in_dim(v.reshape(dp, -1), i, 0, keepdims=False)
    return (
        result,
        gradient_tokens,
        gradient_time,
        part(sums[0:4]),
        part(sums[4]),
        gradient_in,
        gradient_out,
        part(sums[6]),
        part(sums[5]),
        gradient_up,
        part(sums[9:]),
        gradient_down,
        part(sums[7]),
    )


def solution(mesh):
    whole = P()
    rows = P("dp", "seq", None)
    return jax.shard_map(
        functools.partial(body, mesh.shape["dp"], mesh.shape["seq"]),
        mesh=mesh,
        in_specs=(rows, P("dp"), P("dp"), *(whole,) * 11, rows),
        out_specs=(
            rows, rows, P("dp", None), P("dp"), P("dp"), P("dp", None), P("dp", None),
            P("dp"), P("dp"), P("dp", None), P("dp"), P("dp", None), P("dp"),
        ),
        check_vma=False,
    )
```

time: 1170 us -> 542 us (0.46)
  waiting for transfers between devices: 433 us -> 98.9 us
  matrix products: 278 us -> 6.28 us
  Pallas kernels: 0 us -> 242 us
  blocking collectives: 176 us -> 0 us
  local copies, waits for them, and re-layouts: 130 us -> 33.4 us
  starting transfers between devices: 14.7 us -> 96.5 us
  other arithmetic: 111 us -> 52.7 us
  between operations: 17.9 us -> 4.37 us
    reduce_scatter x5 -> x0, waiting for transfers between devices: 367 us -> none  [the longest x1 108 us: body(): lax.psum_scatter(grad_time_weight.astype(jnp.bfloat16), 'dp', scatter_dim...]
    dot_general x22 -> x2, matrix products: 259 us -> 6.28 us  [the longest x1 4.58 us: body(): jnp.dot(table, time_weight, preferred_element_type=F32) + time_bias]
    pallas_call x0 -> x28, Pallas kernels: none -> 242 us  [call(): pl.pallas_call(kernel, name=name, grid_spec=pltpu.PrefetchScalarGridSpec(...]
    all_to_all x3 -> x0, blocking collectives: 111 us -> none  [the longest x1 49.1 us: forward_pass(): lax.all_to_all(packed, 'seq', split_axis=3, concat_axis=1, tiled=True)]
    ppermute x0 -> x66, waiting for transfers between devices: none -> 98.9 us  [the longest x24 72 us: z_shift(): lax.ppermute(a, 'dp', [(n, (n // 4 + k) % nz * 4 + n % 4) for n in range(...]
    ppermute x0 -> x66, starting transfers between devices: none -> 96.5 us  [the longest x24 43 us: z_shift(): lax.ppermute(a, 'dp', [(n, (n // 4 + k) % nz * 4 + n % 4) for n in range(...]
    all_to_all x3 -> x0, waiting for transfers between devices: 65.8 us -> none  [the longest x1 48.2 us: forward_pass(): lax.all_to_all(packed, 'seq', split_axis=3, concat_axis=1, tiled=True)]
    unnamed x1 -> x0, blocking collectives: 60.2 us -> none
  transfers between devices with their start and end apart: 9 -> 66, of which waited for: 7 -> 21; matrix products, arithmetic and copies ran while one was open for 17% -> 16% of each run, Pallas kernels for 0% -> 39%
where the time goes in v1:
time: 542 us; the launch traced here: 534 us
  Pallas kernels  242 us (45%)
  waiting for transfers between devices  98.9 us (18%)
  starting transfers between devices  96.5 us (18%)
  other arithmetic  52.7 us (10%)
  local copies, waits for them, and re-layouts  33.4 us (6%)
  matrix products  6.28 us (1%)
    pallas_call x28, Pallas kernels, call(): pl.pallas_call(kernel, name=name, grid_spec=pltpu.PrefetchScalarGridSpec(...  242 us
    ppermute x24, waiting for transfers between devices, z_shift(): lax.ppermute(a, 'dp', [(n, (n // 4 + k) % nz * 4 + n % 4) for n in range(...  72 us
    ppermute x24, starting transfers between devices, z_shift(): lax.ppermute(a, 'dp', [(n, (n // 4 + k) % nz * 4 + n % 4) for n in range(...  43 us
    ppermute x11, starting transfers between devices, y_shift(): return lax.ppermute(a, 'seq', [(n, (n + k) % seq) for n in range(seq)])  18.6 us
    ppermute x8, waiting for transfers between devices, body(): x_swap = lambda a: lax.ppermute(a, 'dp', [(n, n ^ 2) for n in range(dp)])  16 us
    ppermute x15, starting transfers between devices, body(): core_swap = lambda a: lax.ppermute(a, 'dp', [(n, n ^ 1) for n in range(dp)])  11.8 us
  transfers between devices with their start and end apart: 66, of which 21 were waited for; matrix products, arithmetic and copies ran while one was open for 16% of the time, Pallas kernels for 39%

profile of v1, /device:TPU:0, one launch (start us, length us, event | category | flops | bytes accessed | tf_op | source)
XLA Modules:
  0.0 533.8 jit_solution(1242011696600859108)
XLA Ops:
  22.0 4.6 fusion.88
  26.5 7.8 %collective-permute-start.10 = (bf16[512,1024]{1,0:T(8,128)(2,1)S(1)}, bf16[512,1024]{1,0:T(8,128)(2,1)}, u32[]{:S(2)}, u32[]{:S(2)}) collective-permute-start(bf16[512,1024]{1,0:T(8,128)(2,1)S(1)} %bitcast.249), channel_id=1, source_target_pairs={{0,2},{2,0},{4,6},{6,4},{8,10},{10,8},{12,14},{14,12},{16,18},{18,... | collective-permute-start | bytes 3145736 | tf_op jit(solution)/shard_map/ppermute | solution.py:538
  42.6 6.7 %project.2 = (bf16[1024,1024]{1,0:T(8,128)(2,1)}, bf16[1024,1536]{1,0:T(8,128)(2,1)}) custom-call(s32[3]{0:T(128)} %pad_add_fusion.3.info_ref, bf16[512,1024]{1,0:T(8,128)(2,1)} %broadcast_select_fusion.2.x_ref, f32[1,1024]{1,0:T(1,128)} %bitcast.280, f32[4,1024]{1,0:T(4,128)} %copy-done.17, bf16[1024,3072]{1,0:T(8,128)(2,1)} %refs_8_.9, ...), custom_call_target="tpu_custom_call" | custom-call | flops 1610612736 | bytes 25186304 | tf_op jit(solution)/shard_map/project/pallas_call | solution.py:38
  49.3 6.2 %project.3 = (bf16[1024,1024]{1,0:T(8,128)(2,1)}, bf16[1024,1536]{1,0:T(8,128)(2,1)}) custom-call(s32[3]{0:T(128)} %pad_add_fusion.3.info_ref, bf16[512,1024]{1,0:T(8,128)(2,1)} %pad_maximum_fusion.2.x_ref, f32[1,1024]{1,0:T(1,128)} %bitcast.281, f32[4,1024]{1,0:T(4,128)} %copy-done.17, ...), custom_call_target="tpu_custom_call", output_to_operand_aliasing={{0}: (7, {}), {1}: (8, {})} | custom-call | flops 1610612736 | bytes 30429184 | tf_op jit(solution)/shard_map/project/pallas_call | solution.py:38
  55.5 23.1 %attend_forward.1 = (bf16[1024,512]{1,0:T(8,128)(2,1)}, f32[1024,512]{1,0:T(8,128)}) custom-call(s32[3]{0:T(128)} %pad_add_fusion.3.info_ref, bf16[1024,1536]{1,0:T(8,128)(2,1)} %get-tuple-element.39.q_ref.k_ref.v_ref, bf16[1024,1536]{1,0:T(8,128)(2,1)} %get-tuple-element.39.q_ref.k_ref.v_ref, bf16[1024,1536]{1,0:T(8,128)(2,1)} %get-tuple-element.39.q_ref.k_ref.v_ref), custom_call_target="tpu_custom_call" | custom-call | flops 8589934592 | bytes 12582912 | tf_op jit(solution)/shard_map/attend_forward/pallas_call | solution.py:38
  83.1 3.9 convert_reduce_fusion
  90.1 8.2 %mix_out.1 = (f32[1024,1024]{1,0:T(8,128)}, bf16[1024,1024]{1,0:T(8,128)(2,1)}) custom-call(s32[3]{0:T(128)} %pad_add_fusion.3.info_ref, bf16[1024,512]{1,0:T(8,128)(2,1)} %get-tuple-element.40.mine_ref.o_ref.lhs_ref, bf16[1024,512]{1,0:T(8,128)(2,1)} %copy-done.16, bf16[1024,1024]{1,0:T(8,128)(2,1)} %w_ref.5, bf16[1024,1024]{1,0:T(8,128)(2,1)} %w_ref.5, ...), custom_call_target="tpu_custom_call" | custom-call | flops 2147483648 | bytes 14704640 | tf_op jit(solution)/shard_map/mix_out/pallas_call | solution.py:38
  98.2 12.9 %raise_up.1 = (bf16[1024,2048]{1,0:T(8,128)(2,1)}, bf16[1024,2048]{1,0:T(8,128)(2,1)}) custom-call(s32[3]{0:T(128)} %pad_add_fusion.3.info_ref, bf16[1024,1024]{1,0:T(8,128)(2,1)} %get-tuple-element.42.act_ref.lhs_ref, bf16[1024,4096]{1,0:T(8,128)(2,1)} %refs_8_.7, f32[1,4096]{1,0:T(1,128)} %bitcast.291), custom_call_target="tpu_custom_call" | custom-call | flops 4294967296 | bytes 18890752 | tf_op jit(solution)/shard_map/raise_up/pallas_call | solution.py:38
  111.1 5.5 %down_gradient.5 = bf16[1024,512]{1,0:T(8,128)(2,1)} custom-call(s32[5]{0:T(128)} %pad_add_fusion.index_ref, bf16[1024,2048]{1,0:T(8,128)(2,1)} %get-tuple-element.43.refs_0_.lhs_ref, bf16[1024,512]{1,0:T(8,128)(2,1)} %get-tuple-element.73.refs_0_), custom_call_target="tpu_custom_call" | custom-call | flops 1073741824 | bytes 6291456 | tf_op jit(solution)/shard_map/down_gradient/pallas_call | solution.py:38
  118.1 8.0 %down_gradient.7 = bf16[2048,256]{1,0:T(8,128)(2,1)} custom-call(s32[9]{0:T(128)} %get-tuple-element.150.index_ref, bf16[1024,2048]{1,0:T(8,128)(2,1)} %get-tuple-element.43.refs_0_.lhs_ref, bf16[1024,512]{1,0:T(8,128)(2,1)} %get-tuple-element.74.refs_0_), custom_call_target="tpu_custom_call" | custom-call | flops 1073741824 | bytes 6291456 | tf_op jit(solution)/shard_map/down_gradient/pallas_call | solution.py:38
  129.3 11.7 %raise_back.1 = (bf16[1024,2048]{1,0:T(8,128)(2,1)}, f32[1,2048]{1,0:T(1,128)}) custom-call(s32[3]{0:T(128)} %pad_add_fusion.3.info_ref, bf16[1024,1024]{1,0:T(8,128)(2,1)} %copy-done.3, bf16[4096,1024]{1,0:T(8,128)(2,1)} %w_ref.4, bf16[1024,2048]{1,0:T(8,128)(2,1)} %get-tuple-element.44.der_ref), custom_call_target="tpu_custom_call" | custom-call | flops 4294967296 | bytes 18882560 | tf_op jit(solution)/shard_map/raise_back/pallas_call | solution.py:38
  141.0 4.6 fusion.79
  145.6 7.7 %up_gradient.7 = bf16[1024,512]{1,0:T(8,128)(2,1)} custom-call(s32[9]{0:T(128)} %get-tuple-element.150.index_ref, bf16[1024,1024]{1,0:T(8,128)(2,1)} %get-tuple-element.42.act_ref.lhs_ref, bf16[1024,1024]{1,0:T(8,128)(2,1)} %get-tuple-element.71.refs_0_), custom_call_target="tpu_custom_call" | custom-call | flops 1073741824 | bytes 5242880 | tf_op jit(solution)/shard_map/up_gradient/pallas_call | solution.py:38
  153.3 5.8 %up_gradient.5 = bf16[512,1024]{1,0:T(8,128)(2,1)} custom-call(s32[5]{0:T(128)} %pad_add_fusion.index_ref, bf16[1024,1024]{1,0:T(8,128)(2,1)} %get-tuple-element.42.act_ref.lhs_ref, bf16[1024,1024]{1,0:T(8,128)(2,1)} %get-tuple-element.72.refs_0_), custom_call_target="tpu_custom_call" | custom-call | flops 1073741824 | bytes 5242880 | tf_op jit(solution)/shard_map/up_gradient/pallas_call | solution.py:38
  159.7 6.6 %lower.3 = bf16[512,1024]{1,0:T(8,128)(2,1)} custom-call(s32[3]{0:T(128)} %pad_add_fusion.5.index_ref, bf16[1024,2048]{1,0:T(8,128)(2,1)} %get-tuple-element.43.refs_0_.lhs_ref, bf16[4096,1024]{1,0:T(8,128)(2,1)} %w_ref.4, bf16[4096,1024]{1,0:T(8,128)(2,1)} %w_ref.4, bf16[4096,1024]{1,0:T(8,128)(2,1)} %w_ref.4, bf16[4096,1024]{1,0:T(8,128)(2,1)} %w_ref.4, ...), custom_call_target="tpu_custom_call" | custom-call | flops 2147483648 | bytes 72351744 | tf_op jit(solution)/shard_map/lower/pallas_call | solution.py:38
  166.4 8.0 %down_gradient.6 = bf16[2048,256]{1,0:T(8,128)(2,1)} custom-call(s32[9]{0:T(128)} %get-tuple-element.149.index_ref, bf16[1024,2048]{1,0:T(8,128)(2,1)} %get-tuple-element.43.refs_0_.lhs_ref, bf16[1024,512]{1,0:T(8,128)(2,1)} %get-tuple-element.74.refs_0_), custom_call_target="tpu_custom_call" | custom-call | flops 1073741824 | bytes 6291456 | tf_op jit(solution)/shard_map/down_gradient/pallas_call | solution.py:38
  174.4 7.8 %up_gradient.6 = bf16[1024,512]{1,0:T(8,128)(2,1)} custom-call(s32[9]{0:T(128)} %get-tuple-element.149.index_ref, bf16[1024,1024]{1,0:T(8,128)(2,1)} %get-tuple-element.42.act_ref.lhs_ref, bf16[1024,1024]{1,0:T(8,128)(2,1)} %get-tuple-element.71.refs_0_), custom_call_target="tpu_custom_call" | custom-call | flops 1073741824 | bytes 5242880 | tf_op jit(solution)/shard_map/up_gradient/pallas_call | solution.py:38
  182.2 5.5 %down_gradient.4 = bf16[1024,512]{1,0:T(8,128)(2,1)} custom-call(s32[5]{0:T(128)} %pad_add_fusion.1.index_ref, bf16[1024,2048]{1,0:T(8,128)(2,1)} %get-tuple-element.43.refs_0_.lhs_ref, bf16[1024,512]{1,0:T(8,128)(2,1)} %get-tuple-element.73.refs_0_), custom_call_target="tpu_custom_call" | custom-call | flops 1073741824 | bytes 6291456 | tf_op jit(solution)/shard_map/down_gradient/pallas_call | solution.py:38
  187.7 9.4 %raise_input_back.1.a_ref = bf16[1024,1024]{1,0:T(8,128)(2,1)} custom-call(s32[5]{0:T(128)} %pad_add_fusion.6.index_ref, bf16[1024,2048]{1,0:T(8,128)(2,1)} %get-tuple-element.45.refs_0_, bf16[1024,4096]{1,0:T(8,128)(2,1)} %refs_8_.7, bf16[1024,4096]{1,0:T(8,128)(2,1)} %refs_8_.7, bf16[1024,4096]{1,0:T(8,128)(2,1)} %refs_8_.7, bf16[1024,4096]{1,0:T(8,128)(2,1)} %refs_8_.7, ...), custom_call_target="tpu_custom_call" | custom-call | flops 4294967296 | bytes 73400320 | tf_op jit(solution)/shard_map/raise_input_back/pallas_call | solution.py:38
  197.1 5.7 %up_gradient.4 = bf16[512,1024]{1,0:T(8,128)(2,1)} custom-call(s32[5]{0:T(128)} %pad_add_fusion.1.index_ref, bf16[1024,1024]{1,0:T(8,128)(2,1)} %get-tuple-element.42.act_ref.lhs_ref, bf16[1024,1024]{1,0:T(8,128)(2,1)} %get-tuple-element.72.refs_0_), custom_call_target="tpu_custom_call" | custom-call | flops 1073741824 | bytes 5242880 | tf_op jit(solution)/shard_map/up_gradient/pallas_call | solution.py:38
  202.8 6.7 %lower.2 = bf16[512,1024]{1,0:T(8,128)(2,1)} custom-call(s32[3]{0:T(128)} %pad_add_fusion.4.index_ref, bf16[1024,2048]{1,0:T(8,128)(2,1)} %get-tuple-element.43.refs_0_.lhs_ref, bf16[4096,1024]{1,0:T(8,128)(2,1)} %w_ref.4, bf16[4096,1024]{1,0:T(8,128)(2,1)} %w_ref.4, bf16[4096,1024]{1,0:T(8,128)(2,1)} %w_ref.4, bf16[4096,1024]{1,0:T(8,128)(2,1)} %w_ref.4, ...), custom_call_target="tpu_custom_call" | custom-call | flops 2147483648 | bytes 72351744 | tf_op jit(solution)/shard_map/lower/pallas_call | solution.py:38
  224.1 9.4 %collective-permute-done.57 = bf16[256,512]{1,0:T(8,128)(2,1)S(1)} collective-permute-done((bf16[256,512]{1,0:T(8,128)(2,1)S(1)}, bf16[256,512]{1,0:T(8,128)(2,1)S(1)}, u32[]{:S(2)}, u32[]{:S(2)}) %collective-permute-start.57) | collective-permute-done | bytes 262176 | tf_op jit(solution)/shard_map/ppermute | solution.py:542
  234.3 4.9 collective-permute-done.44
  239.2 3.9 collective-permute-start.8
  243.1 12.5 %collective-permute-done.45 = bf16[128,1024]{1,0:T(8,128)(2,1)S(1)} collective-permute-done((bf16[128,1024]{1,0:T(8,128)(2,1)S(1)}, bf16[128,1024]{1,0:T(8,128)(2,1)S(1)}, u32[]{:S(2)}, u32[]{:S(2)}) %collective-permute-start.45) | collective-permute-done | bytes 262176 | tf_op jit(solution)/shard_map/ppermute | solution.py:542
  258.8 10.0 %collective-permute-done.61 = bf16[4,256,256]{2,1,0:T(8,128)(2,1)S(1)} collective-permute-done((bf16[4,256,256]{2,1,0:T(8,128)(2,1)S(1)}, bf16[4,256,256]{2,1,0:T(8,128)(2,1)S(1)}, u32[]{:S(2)}, u32[]{:S(2)}) %collective-permute-start.61) | collective-permute-done | bytes 524320 | tf_op jit(solution)/shard_map/ppermute | solution.py:539
  268.8 5.0 collective-permute-start.59
  274.1 6.0 %collective-permute-done.49 = bf16[4,128,512]{2,1,0:T(8,128)(2,1)S(1)} collective-permute-done((bf16[4,128,512]{2,1,0:T(8,128)(2,1)S(1)}, bf16[4,128,512]{2,1,0:T(8,128)(2,1)S(1)}, u32[]{:S(2)}, u32[]{:S(2)}) %collective-permute-start.49) | collective-permute-done | bytes 524320 | tf_op jit(solution)/shard_map/ppermute | solution.py:539
  280.0 4.4 collective-permute-start.47
  284.6 4.5 collective-permute-start.62
  298.3 5.4 %collective-permute-done.63 = bf16[256,256]{1,0:T(8,128)(2,1)S(1)} collective-permute-done((bf16[256,256]{1,0:T(8,128)(2,1)S(1)}, bf16[256,256]{1,0:T(8,128)(2,1)S(1)}, u32[]{:S(2)}, u32[]{:S(2)}) %collective-permute-start.63) | collective-permute-done | bytes 131104 | tf_op jit(solution)/shard_map/ppermute | solution.py:542
  305.4 5.8 %collective-permute-done.51 = bf16[128,512]{1,0:T(8,128)(2,1)S(1)} collective-permute-done((bf16[128,512]{1,0:T(8,128)(2,1)S(1)}, bf16[128,512]{1,0:T(8,128)(2,1)S(1)}, u32[]{:S(2)}, u32[]{:S(2)}) %collective-permute-start.51) | collective-permute-done | bytes 131104 | tf_op jit(solution)/shard_map/ppermute | solution.py:542
  319.5 10.9 %dense_norm_back.1 = (f32[1024,1024]{1,0:T(8,128)}, bf16[1024,1024]{1,0:T(8,128)(2,1)}, bf16[1024,512]{1,0:T(8,128)(2,1)}, f32[8,1024]{1,0:T(8,128)}) custom-call(s32[3]{0:T(128)} %pad_add_fusion.3.info_ref, bf16[1024,1024]{1,0:T(8,128)(2,1)} %raise_input_back.1.a_ref, bf16[1024,1024]{1,0:T(8,128)(2,1)} %collective-permute-done.14.b_ref, ...), custom_call_target="tpu_custom_call" | custom-call | flops 1073741824 | bytes 19976192 | tf_op jit(solution)/shard_map/dense_norm_back/pallas_call | solution.py:38
  330.4 18.0 %attend_backward.3 = (bf16[1024,256]{1,0:T(8,128)(2,1)}, bf16[1024,256]{1,0:T(8,128)(2,1)}, bf16[1024,256]{1,0:T(8,128)(2,1)}) custom-call(s32[3]{0:T(128)} %pad_add_fusion.3.info_ref, bf16[1024,1536]{1,0:T(8,128)(2,1)} %get-tuple-element.39.q_ref.k_ref.v_ref, bf16[1024,512]{1,0:T(8,128)(2,1)} %get-tuple-element.46.g_ref, ...), custom_call_target="tpu_custom_call" | custom-call | flops 10737418240 | bytes 15204352 | tf_op jit(solution)/shard_map/attend_backward/pallas_call | solution.py:38
  348.4 17.9 %attend_backward.2 = (bf16[1024,256]{1,0:T(8,128)(2,1)}, bf16[1024,256]{1,0:T(8,128)(2,1)}, bf16[1024,256]{1,0:T(8,128)(2,1)}) custom-call(s32[3]{0:T(128)} %pad_add_fusion.3.info_ref, bf16[1024,1536]{1,0:T(8,128)(2,1)} %get-tuple-element.39.q_ref.k_ref.v_ref, bf16[1024,512]{1,0:T(8,128)(2,1)} %get-tuple-element.46.g_ref, ...), custom_call_target="tpu_custom_call" | custom-call | flops 10737418240 | bytes 15204352 | tf_op jit(solution)/shard_map/attend_backward/pallas_call | solution.py:38
  366.8 5.7 %out_gradient.1 = bf16[512,1024]{1,0:T(8,128)(2,1)} custom-call(s32[5]{0:T(128)} %constant.434.clone.1.index_ref, bf16[1024,512]{1,0:T(8,128)(2,1)} %get-tuple-element.40.mine_ref.o_ref.lhs_ref, bf16[1024,1024]{1,0:T(8,128)(2,1)} %get-tuple-element.60.refs_0_), custom_call_target="tpu_custom_call" | custom-call | flops 1073741824 | bytes 4194304 | tf_op jit(solution)/shard_map/out_gradient/pallas_call | solution.py:38
  374.2 5.3 in_gradient.5
  381.0 7.8 %in_gradient.6 = bf16[1024,384]{1,0:T(8,128)(2,1)} custom-call(s32[9]{0:T(128)} %get-tuple-element.149.index_ref, bf16[1024,1024]{1,0:T(8,128)(2,1)} %get-tuple-element.59.lhs_ref, bf16[1024,256]{1,0:T(8,128)(2,1)} %get-tuple-element.49.refs_1_.refs_0_, bf16[1024,256]{1,0:T(8,128)(2,1)} %get-tuple-element.51.refs_3_.refs_1_, ...), custom_call_target="tpu_custom_call" | custom-call | flops 805306368 | bytes 4456448 | tf_op jit(solution)/shard_map/in_gradient/pallas_call | solution.py:38
  388.9 6.0 %project_back.3 = bf16[512,1024]{1,0:T(8,128)(2,1)} custom-call(s32[3]{0:T(128)} %pad_add_fusion.5.index_ref, bf16[1024,256]{1,0:T(8,128)(2,1)} %get-tuple-element.48.refs_0_, bf16[1024,256]{1,0:T(8,128)(2,1)} %get-tuple-element.49.refs_1_.refs_0_, bf16[1024,256]{1,0:T(8,128)(2,1)} %get-tuple-element.50.refs_2_.refs_1_, ...), custom_call_target="tpu_custom_call" | custom-call | flops 1610612736 | bytes 23068672 | tf_op jit(solution)/shard_map/project_back/pallas_call | solution.py:38
  394.8 7.8 %in_gradient.7 = bf16[1024,384]{1,0:T(8,128)(2,1)} custom-call(s32[9]{0:T(128)} %get-tuple-element.150.index_ref, bf16[1024,1024]{1,0:T(8,128)(2,1)} %get-tuple-element.59.lhs_ref, bf16[1024,256]{1,0:T(8,128)(2,1)} %get-tuple-element.49.refs_1_.refs_0_, bf16[1024,256]{1,0:T(8,128)(2,1)} %get-tuple-element.51.refs_3_.refs_1_, ...), custom_call_target="tpu_custom_call" | custom-call | flops 805306368 | bytes 4456448 | tf_op jit(solution)/shard_map/in_gradient/pallas_call | solution.py:38
  406.2 5.3 in_gradient.4
  411.5 6.4 %project_back.2.a_ref = bf16[512,1024]{1,0:T(8,128)(2,1)} custom-call(s32[3]{0:T(128)} %pad_add_fusion.4.index_ref, bf16[1024,256]{1,0:T(8,128)(2,1)} %get-tuple-element.48.refs_0_, bf16[1024,256]{1,0:T(8,128)(2,1)} %get-tuple-element.49.refs_1_.refs_0_, bf16[1024,256]{1,0:T(8,128)(2,1)} %get-tuple-element.50.refs_2_.refs_1_, ...), custom_call_target="tpu_custom_call" | custom-call | flops 1610612736 | bytes 23068672 | tf_op jit(solution)/shard_map/project_back/pallas_call | solution.py:38
  434.2 6.2 %collective-permute-done.27 = bf16[128,768]{1,0:T(8,128)(2,1)} collective-permute-done((bf16[128,768]{1,0:T(8,128)(2,1)}, bf16[128,768]{1,0:T(8,128)(2,1)}, u32[]{:S(2)}, u32[]{:S(2)}) %collective-permute-start.27) | collective-permute-done | bytes 196640 | tf_op jit(solution)/shard_map/ppermute | solution.py:542
  442.8 5.2 attend_norm_back.1
  452.6 4.6 collective-permute-start.39
  463.2 5.2 collective-permute-done.40
  481.2 13.6 %collective-permute-done.33 = bf16[128,384]{0,1:T(8,128)(2,1)} collective-permute-done((bf16[128,384]{0,1:T(8,128)(2,1)}, bf16[128,384]{0,1:T(8,128)(2,1)}, u32[]{:S(2)}, u32[]{:S(2)}) %collective-permute-start.33) | collective-permute-done | bytes 98336 | tf_op jit(solution)/shard_map/ppermute | solution.py:542
  525.9 6.0 %collective-permute-done.17 = bf16[256,1024]{1,0:T(8,128)(2,1)S(1)} collective-permute-done((bf16[256,1024]{1,0:T(8,128)(2,1)S(1)}, bf16[256,1024]{1,0:T(8,128)(2,1)S(1)}, u32[]{:S(2)}, u32[]{:S(2)}) %collective-permute-start.17) | collective-permute-done | bytes 524320 | tf_op jit(solution)/shard_map/ppermute | solution.py:578
  (334 shorter events, 159.3 us)
Async XLA Ops:
  2.1 12.8 %collective-permute-start = (s32[2,1]{0,1:T(1,128)S(1)}, s32[2,1]{0,1:T(1,128)S(1)}, u32[]{:S(2)}, u32[]{:S(2)}) collective-permute-start(s32[2,1]{0,1:T(1,128)S(1)} %pad_add_fusion.2), channel_id=1, source_target_pairs={{0,2},{2,0},{4,6},{6,4},{8,10},{10,8},{12,14},{14,12},{16,18},{18,... | collective-permute-start | bytes 32 | tf_op jit(solution)/shard_map/ppermute | solution.py:538
  2.6 39.0 %collective-permute-start.4 = (bf16[512,1024]{1,0:T(8,128)(2,1)}, bf16[512,1024]{1,0:T(8,128)(2,1)S(1)}, u32[]{:S(2)}, u32[]{:S(2)}) collective-permute-start(bf16[512,1024]{1,0:T(8,128)(2,1)} %bitcast.248), channel_id=1, source_target_pairs={{0,2},{2,0},{4,6},{6,4},{8,10},{10,8},{12,14},{14,12},{16,18},{18,... | collective-permute-start | bytes 3145736 | tf_op jit(solution)/shard_map/ppermute | solution.py:538
  4.9 21.7 %collective-permute-start.1 = (bf16[256,1024]{1,0:T(8,128)(2,1)}, bf16[256,1024]{1,0:T(8,128)(2,1)S(1)}, u32[]{:S(2)}, u32[]{:S(2)}) collective-permute-start(bf16[256,1024]{1,0:T(8,128)(2,1)} %get-tuple-element.99), channel_id=1, source_target_pairs={{2,1},{1,0},{6,5},{5,4},{10,9},{9,8},{14,13},{13,12},{18,17},{17,1... | collective-permute-start | bytes 1572872 | tf_op jit(solution)/shard_map/ppermute | solution.py:568
  6.2 28.2 %collective-permute-start.2 = (bf16[256,1024]{1,0:T(8,128)(2,1)}, bf16[256,1024]{1,0:T(8,128)(2,1)}, u32[]{:S(2)}, u32[]{:S(2)}) collective-permute-start(bf16[256,1024]{1,0:T(8,128)(2,1)} %get-tuple-element.98), channel_id=1, source_target_pairs={{2,3},{1,2},{6,7},{5,6},{10,11},{9,10},{14,15},{13,14},{18,19},{17... | collective-permute-start | bytes 1572872 | tf_op jit(solution)/shard_map/ppermute | solution.py:568
  8.7 29.5 %collective-permute-start.11 = (bf16[256,1024]{1,0:T(8,128)(2,1)}, bf16[256,1024]{1,0:T(8,128)(2,1)S(1)}, u32[]{:S(2)}, u32[]{:S(2)}) collective-permute-start(bf16[256,1024]{1,0:T(8,128)(2,1)} %get-tuple-element.93), channel_id=1, source_target_pairs={{2,1},{1,0},{6,5},{5,4},{10,9},{9,8},{14,13},{13,12},{18,17},{17,1... | collective-permute-start | bytes 1572872 | tf_op jit(solution)/shard_map/ppermute | solution.py:568
  14.9 23.3 %collective-permute-start.12 = (bf16[256,1024]{1,0:T(8,128)(2,1)}, bf16[256,1024]{1,0:T(8,128)(2,1)}, u32[]{:S(2)}, u32[]{:S(2)}) collective-permute-start(bf16[256,1024]{1,0:T(8,128)(2,1)} %get-tuple-element.92), channel_id=1, source_target_pairs={{2,3},{1,2},{6,7},{5,6},{10,11},{9,10},{14,15},{13,14},{18,19},{17... | collective-permute-start | bytes 1572872 | tf_op jit(solution)/shard_map/ppermute | solution.py:568
  26.5 52.3 %collective-permute-start.10 = (bf16[512,1024]{1,0:T(8,128)(2,1)S(1)}, bf16[512,1024]{1,0:T(8,128)(2,1)}, u32[]{:S(2)}, u32[]{:S(2)}) collective-permute-start(bf16[512,1024]{1,0:T(8,128)(2,1)S(1)} %bitcast.249), channel_id=1, source_target_pairs={{0,2},{2,0},{4,6},{6,4},{8,10},{10,8},{12,14},{14,12},{16,18},{18,... | collective-permute-start | bytes 3145736 | tf_op jit(solution)/shard_map/ppermute | solution.py:538
  38.3 40.5 %collective-permute-start.13 = (bf16[256,1024]{1,0:T(8,128)(2,1)S(1)}, bf16[256,1024]{1,0:T(8,128)(2,1)S(1)}, u32[]{:S(2)}, u32[]{:S(2)}) collective-permute-start(bf16[256,1024]{1,0:T(8,128)(2,1)S(1)} %broadcast_select_fusion.7), channel_id=1, source_target_pairs={{0,2},{2,0},{4,6},{6,4},{8,10},{10,8},{12,14},{14,12},{16,18},{18,... | collective-permute-start | bytes 1572872 | tf_op jit(solution)/shard_map/ppermute | solution.py:538
  116.6 92.9 %collective-permute-start.55 = (bf16[1024,512]{1,0:T(8,128)(2,1)}, bf16[1024,512]{1,0:T(8,128)(2,1)}, u32[]{:S(2)}, u32[]{:S(2)}) collective-permute-start(bf16[1024,512]{1,0:T(8,128)(2,1)} %down_gradient.5), channel_id=1, source_target_pairs={{0,4},{2,6},{4,0},{6,2},{8,12},{10,14},{12,8},{14,10},{16,20},{18,... | collective-permute-start | bytes 3145736 | tf_op jit(solution)/shard_map/ppermute | solution.py:539
  126.1 92.3 %collective-permute-start.60 = (bf16[2048,256]{1,0:T(8,128)(2,1)}, bf16[2048,256]{1,0:T(8,128)(2,1)S(1)}, u32[]{:S(2)}, u32[]{:S(2)}) collective-permute-start(bf16[2048,256]{1,0:T(8,128)(2,1)} %down_gradient.7), channel_id=1, source_target_pairs={{0,1},{1,0},{2,3},{3,2},{4,5},{5,4},{6,7},{7,6},{8,9},{9,8},{10,11... | collective-permute-start | bytes 3145736 | tf_op jit(solution)/shard_map/ppermute | solution.py:545
  153.3 66.2 %collective-permute-start.48 = (bf16[1024,512]{1,0:T(8,128)(2,1)}, bf16[1024,512]{1,0:T(8,128)(2,1)S(1)}, u32[]{:S(2)}, u32[]{:S(2)}) collective-permute-start(bf16[1024,512]{1,0:T(8,128)(2,1)} %up_gradient.7), channel_id=1, source_target_pairs={{0,1},{1,0},{2,3},{3,2},{4,5},{5,4},{6,7},{7,6},{8,9},{9,8},{10,11... | collective-permute-start | bytes 3145736 | tf_op jit(solution)/shard_map/ppermute | solution.py:545
  159.1 56.7 %collective-permute-start.43 = (bf16[512,1024]{1,0:T(8,128)(2,1)}, bf16[512,1024]{1,0:T(8,128)(2,1)S(1)}, u32[]{:S(2)}, u32[]{:S(2)}) collective-permute-start(bf16[512,1024]{1,0:T(8,128)(2,1)} %up_gradient.5), channel_id=1, source_target_pairs={{0,4},{2,6},{4,0},{6,2},{8,12},{10,14},{12,8},{14,10},{16,20},{18,... | collective-permute-start | bytes 3145736 | tf_op jit(solution)/shard_map/ppermute | solution.py:539
  166.3 46.5 %collective-permute-start.6 = (bf16[512,1024]{1,0:T(8,128)(2,1)}, bf16[512,1024]{1,0:T(8,128)(2,1)S(1)}, u32[]{:S(2)}, u32[]{:S(2)}) collective-permute-start(bf16[512,1024]{1,0:T(8,128)(2,1)} %lower.3), channel_id=1, source_target_pairs={{0,2},{2,0},{4,6},{6,4},{8,10},{10,8},{12,14},{14,12},{16,18},{18,... | collective-permute-start | bytes 3145736 | tf_op jit(solution)/shard_map/ppermute | solution.py:538
  212.8 20.7 %collective-permute-start.57 = (bf16[256,512]{1,0:T(8,128)(2,1)S(1)}, bf16[256,512]{1,0:T(8,128)(2,1)S(1)}, u32[]{:S(2)}, u32[]{:S(2)}) collective-permute-start(bf16[256,512]{1,0:T(8,128)(2,1)S(1)} %get-tuple-element.83), channel_id=1, source_target_pairs={{0,16},{2,18},{4,20},{6,22},{8,24},{10,26},{12,28},{14,30},{16,0},... | collective-permute-start | bytes 786440 | tf_op jit(solution)/shard_map/ppermute | solution.py:542
  215.8 17.7 %collective-permute-start.58 = (bf16[256,512]{1,0:T(8,128)(2,1)S(1)}, bf16[256,512]{1,0:T(8,128)(2,1)S(1)}, u32[]{:S(2)}, u32[]{:S(2)}) collective-permute-start(bf16[256,512]{1,0:T(8,128)(2,1)S(1)} %get-tuple-element.82), channel_id=1, source_target_pairs={{0,24},{2,26},{4,28},{6,30},{8,0},{10,2},{12,4},{14,6},{16,8},{18,... | collective-permute-start | bytes 786440 | tf_op jit(solution)/shard_map/ppermute | solution.py:542
  218.3 20.8 %collective-permute-start.44 = (bf16[128,1024]{1,0:T(8,128)(2,1)S(1)}, bf16[128,1024]{1,0:T(8,128)(2,1)S(1)}, u32[]{:S(2)}, u32[]{:S(2)}) collective-permute-start(bf16[128,1024]{1,0:T(8,128)(2,1)S(1)} %get-tuple-element.84), channel_id=1, source_target_pairs={{0,8},{2,10},{4,12},{6,14},{8,16},{10,18},{12,20},{14,22},{16,24},... | collective-permute-start | bytes 786440 | tf_op jit(solution)/shard_map/ppermute | solution.py:542
  219.5 36.1 %collective-permute-start.45 = (bf16[128,1024]{1,0:T(8,128)(2,1)S(1)}, bf16[128,1024]{1,0:T(8,128)(2,1)S(1)}, u32[]{:S(2)}, u32[]{:S(2)}) collective-permute-start(bf16[128,1024]{1,0:T(8,128)(2,1)S(1)} %get-tuple-element.86), channel_id=1, source_target_pairs={{0,16},{2,18},{4,20},{6,22},{8,24},{10,26},{12,28},{14,30},{16,0},... | collective-permute-start | bytes 786440 | tf_op jit(solution)/shard_map/ppermute | solution.py:542
  222.3 34.1 %collective-permute-start.46 = (bf16[128,1024]{1,0:T(8,128)(2,1)S(1)}, bf16[128,1024]{1,0:T(8,128)(2,1)S(1)}, u32[]{:S(2)}, u32[]{:S(2)}) collective-permute-start(bf16[128,1024]{1,0:T(8,128)(2,1)S(1)} %get-tuple-element.85), channel_id=1, source_target_pairs={{0,24},{2,26},{4,28},{6,30},{8,0},{10,2},{12,4},{14,6},{16,8},{18,... | collective-permute-start | bytes 786440 | tf_op jit(solution)/shard_map/ppermute | solution.py:542
  233.5 24.6 %collective-permute-start.7 = (bf16[256,1024]{1,0:T(8,128)(2,1)S(1)}, bf16[256,1024]{1,0:T(8,128)(2,1)S(1)}, u32[]{:S(2)}, u32[]{:S(2)}) collective-permute-start(bf16[256,1024]{1,0:T(8,128)(2,1)S(1)} %get-tuple-element.95), channel_id=1, source_target_pairs={{0,2},{2,0},{4,6},{6,4},{8,10},{10,8},{12,14},{14,12},{16,18},{18,... | collective-permute-start | bytes 1572872 | tf_op jit(solution)/shard_map/ppermute | solution.py:538
  233.6 85.9 %collective-permute-start.14 = (bf16[1024,1024]{1,0:T(8,128)(2,1)S(1)}, bf16[1024,1024]{1,0:T(8,128)(2,1)}, u32[]{:S(2)}, u32[]{:S(2)}) collective-permute-start(bf16[1024,1024]{1,0:T(8,128)(2,1)S(1)} %copy-done.2), channel_id=1, source_target_pairs={{0,2},{2,0},{4,6},{6,4},{8,10},{10,8},{12,14},{14,12},{16,18},{18,... | collective-permute-start | bytes 6291464 | tf_op jit(solution)/shard_map/ppermute | solution.py:538
  239.2 45.4 %collective-permute-start.8 = (bf16[256,1024]{1,0:T(8,128)(2,1)S(1)}, bf16[256,1024]{1,0:T(8,128)(2,1)S(1)}, u32[]{:S(2)}, u32[]{:S(2)}) collective-permute-start(bf16[256,1024]{1,0:T(8,128)(2,1)S(1)} %get-tuple-element.94), channel_id=1, source_target_pairs={{1,2},{0,1},{5,6},{4,5},{9,10},{8,9},{13,14},{12,13},{17,18},{16,1... | collective-permute-start | bytes 1572872 | tf_op jit(solution)/shard_map/ppermute | solution.py:578
  255.7 33.5 %collective-permute-start.9 = (bf16[256,1024]{1,0:T(8,128)(2,1)S(1)}, bf16[256,1024]{1,0:T(8,128)(2,1)S(1)}, u32[]{:S(2)}, u32[]{:S(2)}) collective-permute-start(bf16[256,1024]{1,0:T(8,128)(2,1)S(1)} %get-tuple-element.94), channel_id=1, source_target_pairs={{3,2},{2,1},{7,6},{6,5},{11,10},{10,9},{15,14},{14,13},{19,18},{18... | collective-permute-start | bytes 1572872 | tf_op jit(solution)/shard_map/ppermute | solution.py:578
  256.4 12.4 %collective-permute-start.61 = (bf16[4,256,256]{2,1,0:T(8,128)(2,1)S(1)}, bf16[4,256,256]{2,1,0:T(8,128)(2,1)S(1)}, u32[]{:S(2)}, u32[]{:S(2)}) collective-permute-start(bf16[4,256,256]{2,1,0:T(8,128)(2,1)S(1)} %dynamic-slice_bitcast_fusion), channel_id=1, source_target_pairs={{0,4},{2,6},{4,0},{6,2},{8,12},{10,14},{12,8},{14,10},{16,20},{18,... | collective-permute-start | bytes 1572872 | tf_op jit(solution)/shard_map/ppermute | solution.py:539
  258.1 21.9 %collective-permute-start.49 = (bf16[4,128,512]{2,1,0:T(8,128)(2,1)S(1)}, bf16[4,128,512]{2,1,0:T(8,128)(2,1)S(1)}, u32[]{:S(2)}, u32[]{:S(2)}) collective-permute-start(bf16[4,128,512]{2,1,0:T(8,128)(2,1)S(1)} %dynamic-slice_bitcast_fusion.1), channel_id=1, source_target_pairs={{0,4},{2,6},{4,0},{6,2},{8,12},{10,14},{12,8},{14,10},{16,20},{18,... | collective-permute-start | bytes 1572872 | tf_op jit(solution)/shard_map/ppermute | solution.py:539
  268.8 24.8 %collective-permute-start.59 = (bf16[256,512]{1,0:T(8,128)(2,1)S(1)}, bf16[256,512]{1,0:T(8,128)(2,1)S(1)}, u32[]{:S(2)}, u32[]{:S(2)}) collective-permute-start(bf16[256,512]{1,0:T(8,128)(2,1)S(1)} %fusion.11), channel_id=1, source_target_pairs={{0,1},{1,0},{2,3},{3,2},{4,5},{5,4},{6,7},{7,6},{8,9},{9,8},{10,11... | collective-permute-start | bytes 786440 | tf_op jit(solution)/shard_map/ppermute | solution.py:545
  280.0 13.7 %collective-permute-start.47 = (bf16[128,1024]{1,0:T(8,128)(2,1)S(1)}, bf16[128,1024]{1,0:T(8,128)(2,1)S(1)}, u32[]{:S(2)}, u32[]{:S(2)}) collective-permute-start(bf16[128,1024]{1,0:T(8,128)(2,1)S(1)} %fusion.14), channel_id=1, source_target_pairs={{0,1},{1,0},{2,3},{3,2},{4,5},{5,4},{6,7},{7,6},{8,9},{9,8},{10,11... | collective-permute-start | bytes 786440 | tf_op jit(solution)/shard_map/ppermute | solution.py:545
  289.1 14.7 %collective-permute-start.63 = (bf16[256,256]{1,0:T(8,128)(2,1)S(1)}, bf16[256,256]{1,0:T(8,128)(2,1)S(1)}, u32[]{:S(2)}, u32[]{:S(2)}) collective-permute-start(bf16[256,256]{1,0:T(8,128)(2,1)S(1)} %get-tuple-element.111), channel_id=1, source_target_pairs={{0,16},{2,18},{4,20},{6,22},{8,24},{10,26},{12,28},{14,30},{16,0},... | collective-permute-start | bytes 393224 | tf_op jit(solution)/shard_map/ppermute | solution.py:542
  293.6 11.6 %collective-permute-start.64 = (bf16[256,256]{1,0:T(8,128)(2,1)S(1)}, bf16[256,256]{1,0:T(8,128)(2,1)S(1)}, u32[]{:S(2)}, u32[]{:S(2)}) collective-permute-start(bf16[256,256]{1,0:T(8,128)(2,1)S(1)} %get-tuple-element.110), channel_id=1, source_target_pairs={{0,24},{2,26},{4,28},{6,30},{8,0},{10,2},{12,4},{14,6},{16,8},{18,... | collective-permute-start | bytes 393224 | tf_op jit(solution)/shard_map/ppermute | solution.py:542
  293.7 11.6 %collective-permute-start.50 = (bf16[128,512]{1,0:T(8,128)(2,1)S(1)}, bf16[128,512]{1,0:T(8,128)(2,1)S(1)}, u32[]{:S(2)}, u32[]{:S(2)}) collective-permute-start(bf16[128,512]{1,0:T(8,128)(2,1)S(1)} %get-tuple-element.112), channel_id=1, source_target_pairs={{0,8},{2,10},{4,12},{6,14},{8,16},{10,18},{12,20},{14,22},{16,24},... | collective-permute-start | bytes 393224 | tf_op jit(solution)/shard_map/ppermute | solution.py:542
  296.1 15.1 %collective-permute-start.51 = (bf16[128,512]{1,0:T(8,128)(2,1)S(1)}, bf16[128,512]{1,0:T(8,128)(2,1)S(1)}, u32[]{:S(2)}, u32[]{:S(2)}) collective-permute-start(bf16[128,512]{1,0:T(8,128)(2,1)S(1)} %get-tuple-element.114), channel_id=1, source_target_pairs={{0,16},{2,18},{4,20},{6,22},{8,24},{10,26},{12,28},{14,30},{16,0},... | collective-permute-start | bytes 393224 | tf_op jit(solution)/shard_map/ppermute | solution.py:542
  317.3 49.1 %collective-permute-start.54 = (bf16[64,1,2048]{2,0,1:T(8,128)(2,1)S(1)}, bf16[64,1,2048]{2,0,1:T(8,128)(2,1)S(1)}, u32[]{:S(2)}, u32[]{:S(2)}) collective-permute-start(bf16[64,1,2048]{2,0,1:T(8,128)(2,1)S(1)} %fusion.19), channel_id=1, source_target_pairs={{0,2},{2,0},{4,6},{6,4},{8,10},{10,8},{12,14},{14,12},{16,18},{18,... | collective-permute-start | bytes 786440 | tf_op jit(solution)/shard_map/ppermute | solution.py:538
  373.6 44.2 %collective-permute-start.37 = (bf16[4,64,1024]{2,1,0:T(8,128)(2,1)S(1)}, bf16[4,64,1024]{2,1,0:T(8,128)(2,1)}, u32[]{:S(2)}, u32[]{:S(2)}) collective-permute-start(bf16[4,64,1024]{2,1,0:T(8,128)(2,1)S(1)} %dynamic-slice_bitcast_fusion.2), channel_id=1, source_target_pairs={{0,2},{2,0},{4,6},{6,4},{8,10},{10,8},{12,14},{14,12},{16,18},{18,... | collective-permute-start | bytes 1572872 | tf_op jit(solution)/shard_map/ppermute | solution.py:538
  379.5 41.1 %collective-permute-start.25 = (bf16[512,768]{1,0:T(8,128)(2,1)}, bf16[512,768]{1,0:T(8,128)(2,1)}, u32[]{:S(2)}, u32[]{:S(2)}) collective-permute-start(bf16[512,768]{1,0:T(8,128)(2,1)} %in_gradient.5), channel_id=1, source_target_pairs={{0,4},{2,6},{4,0},{6,2},{8,12},{10,14},{12,8},{14,10},{16,20},{18,... | collective-permute-start | bytes 2359304 | tf_op jit(solution)/shard_map/ppermute | solution.py:539
  405.3 20.9 %collective-permute-start.30 = (bf16[1024,384]{1,0:T(8,128)(2,1)S(1)}, bf16[1024,384]{1,0:T(8,128)(2,1)S(1)}, u32[]{:S(2)}, u32[]{:S(2)}) collective-permute-start(bf16[1024,384]{1,0:T(8,128)(2,1)S(1)} %copy-done.18), channel_id=1, source_target_pairs={{0,1},{1,0},{2,3},{3,2},{4,5},{5,4},{6,7},{7,6},{8,9},{9,8},{10,11... | collective-permute-start | bytes 2359304 | tf_op jit(solution)/shard_map/ppermute | solution.py:545
  406.2 36.6 %collective-permute-start.15 = (bf16[512,1024]{1,0:T(8,128)(2,1)S(1)}, bf16[512,1024]{1,0:T(8,128)(2,1)}, u32[]{:S(2)}, u32[]{:S(2)}) collective-permute-start(bf16[512,1024]{1,0:T(8,128)(2,1)S(1)} %copy-done.15), channel_id=1, source_target_pairs={{0,2},{2,0},{4,6},{6,4},{8,10},{10,8},{12,14},{14,12},{16,18},{18,... | collective-permute-start | bytes 3145736 | tf_op jit(solution)/shard_map/ppermute | solution.py:538
  420.0 29.1 %collective-permute-start.38 = (bf16[256,1024]{1,0:T(8,128)(2,1)}, bf16[256,1024]{1,0:T(8,128)(2,1)}, u32[]{:S(2)}, u32[]{:S(2)}) collective-permute-start(bf16[256,1024]{1,0:T(8,128)(2,1)} %bitcast.66), channel_id=1, source_target_pairs={{0,4},{2,6},{4,0},{6,2},{8,12},{10,14},{12,8},{14,10},{16,20},{18,... | collective-permute-start | bytes 1572872 | tf_op jit(solution)/shard_map/ppermute | solution.py:539
  426.1 14.3 %collective-permute-start.27 = (bf16[128,768]{1,0:T(8,128)(2,1)}, bf16[128,768]{1,0:T(8,128)(2,1)}, u32[]{:S(2)}, u32[]{:S(2)}) collective-permute-start(bf16[128,768]{1,0:T(8,128)(2,1)} %get-tuple-element.108), channel_id=1, source_target_pairs={{0,16},{2,18},{4,20},{6,22},{8,24},{10,26},{12,28},{14,30},{16,0},... | collective-permute-start | bytes 589832 | tf_op jit(solution)/shard_map/ppermute | solution.py:542
  426.2 14.2 %collective-permute-start.28 = (bf16[128,768]{1,0:T(8,128)(2,1)}, bf16[128,768]{1,0:T(8,128)(2,1)S(1)}, u32[]{:S(2)}, u32[]{:S(2)}) collective-permute-start(bf16[128,768]{1,0:T(8,128)(2,1)} %get-tuple-element.107), channel_id=1, source_target_pairs={{0,24},{2,26},{4,28},{6,30},{8,0},{10,2},{12,4},{14,6},{16,8},{18,... | collective-permute-start | bytes 589832 | tf_op jit(solution)/shard_map/ppermute | solution.py:542
  432.7 38.5 %collective-permute-start.31 = (bf16[4,128,384]{1,2,0:T(8,128)(2,1)}, bf16[4,128,384]{1,2,0:T(8,128)(2,1)}, u32[]{:S(2)}, u32[]{:S(2)}) collective-permute-start(bf16[4,128,384]{1,2,0:T(8,128)(2,1)} %bitcast.47), channel_id=1, source_target_pairs={{0,4},{2,6},{4,0},{6,2},{8,12},{10,14},{12,8},{14,10},{16,20},{18,... | collective-permute-start | bytes 1179656 | tf_op jit(solution)/shard_map/ppermute | solution.py:539
  441.5 33.6 %collective-permute-start.29 = (bf16[128,768]{1,0:T(8,128)(2,1)S(1)}, bf16[128,768]{1,0:T(8,128)(2,1)S(1)}, u32[]{:S(2)}, u32[]{:S(2)}) collective-permute-start(bf16[128,768]{1,0:T(8,128)(2,1)S(1)} %fusion.17), channel_id=1, source_target_pairs={{0,1},{1,0},{2,3},{3,2},{4,5},{5,4},{6,7},{7,6},{8,9},{9,8},{10,11... | collective-permute-start | bytes 589832 | tf_op jit(solution)/shard_map/ppermute | solution.py:545
  463.2 54.1 %collective-permute-start.16 = (bf16[256,1024]{1,0:T(8,128)(2,1)S(1)}, bf16[256,1024]{1,0:T(8,128)(2,1)}, u32[]{:S(2)}, u32[]{:S(2)}) collective-permute-start(bf16[256,1024]{1,0:T(8,128)(2,1)S(1)} %slice.121), channel_id=1, source_target_pairs={{0,2},{2,0},{4,6},{6,4},{8,10},{10,8},{12,14},{14,12},{16,18},{18,... | collective-permute-start | bytes 1572872 | tf_op jit(solution)/shard_map/ppermute | solution.py:538
  470.1 25.8 %collective-permute-start.42 = (bf16[64,1024]{1,0:T(8,128)(2,1)}, bf16[64,1024]{1,0:T(8,128)(2,1)}, u32[]{:S(2)}, u32[]{:S(2)}) collective-permute-start(bf16[64,1024]{1,0:T(8,128)(2,1)} %fusion.30), channel_id=1, source_target_pairs={{0,1},{1,0},{2,3},{3,2},{4,5},{5,4},{6,7},{7,6},{8,9},{9,8},{10,11... | collective-permute-start | bytes 393224 | tf_op jit(solution)/shard_map/ppermute | solution.py:545
  475.2 19.6 %collective-permute-start.33 = (bf16[128,384]{0,1:T(8,128)(2,1)}, bf16[128,384]{0,1:T(8,128)(2,1)}, u32[]{:S(2)}, u32[]{:S(2)}) collective-permute-start(bf16[128,384]{0,1:T(8,128)(2,1)} %get-tuple-element.120), channel_id=1, source_target_pairs={{0,16},{2,18},{4,20},{6,22},{8,24},{10,26},{12,28},{14,30},{16,0},... | collective-permute-start | bytes 294920 | tf_op jit(solution)/shard_map/ppermute | solution.py:542
  477.3 17.5 %collective-permute-start.34 = (bf16[128,384]{0,1:T(8,128)(2,1)}, bf16[128,384]{0,1:T(8,128)(2,1)S(1)}, u32[]{:S(2)}, u32[]{:S(2)}) collective-permute-start(bf16[128,384]{0,1:T(8,128)(2,1)} %get-tuple-element.119), channel_id=1, source_target_pairs={{0,24},{2,26},{4,28},{6,30},{8,0},{10,2},{12,4},{14,6},{16,8},{18,... | collective-permute-start | bytes 294920 | tf_op jit(solution)/shard_map/ppermute | solution.py:542
  480.7 20.6 %collective-permute-start.22 = (f32[4,13,1024]{2,1,0:T(8,128)S(1)}, f32[4,13,1024]{2,1,0:T(8,128)S(1)}, u32[]{:S(2)}, u32[]{:S(2)}) collective-permute-start(f32[4,13,1024]{2,1,0:T(8,128)S(1)} %pad_maximum_fusion.7), channel_id=1, source_target_pairs={{0,8},{2,10},{4,12},{6,14},{8,16},{10,18},{12,20},{14,22},{16,24},... | collective-permute-start | bytes 638984 | tf_op jit(solution)/shard_map/ppermute | solution.py:542
  494.8 13.2 %collective-permute-start.24 = (f32[4,13,1024]{2,1,0:T(8,128)S(1)}, f32[4,13,1024]{2,1,0:T(8,128)}, u32[]{:S(2)}, u32[]{:S(2)}) collective-permute-start(f32[4,13,1024]{2,1,0:T(8,128)S(1)} %pad_maximum_fusion.7), channel_id=1, source_target_pairs={{0,24},{2,26},{4,28},{6,30},{8,0},{10,2},{12,4},{14,6},{16,8},{18,... | collective-permute-start | bytes 638984 | tf_op jit(solution)/shard_map/ppermute | solution.py:542
  501.2 21.2 %collective-permute-start.36 = (bf16[64,3,512]{2,1,0:T(4,128)(2,1)S(1)}, bf16[64,3,512]{2,1,0:T(4,128)(2,1)}, u32[]{:S(2)}, u32[]{:S(2)}) collective-permute-start(bf16[64,3,512]{2,1,0:T(4,128)(2,1)S(1)} %dynamic-slice_bitcast_fusion.9), channel_id=1, source_target_pairs={{0,2},{2,0},{4,6},{6,4},{8,10},{10,8},{12,14},{14,12},{16,18},{18,... | collective-permute-start | bytes 589832 | tf_op jit(solution)/shard_map/ppermute | solution.py:538
  518.5 13.4 %collective-permute-start.17 = (bf16[256,1024]{1,0:T(8,128)(2,1)S(1)}, bf16[256,1024]{1,0:T(8,128)(2,1)S(1)}, u32[]{:S(2)}, u32[]{:S(2)}) collective-permute-start(bf16[256,1024]{1,0:T(8,128)(2,1)S(1)} %get-tuple-element.89), channel_id=1, source_target_pairs={{1,2},{0,1},{5,6},{4,5},{9,10},{8,9},{13,14},{12,13},{17,18},{16,1... | collective-permute-start | bytes 1572872 | tf_op jit(solution)/shard_map/ppermute | solution.py:578
  (49 other events, 332.0 us)

commit v2 on v1

v2 whole, which is shorter than its diff:
```python
import functools
import math

import jax
import jax.numpy as jnp
from jax import lax
from jax.experimental import pallas as pl
from jax.experimental.pallas import tpu as pltpu
from jax.sharding import PartitionSpec as P

HD = 64
CORE, OFFSET, LENGTH, NEAR, FAR, X, Z, HALF, Y = range(9)
EPS = 1e-05
COST = 1
MASKED = -1e30
EXP2_SCALE = math.log2(math.e) * HD ** (-0.5)
BF = jnp.bfloat16
F32 = jnp.float32
VMEM = 20 * 1024 * 1024
ROOM = 56 * 1024 * 1024


class Order:
    def __init__(self, info):
        self.info = info

    def run(self, kernel, *args):
        return self.after(kernel(self.info, *args))

    def after(self, values):
        values, self.info = lax.optimization_barrier((values, self.info))
        return values


def sds(shape, dtype):
    return jax.ShapeDtypeStruct(shape, dtype)


def nt(a, b):
    return lax.dot_general(a, b, (((1,), (1,)), ((), ())), preferred_element_type=F32)


def nn(a, b):
    return jnp.dot(a, b, preferred_element_type=F32)


def tn_dot(a, b):
    return lax.dot_general(a, b, (((0,), (0,)), ((), ())), preferred_element_type=F32)


def call(kernel, name, scalars, grid, ins, in_specs, outs, out_specs, scratch=(), flops=0, aliases=None, room=VMEM):
    return pl.pallas_call(
        kernel,
        name=name,
        grid_spec=pltpu.PrefetchScalarGridSpec(
            num_scalar_prefetch=len(scalars),
            grid=grid,
            in_specs=in_specs,
            out_specs=out_specs,
            scratch_shapes=list(scratch),
        ),
        out_shape=outs,
        input_output_aliases=aliases or {},
        compiler_params=pltpu.CompilerParams(
            vmem_limit_bytes=room, dimension_semantics=("arbitrary",) * len(grid)
        ),
        cost_estimate=pl.CostEstimate(flops=COST, bytes_accessed=1, transcendentals=0),
    )(*scalars, *ins)


def norm_rows(v):
    centre = v - jnp.mean(v, axis=-1, keepdims=True)
    inverse = lax.rsqrt(jnp.mean(centre * centre, axis=-1, keepdims=True) + EPS)
    return centre * inverse, inverse


def live_column(rows, first, info_ref, local, total):
    r = first + lax.broadcasted_iota(jnp.int32, (rows, 1), 0)
    low = lax.rem(r, local)
    start = info_ref[OFFSET] - (r - low)
    slot = jnp.where(start < 0, start + total, start) + low
    return slot < info_ref[LENGTH]


def own_projection_kernel(info_ref, q_ref, k_ref, v_ref, out_ref):
    w = q_ref.shape[1]
    for n, ref in enumerate((q_ref, k_ref, v_ref)):
        out_ref[:, n * w : (n + 1) * w] = ref[...]


def own_projection(info, weight):
    d, half = weight.shape[0], weight.shape[1] // 6
    block = min(256, d)
    return call(
        own_projection_kernel, "own_projection", (info,), (d // block,), [weight] * 3,
        [pl.BlockSpec((block, half), lambda i, s, n=n: (i, 2 * n + s[CORE])) for n in range(3)],
        sds((d, 3 * half), BF), pl.BlockSpec((block, 3 * half), lambda i, s: (i, 0)), flops=d * d, room=ROOM,
    )


def own_units_kernel(fb, info_ref, *refs):
    up, down, (up_out, down_out) = refs[:-2:2], refs[1:-2:2], refs[-2:]
    for n, (u, w) in enumerate(zip(up, down, strict=True)):
        up_out[:, n * fb : (n + 1) * fb] = u[...]
        down_out[n * fb : (n + 1) * fb, :] = w[...]


def own_units(info, up, down, fb):
    d, ff = up.shape
    each = 2
    specs = []
    for n in range(each):
        specs.append(pl.BlockSpec((d, fb), lambda i, s, n=n: (0, 2 * (each * i + n) + s[CORE])))
        specs.append(pl.BlockSpec((fb, d), lambda i, s, n=n: (2 * (each * i + n) + s[CORE], 0)))
    return call(
        functools.partial(own_units_kernel, fb), "own_units", (info,), (ff // (2 * fb * each),), [up, down] * each, specs,
        (sds((d, ff // 2), BF), sds((ff // 2, d), BF)),
        (pl.BlockSpec((d, each * fb), lambda i, s: (0, i)), pl.BlockSpec((each * fb, d), lambda i, s: (i, 0))),
        flops=d * ff, room=ROOM,
    )


def choose(flag, a, b):
    return jnp.where(flag == 1, a, b)


def project_kernel(flag, info_ref, a_ref, b_ref, gain_ref, cond_ref, w_ref, *rest):
    full_ref, act_ref, qkv_ref = rest[-3:]
    x = choose(info_ref[flag], a_ref[...].astype(F32), b_ref[...].astype(F32))
    full_ref[...] = x.astype(BF)
    normal, _ = norm_rows(x)
    act = (normal * (gain_ref[...] * (1.0 + cond_ref[0:1, :])) + cond_ref[1:2, :]).astype(BF)
    act_ref[...] = act
    qkv_ref[...] = nn(act, w_ref[...]).astype(BF)


def project(info, flag, a, b, first, total, gain, cond, weight, before=None):
    rows, width = a.shape
    block = min(256, rows)
    skip = first // block
    row = pl.BlockSpec((block, width), lambda i, s: (i, 0))
    ins = [a, b, gain, cond, weight]
    specs = [
        row, row,
        pl.BlockSpec((1, width), lambda i, s: (0, 0)),
        pl.BlockSpec(cond.shape, lambda i, s: (0, 0)),
        pl.BlockSpec(weight.shape, lambda i, s: (0, 0)),
    ]
    aliases = {}
    if before is not None:
        ins += list(before)
        specs += [pl.BlockSpec(memory_space=pl.ANY)] * 3
        aliases = {6: 0, 7: 1, 8: 2}
    out = pl.BlockSpec((block, width), lambda i, s: (i + skip, 0))
    return call(
        functools.partial(project_kernel, flag), "project", (info,), (rows // block,), ins, specs,
        (sds((total, width), BF), sds((total, width), BF), sds((total, weight.shape[1]), BF)),
        (out, out, pl.BlockSpec((block, weight.shape[1]), lambda i, s: (i + skip, 0))),
        flops=2 * rows * width * weight.shape[1], aliases=aliases,
    )


def assemble_kernel(local, total, info_ref, n1_ref, n2_ref, f1_ref, f2_ref, cot_ref, g_ref, sum_ref):
    near = choose(info_ref[NEAR], n1_ref[...].astype(F32), n2_ref[...].astype(F32))
    far = choose(info_ref[FAR], f1_ref[...].astype(F32), f2_ref[...].astype(F32))
    sums = jnp.zeros((1, near.shape[1]), F32)
    for first, piece in ((0, near), (near.shape[0], far)):
        rows = slice(first, first + piece.shape[0])
        live = live_column(piece.shape[0], first, info_ref, local, total)
        masked = jnp.where(live, piece, 0.0)
        cot_ref[rows, :] = piece.astype(BF)
        g_ref[rows, :] = masked.astype(BF)
        sums += jnp.sum(masked, axis=0, keepdims=True)
    sum_ref[...] = jnp.broadcast_to(sums, sum_ref.shape)


def assemble(info, near, far, local):
    total, width = near[0].shape[0] + far[0].shape[0], near[0].shape[1]
    whole = lambda a: pl.BlockSpec(a.shape, lambda i, s: (0, 0))
    ins = [*near, *far]
    outs = (sds((total, width), BF), sds((total, width), BF), sds((8, width), F32))
    return call(
        functools.partial(assemble_kernel, local, total), "assemble", (info,), (1,),
        ins, [whole(a) for a in ins], outs, tuple(whole(a) for a in outs), flops=total * width,
    )


def augment(main, rows, values):
    lane = lax.broadcasted_iota(jnp.int32, (1, 2 * HD), 1)
    extra = jnp.zeros((rows, 2 * HD), F32)
    for n, value in enumerate(values):
        extra = jnp.where(lane == n, value, extra)
    return jnp.concatenate([main.astype(BF), extra.astype(BF)], axis=1)


def stack_heads(pair):
    first = lax.broadcasted_iota(jnp.int32, (1, 2 * HD), 1) < HD
    zero = jnp.zeros_like(pair)
    return jnp.concatenate([jnp.where(first, pair, zero), jnp.where(first, zero, pair)], axis=0)


def merge_heads(stacked):
    rows = stacked.shape[0] // 2
    first = lax.broadcasted_iota(jnp.int32, (1, 2 * HD), 1) < HD
    return jnp.where(first, stacked[:rows], stacked[rows:])


TILE = 256


def attend_forward_kernel(local, info_ref, q_ref, k_ref, v_ref, o_ref, l_ref, ka, va):
    total = k_ref.shape[0]
    pair = pl.program_id(0)
    live = live_column(total, 0, info_ref, local, total)
    ka[...] = augment(k_ref[...], total, (jnp.where(live, 0.0, MASKED),))
    va[...] = augment(v_ref[...], total, (1.0,))

    def scores_of(start):
        return nt(augment(stack_heads(q_ref[start : start + TILE, :]), 2 * TILE, (1.0,)), ka[...])

    def mix(start, top, weights):
        rows = slice(start, start + TILE)
        mixed = nn(weights, va[...])
        sums = mixed[:, 2 * HD : 2 * HD + 1]
        o_ref[rows, :] = merge_heads(mixed[:, : 2 * HD] / sums).astype(BF)
        logs = top + jnp.log(sums) * HD**0.5
        column = lax.broadcasted_iota(jnp.int32, (1, 2 * HD), 1) - 2 * pair
        held = jnp.where(pair == 0, 0.0, l_ref[rows, :])
        l_ref[rows, :] = jnp.where(column == 0, logs[:TILE], jnp.where(column == 1, logs[TILE:], held))

    scores, waiting = scores_of(0), None
    for start in range(0, total, TILE):
        ahead = scores_of(start + TILE) if start + TILE < total else None
        top = jnp.max(scores, axis=-1, keepdims=True)
        weights = jnp.exp2((scores - top) * EXP2_SCALE).astype(BF)
        if waiting is not None:
            mix(*waiting)
        scores, waiting = ahead, (start, top, weights)
    mix(*waiting)


def attend_forward(info, qkv, local, first, count):
    total = qkv.shape[0]
    pairs = qkv.shape[1] // (6 * HD)
    out = pl.BlockSpec((total, 2 * HD), lambda j, s: (0, j))
    return call(
        functools.partial(attend_forward_kernel, local), "attend_forward", (info,), (count,),
        [qkv, qkv, qkv],
        [pl.BlockSpec((total, 2 * HD), lambda j, s, m=m: (0, m * pairs + first + j)) for m in range(3)],
        (sds((total, count * 2 * HD), BF), sds((total, 2 * HD), F32)),
        (out, pl.BlockSpec((total, 2 * HD), lambda j, s: (0, 0))),
        scratch=[pltpu.VMEM((total, 4 * HD), BF), pltpu.VMEM((total, 4 * HD), BF)],
        flops=32 * total * total * count * HD,
    )


def attend_backward_kernel(
    local, info_ref, q_ref, g_ref, o_ref, l_ref, k_ref, v_ref, gq_ref, gk_ref, gv_ref, ka, va, acck, accv
):
    total = k_ref.shape[0]

    @pl.when(pl.program_id(1) == 0)
    def _():
        live = live_column(total, 0, info_ref, local, total)
        ka[...] = augment(k_ref[...], total, (jnp.where(live, 0.0, MASKED), 1.0, 1.0, 1.0))
        va[...] = augment(v_ref[...], total, (1.0, 1.0))
        acck[...] = jnp.zeros_like(acck)
        accv[...] = jnp.zeros_like(accv)

    for start in range(0, q_ref.shape[0], TILE):
        rows = slice(start, start + TILE)
        q = stack_heads(q_ref[rows, :])
        g = stack_heads(g_ref[rows, :])
        o = o_ref[rows, :].astype(F32)
        inner = jnp.sum(g.astype(F32) * jnp.concatenate([o, o], axis=0), axis=-1, keepdims=True)
        column = lax.broadcasted_iota(jnp.int32, (1, 2 * HD), 1) - 2 * pl.program_id(0)
        logs = [jnp.sum(jnp.where(column == k, l_ref[rows, :], 0.0), axis=-1, keepdims=True) for k in range(2)]
        logs = jnp.concatenate(logs, axis=0)
        high = logs.astype(BF).astype(F32)
        middle = (logs - high).astype(BF).astype(F32)
        inner_high = inner.astype(BF).astype(F32)
        qa = augment(q, 2 * TILE, (1.0, -high, -middle, high + middle - logs))
        ga = augment(g, 2 * TILE, (-inner_high, inner_high - inner))
        probability = jnp.exp2(nt(ka[...], qa) * EXP2_SCALE)
        g_scores = (probability * nt(va[...], ga)).astype(BF)
        acck[...] += nn(g_scores, q)
        accv[...] += nn(probability.astype(BF), g)
        gq_ref[rows, :] = merge_heads(tn_dot(g_scores, k_ref[...]) * HD**-0.5).astype(BF)

    @pl.when(pl.program_id(1) == pl.num_programs(1) - 1)
    def _():
        gk_ref[...] = (acck[...] * HD**-0.5).astype(BF)
        gv_ref[...] = accv[...].astype(BF)


def attend_backward(info, qkv, g, o, logs, local, first, count):
    total = qkv.shape[0]
    pairs = qkv.shape[1] // (6 * HD)
    block = total
    part = pl.BlockSpec((block, 2 * HD), lambda j, i, s: (i, first + j))
    own = pl.BlockSpec((block, 2 * HD), lambda j, i, s: (i, j))
    return call(
        functools.partial(attend_backward_kernel, local), "attend_backward", (info,), (count, total // block),
        [qkv, g, o, logs, qkv, qkv],
        [
            part, part, own, pl.BlockSpec((total, 2 * HD), lambda j, i, s: (i, 0)),
            pl.BlockSpec((total, 2 * HD), lambda j, i, s: (0, pairs + first + j)),
            pl.BlockSpec((total, 2 * HD), lambda j, i, s: (0, 2 * pairs + first + j)),
        ],
        (sds((total, count * 2 * HD), BF),) * 3,
        (
            own,
            pl.BlockSpec((total, 2 * HD), lambda j, i, s: (0, j)),
            pl.BlockSpec((total, 2 * HD), lambda j, i, s: (0, j)),
        ),
        scratch=[
            pltpu.VMEM((total, 4 * HD), BF),
            pltpu.VMEM((total, 4 * HD), BF),
            pltpu.VMEM((total, 2 * HD), F32),
            pltpu.VMEM((total, 2 * HD), F32),
        ],
        flops=80 * total * total * count * HD,
    )


def mix_out_kernel(local, total, info_ref, *refs):
    mine, other = refs[:2], refs[2:4]
    w_ref, bias_ref, x_ref, gain_ref, cond_ref, mix_ref, res_ref, act_ref = refs[4:]
    rows = x_ref.shape[0]
    live = live_column(rows, pl.program_id(0) * rows, info_ref, local, total).astype(F32)
    mine, other = [jnp.concatenate([r[...] for r in side], axis=1) for side in (mine, other)]
    first = info_ref[CORE] == 0
    mixture = jnp.concatenate([jnp.where(first, mine, other), jnp.where(first, other, mine)], axis=1)
    mix_ref[...] = mixture
    residual = x_ref[...].astype(F32) + live * (nn(mixture, w_ref[...]) + bias_ref[...])
    res_ref[...] = residual.astype(BF)
    normal, _ = norm_rows(residual)
    act_ref[...] = (normal * (gain_ref[...] * (1.0 + cond_ref[2:3, :])) + cond_ref[3:4, :]).astype(BF)


def mix_out(info, mine, other, weight, bias, x, gain, cond, local):
    total, width = x.shape
    block = 256
    row = lambda w: pl.BlockSpec((block, w), lambda i, s: (i, 0))
    vec = pl.BlockSpec((1, width), lambda i, s: (0, 0))
    parts = [*mine, *other]
    return call(
        functools.partial(mix_out_kernel, local, total), "mix_out", (info,), (total // block,),
        [*parts, weight, bias, x, gain, cond],
        [row(a.shape[1]) for a in parts]
        + [
            pl.BlockSpec(weight.shape, lambda i, s: (0, 0)),
            vec, row(width), vec, pl.BlockSpec(cond.shape, lambda i, s: (0, 0)),
        ],
        (sds((total, width), BF),) * 3, (row(width),) * 3,
        flops=2 * total * width * width,
    )


def raise_kernel(info_ref, act_ref, w_ref, bias_ref, hid_ref, der_ref):
    raised = nn(act_ref[...], w_ref[...]) + bias_ref[...]
    scaled = raised * 0.5**0.5
    half = 0.5 * lax.erf(scaled) + 0.5
    hid_ref[...] = (raised * half).astype(BF)
    slope = half + (raised * (2.0 * math.pi) ** -0.5) * jnp.exp2(scaled * scaled * -math.log2(math.e))
    der_ref[...] = slope.astype(BF)


def raise_up(info, act, weight, bias, block):
    total, width = act.shape
    units = weight.shape[1]
    col = pl.BlockSpec((total, block), lambda j, s: (0, j))
    return call(
        raise_kernel, "raise_up", (info,), (units // block,),
        [act, weight, bias],
        [
            pl.BlockSpec((total, width), lambda j, s: (0, 0)),
            pl.BlockSpec((width, block), lambda j, s: (0, j)),
            pl.BlockSpec((1, block), lambda j, s: (0, j)),
        ],
        (sds((total, units), BF),) * 2, (col, col),
        flops=2 * total * width * units,
    )


def weight_gradient_kernel(which, n, info_ref, *refs):
    lhs, refs = refs[: max(which) + 1], refs[max(which) + 1 :]
    rhs, outs = refs[: len(which)], refs[len(which) :]
    for group, out in enumerate(outs):

        @pl.when(pl.program_id(0) // n == group)
        def _():
            first = 0
            for k, ref in zip(which, rhs, strict=True):
                w = ref.shape[1]
                out[:, first : first + w] = tn_dot(lhs[k][...], ref[...]).astype(BF)
                first += w


def weight_gradient(info, parts, n, mb, row, col, groups, name):
    total, height = parts[0][0].shape
    width = sum(part[3] for part in parts)
    if mb % 128 or any(part[3] % 128 for part in parts):
        results = []
        for g in range(groups):
            sliced = [
                (l, lax.dynamic_slice_in_dim(r, (f(info) + col(g, info)) * w, w, 1), lambda s: 0, w)
                for l, r, f, w in parts
            ]
            every = height // 128
            (whole,) = weight_gradient(info, sliced, every, 128, lambda k, g, s: k, lambda g, s: 0, 1, name)
            rows = jnp.stack([jnp.asarray(row(k, g, info), jnp.int32) for k in range(n)])
            results.append(whole.reshape(height // mb, mb, width)[rows].reshape(n * mb, width))
        return results
    lhs = []
    for part in parts:
        if not any(part[0] is a for a in lhs):
            lhs.append(part[0])
    which = [next(k for k, a in enumerate(lhs) if a is part[0]) for part in parts]
    return call(
        functools.partial(weight_gradient_kernel, which, n), name, (info,), (n * groups,),
        [*lhs, *[part[1] for part in parts]],
        [pl.BlockSpec((total, mb), lambda i, s: (0, row(i % n, i // n, s)))] * len(lhs)
        + [
            pl.BlockSpec((total, part[3]), lambda i, s, f=part[2]: (0, f(s) + col(i // n, s))) for part in parts
        ],
        (sds((n * mb, width), BF),) * groups,
        tuple(
            pl.BlockSpec((mb, width), lambda i, s, g=g: (jnp.clip(i - g * n, 0, n - 1), 0)) for g in range(groups)
        ),
        flops=2 * total * n * mb * width * groups,
    )


def add_split_kernel(info_ref, a1_ref, b1_ref, a2_ref, b2_ref, send_ref, keep_ref):
    send_ref[...] = (a1_ref[...].astype(F32) + b1_ref[...].astype(F32)).astype(BF)
    keep_ref[...] = (a2_ref[...].astype(F32) + b2_ref[...].astype(F32)).astype(BF)


def add_split(info, a, b, bit):
    rows, width = a.shape[0] // 2, a.shape[1]
    give = pl.BlockSpec((rows, width), lambda i, s: (1 - bit(s), 0))
    keep = pl.BlockSpec((rows, width), lambda i, s: (bit(s), 0))
    out = pl.BlockSpec((rows, width), lambda i, s: (0, 0))
    return call(
        add_split_kernel, "add_split", (info,), (1,), [a, b, a, b], [give, give, keep, keep],
        (sds((rows, width), BF),) * 2, (out, out), flops=rows * width,
    )


def raise_back_kernel(info_ref, g_ref, w_ref, der_ref, out_ref, sum_ref):
    back = (nt(g_ref[...], w_ref[...]) * der_ref[...].astype(F32)).astype(BF)
    out_ref[...] = back
    sum_ref[...] = jnp.sum(back.astype(F32), axis=0, keepdims=True)


def raise_back(info, g, weight, der, block):
    total, width = g.shape
    units = weight.shape[0]
    col = pl.BlockSpec((total, block), lambda j, s: (0, j))
    return call(
        raise_back_kernel, "raise_back", (info,), (units // block,),
        [g, weight, der],
        [pl.BlockSpec((total, width), lambda j, s: (0, 0)), pl.BlockSpec((block, width), lambda j, s: (j, 0)), col],
        (sds((total, units), BF), sds((1, units), F32)),
        (col, pl.BlockSpec((1, block), lambda j, s: (0, j))),
        flops=2 * total * width * units,
    )


def rows_product_kernel(transposed, index_ref, lhs_ref, w_ref, out_ref):
    out_ref[...] = (nt if transposed else nn)(lhs_ref[...], w_ref[...]).astype(BF)


def rows_product(info, lhs, weight, n, block, row, transposed, name):
    depth = lhs.shape[1]
    width = weight.shape[0] if transposed else weight.shape[1]
    return call(
        functools.partial(rows_product_kernel, transposed), name, (info,), (n,),
        [lhs, weight],
        [pl.BlockSpec((block, depth), lambda i, s: (row(i, s), 0)), pl.BlockSpec(weight.shape, lambda i, s: (0, 0))],
        sds((n * block, width), BF),
        pl.BlockSpec((block, width), lambda i, s: (i, 0)),
        flops=2 * n * block * depth * width,
    )


def lower_kernel(local, total, info_ref, a_ref, b_ref, res_ref, bias_ref, out_ref):
    rows = out_ref.shape[0]
    first = (info_ref[HALF] * pl.num_programs(0) + pl.program_id(0)) * rows
    live = live_column(rows, first, info_ref, local, total)
    branch = a_ref[...].astype(F32) + b_ref[...].astype(F32) + bias_ref[...]
    out_ref[...] = (res_ref[...].astype(F32) + jnp.where(live, branch, 0.0)).astype(BF)


def add_branch(info, a, b, residual, bias, local):
    total, width = residual.shape
    block = 256
    n = total // 2 // block
    row = pl.BlockSpec((block, width), lambda i, s: (i, 0))
    return call(
        functools.partial(lower_kernel, local, total), "add_branch", (info,), (n,),
        [a, b, residual, bias],
        [row, row, pl.BlockSpec((block, width), lambda i, s: (s[HALF] * n + i, 0)), pl.BlockSpec((1, width), lambda i, s: (0, 0))],
        sds((total // 2, width), BF), row, flops=total * width,
    )


def norm_back(g, v, gain, scale):
    normal, inverse = norm_rows(v)
    e = g * (gain * (1.0 + scale))
    grad = inverse * (
        e - jnp.mean(e, axis=-1, keepdims=True) - normal * jnp.mean(e * normal, axis=-1, keepdims=True)
    )
    return grad, jnp.sum(g * normal, axis=0, keepdims=True), jnp.sum(g, axis=0, keepdims=True)


def accumulate(sum_ref, parts):
    block = jnp.concatenate(parts, axis=0)

    @pl.when(pl.program_id(0) == 0)
    def _():
        sum_ref[...] = block

    @pl.when(pl.program_id(0) > 0)
    def _():
        sum_ref[...] += block


def dense_norm_back_kernel(local, total, info_ref, a1_ref, a2_ref, b1_ref, b2_ref, res_ref, cot_ref, gain_ref, cond_ref, w_ref, gres_ref, gatt_ref, gmix_ref, sum_ref):
    rows = res_ref.shape[0]
    live = live_column(rows, pl.program_id(0) * rows, info_ref, local, total).astype(F32)
    early = pl.program_id(0) < pl.num_programs(0) // 2
    g = jnp.where(early, a1_ref[...].astype(F32) + b1_ref[...].astype(F32), a2_ref[...].astype(F32) + b2_ref[...].astype(F32))
    grad, by_normal, plain = norm_back(g, res_ref[...].astype(F32), gain_ref[...], cond_ref[2:3, :])
    g_residual = cot_ref[...].astype(F32) + grad
    gres_ref[...] = g_residual.astype(BF)
    g_attend = (live * g_residual).astype(BF)
    gatt_ref[...] = g_attend
    gmix_ref[...] = nt(g_attend, w_ref[...]).astype(BF)
    bias = jnp.sum(g_attend.astype(F32), axis=0, keepdims=True)
    accumulate(sum_ref, [by_normal, plain, bias, jnp.zeros((5, bias.shape[1]), F32)])


def dense_norm_back(info, a, b, residual, cot, gain, cond, weight, local):
    total, width = residual.shape
    half = weight.shape[0] // 2
    block = 256
    row = lambda w: pl.BlockSpec((block, w), lambda i, s: (i, 0))
    n = total // block // 2
    first = pl.BlockSpec((block, width), lambda i, s: (jnp.minimum(i, n - 1), 0))
    second = pl.BlockSpec((block, width), lambda i, s: (jnp.maximum(i - n, 0), 0))
    return call(
        functools.partial(dense_norm_back_kernel, local, total), "dense_norm_back", (info,), (total // block,),
        [*a, *b, residual, cot, gain, cond, weight],
        [
            first, second, first, second, row(width), row(width),
            pl.BlockSpec((1, width), lambda i, s: (0, 0)),
            pl.BlockSpec(cond.shape, lambda i, s: (0, 0)),
            pl.BlockSpec((half, width), lambda i, s: (s[CORE], 0)),
        ],
        (sds((total, width), BF), sds((total, width), BF), sds((total, half), BF), sds((8, width), F32)),
        (row(width), row(width), row(half), pl.BlockSpec((8, width), lambda i, s: (0, 0))),
        flops=2 * total * width * half,
    )


def project_back_kernel(count, index_ref, *refs):
    lhs, w_ref, out_ref = refs[:-2], refs[-2], refs[-1]
    first, total = 0, None
    for n in range(3):
        for m in range(count):
            ref = lhs[n * count + m]
            w = ref.shape[1]
            term = nt(ref[...], w_ref[:, first : first + w])
            total = term if total is None else total + term
            first += w
    out_ref[...] = total.astype(BF)


def project_back(info, parts, weight, n, block, row):
    width = weight.shape[0]
    lhs = [part[m] for m in range(3) for part in parts]
    return call(
        functools.partial(project_back_kernel, len(parts)), "project_back", (info,), (n,),
        lhs + [weight],
        [pl.BlockSpec((block, a.shape[1]), lambda i, s: (row(i, s), 0)) for a in lhs]
        + [pl.BlockSpec(weight.shape, lambda i, s: (0, 0))],
        sds((n * block, width), BF),
        pl.BlockSpec((block, width), lambda i, s: (i, 0)),
        flops=2 * n * block * weight.shape[1] * width,
    )


def attend_norm_back_kernel(info_ref, a_ref, b1_ref, b2_ref, x_ref, gres_ref, gain_ref, cond_ref, out_ref, sum_ref):
    early = pl.program_id(0) < pl.num_programs(0) // 2
    g = a_ref[...].astype(F32) + jnp.where(early, b1_ref[...].astype(F32), b2_ref[...].astype(F32))
    grad, by_normal, plain = norm_back(g, x_ref[...].astype(F32), gain_ref[...], cond_ref[0:1, :])
    out_ref[...] = (gres_ref[...].astype(F32) + grad).astype(BF)
    accumulate(sum_ref, [by_normal, plain, jnp.zeros((6, plain.shape[1]), F32)])


def attend_norm_back(info, a, b, x, g_residual, gain, cond):
    width = x.shape[1]
    block = 256
    n = a.shape[0] // block
    plain = pl.BlockSpec((block, width), lambda i, s: (i, 0))
    first = pl.BlockSpec((block, width), lambda i, s: (jnp.minimum(i, n // 2 - 1), 0))
    second = pl.BlockSpec((block, width), lambda i, s: (jnp.maximum(i - n // 2, 0), 0))
    picked = pl.BlockSpec((block, width), lambda i, s: (s[HALF] * n + i, 0))
    return call(
        attend_norm_back_kernel, "attend_norm_back", (info,), (n,),
        [a, *b, x, g_residual, gain, cond],
        [
            plain, first, second, picked, picked,
            pl.BlockSpec((1, width), lambda i, s: (0, 0)),
            pl.BlockSpec(cond.shape, lambda i, s: (0, 0)),
        ],
        (sds((n * block, width), BF), sds((8, width), F32)),
        (plain, pl.BlockSpec((8, width), lambda i, s: (0, 0))),
        flops=n * block * width,
    )


def finish_kernel(places, counts, info_ref, *refs):
    outs = refs[sum(counts) :]
    groups, at = [], 0
    for count in counts:
        groups.append(refs[at : at + count])
        at += count
    first = info_ref[CORE] == 0
    for out, group, source, width, target, stride in places:
        refs_ = groups[group]
        columns = slice(source, source + width)
        mine, other = [sum(r[side, :, columns].astype(F32) for r in refs_) for side in range(2)]
        outs[out][:, target : target + width] = jnp.where(first, mine, other)
        outs[out][:, target + stride : target + stride + width] = jnp.where(first, other, mine)


def finish(info, groups, places, widths):
    r = groups[0][0].shape[1]
    ins = [a for group in groups for a in group]
    outs = tuple(sds((r, w), F32) for w in widths)
    return call(
        functools.partial(finish_kernel, places, [len(g) for g in groups]), "finish", (info,), (1,),
        ins, [pl.BlockSpec(a.shape, lambda i, s: (0, 0, 0)) for a in ins],
        outs, tuple(pl.BlockSpec(a.shape, lambda i, s: (0, 0)) for a in outs), flops=r * sum(widths),
    )


def sinus_angles(time, features, width):
    halfway = width // 2
    rates = jnp.exp(-math.log(10000.0) * (features % halfway).astype(F32) / halfway)
    angles = time[:, None] * rates[None, :]
    return jnp.where((features < halfway)[None, :], jnp.sin(angles), jnp.cos(angles))


def body(
    dp, seq,
    tokens, time_index, lengths, time_weight, time_bias, attend_gain, query_key_value_weight,
    attention_output_weight, attend_bias, dense_gain, feedforward_up_matrix, up_bias,
    feedforward_down_matrix, down_bias, cotangent,
):
    nl, tl, d = tokens.shape
    ff = feedforward_up_matrix.shape[1]
    total = tl * seq
    chips = dp // 2
    nz = dp // 4
    i = lax.axis_index("dp")
    y = lax.axis_index("seq")
    core = i % 2
    x = (i // 2) % 2
    z = i // 4
    h = tl // 2
    half = d // 2
    fb, nb = ff // dp, dp // 2

    entry = lax.broadcasted_iota(jnp.int32, (16,), 0)
    places = {CORE: core, OFFSET: y * tl, NEAR: core == y // nl, FAR: core == 0, X: x, Z: z, HALF: core != y // nl, Y: y}
    info = jnp.zeros((16,), jnp.int32)
    for n, v in places.items():
        info = jnp.where(entry == n, jnp.asarray(v, jnp.int32), info)
    order = Order(info)
    run = order.run


    core_swap = lambda a: lax.ppermute(a, "dp", [(n, n ^ 1) for n in range(dp)])
    x_swap = lambda a: lax.ppermute(a, "dp", [(n, n ^ 2) for n in range(dp)])

    def y_shift(a, k):
        return lax.ppermute(a, "seq", [(n, (n + k) % seq) for n in range(seq)])

    def travel(k):
        pairs = []
        for chip in range(chips):
            for s in range(seq):
                target = (s + k) % seq
                pairs.append(((chip * 2 + target // nl) * seq + s, chip * 2 * seq + target))
        return pairs


    def take(a, axis, n):
        return lax.dynamic_index_in_dim(a, n, axis, keepdims=False)

    def pick(a, index):
        return lax.dynamic_index_in_dim(a, index, 0, keepdims=False)

    def in_core_order(mine, other):
        return jnp.where(core == 0, mine, other), jnp.where(core == 0, other, mine)

    def fetch_near(a):
        mine = pick(a, y % nl)
        return mine, core_swap(mine)

    def fetch_far(a):
        got = [lax.ppermute(pick(a, (y + k) % seq % nl), ("dp", "seq"), travel(k)) for k in range(1, seq)]
        return got[0] if len(got) == 1 else jnp.concatenate(got, axis=0)

    def give_back(a):
        got = [a[0]]
        for k in range(1, seq):
            pairs = []
            for chip in range(chips):
                for s in range(seq):
                    owner = s // nl
                    source = owner if k < seq // 2 else 1 - owner
                    pairs.append(((chip * 2 + source) * seq + s, (chip * 2 + owner) * seq + (s - k) % seq))
            got.append(lax.ppermute(a[k % (seq // 2)], ("dp", "seq"), pairs))
        if nl == 1 and seq == 2:
            return lambda: jnp.where(core == y, *got)[None]
        return lambda: jnp.stack([pick(jnp.stack(got), (core * nl + j - y) % seq) for j in range(nl)])

    steps = nz.bit_length() - 1

    def z_swap(a, j):
        return lax.ppermute(a, "dp", [(n, n ^ (4 << j)) for n in range(dp)])

    z_way = lambda j: (lambda s: (s[Z] >> j) & 1, 2 << j, functools.partial(z_swap, j=j))
    x_way = (lambda s: s[X], 1, x_swap)

    class Chain:
        def __init__(self, parts, mb, name, ways, along=False):
            free = ways if along else ways[1:]
            n = 2 ** len(free)

            def row(k, group, s):
                place = 0
                for t, (_, weight, _) in enumerate(free):
                    place = place + ((k >> (len(free) - 1 - t)) & 1) * weight
                if not along:
                    bit = ways[0][0](s)
                    place = place + (bit + (1 - group) * (1 - 2 * bit)) * ways[0][1]
                return place

            if along:
                parts = [(l, r, lambda s, f=f: f(s) * seq, w // seq) for l, r, f, w in parts]
                col = lambda group, s: lax.rem(s[Y] + group + 1, seq)
                out = run(weight_gradient, parts, n, mb, row, col, seq, name)
                self.came = [y_shift(a, k + 1) for k, a in enumerate(out[:-1])]
            else:
                out = run(weight_gradient, parts, n, mb, row, lambda group, s: 0, 2, name)
                self.came = [ways[0][2](out[0])]
            self.kept = out[-1]
            self.ways = list(free)

        def other(self):
            if len(self.came) == 1:
                return self.came[0]
            return sum(a.astype(F32) for a in self.came).astype(BF)

        def hop(self):
            bit, _, swap = self.ways.pop(0)
            send, self.kept = run(add_split, self.kept, self.other(), bit)
            self.came = [swap(send)]

        def last(self):
            return run(add_split, self.kept, self.other(), lambda s: s[CORE])


    far = fetch_far(tokens)
    mine = jnp.stack([pick(time_index, y % nl), pick(lengths, y % nl)])
    time, length = jnp.where(core == y // nl, mine, core_swap(mine))
    near = fetch_near(tokens)
    weight_qkv = run(own_projection, query_key_value_weight)
    own_up_bias = take(up_bias.reshape(nb, 2, fb), 1, core).reshape(1, nb * fb)
    order.info = jnp.where(entry == LENGTH, length, order.info)
    time = time.astype(F32)[None]
    table = sinus_angles(order.after(time), jnp.arange(d), d).astype(BF)
    cond = order.after((jnp.dot(table, time_weight, preferred_element_type=F32) + time_bias).reshape(4, d))
    gain1, gain2 = attend_gain[None, :], dense_gain[None, :]

    before = run(project, NEAR, *near, 0, total, gain1, cond, weight_qkv)
    cotangent = order.after(cotangent)
    near_cot = fetch_near(cotangent)
    far_cot = fetch_far(cotangent)
    weight_up, weight_down = run(own_units, feedforward_up_matrix, feedforward_down_matrix, fb)
    far = order.after(far)
    full, act1, qkv = run(project, FAR, far, core_swap(far), tl, total, gain1, cond, weight_qkv, before)
    pairs = half // (2 * HD)
    share = pairs // 2
    attended, swapped = [], []
    for n in range(2):
        attended.append(run(attend_forward, qkv, tl, n * share, share))
        swapped.append(core_swap(attended[n][0]))
        far_cot = order.after(far_cot) if n == 0 else far_cot
    cot, g_dense, g_down_bias = run(assemble, near_cot, (far_cot, core_swap(far_cot)), tl)
    mixture, residual, act2 = run(
        mix_out, [a[0] for a in attended], swapped, attention_output_weight, attend_bias[None, :],
        full, gain2, cond, tl,
    )
    hidden, slope = run(raise_up, act2, weight_up, own_up_bias, 2 * fb)

    rows_of = d // chips
    zero = lambda s: 0
    zs = [z_way(j) for j in range(steps)]
    down = Chain([(hidden, g_dense, zero, d)], fb, "down_gradient", [*zs, x_way], along=True)
    g_raised, g_up_bias = run(raise_back, g_dense, weight_down, slope, 2 * fb)
    up = Chain([(act2, g_raised, zero, fb * nb)], rows_of, "up_gradient", [x_way, *zs])
    quarters = max(2, total // 256)
    g_act2, g_act2_other = [], []
    for n in range(2):
        place = lambda i, s, n=n: n * (quarters // 2) + i
        g_act2.append(run(rows_product, g_raised, weight_up, quarters // 2, total // quarters, place, True, "raise_input_back"))
        g_act2_other.append(core_swap(g_act2[n]))

    n = max(1, total // 2 // 256)
    own_half = (n, total // 2 // n, lambda i, s: s[HALF] * n + i)
    their_half = (n, total // 2 // n, lambda i, s: (1 - s[HALF]) * n + i)
    branch_theirs = core_swap(run(rows_product, hidden, weight_down, *their_half, False, "lower"))
    branch = run(rows_product, hidden, weight_down, *own_half, False, "lower")
    g_residual, g_attend, g_mixture, sums2 = run(
        dense_norm_back, g_act2, g_act2_other, residual, cot, gain2, cond, attention_output_weight, tl
    )

    def input_gradients(n):
        back = run(attend_backward, qkv, g_mixture, *attended[n], tl, n * share, share)
        return back, [(act1, a, zero, a.shape[1]) for a in back]

    back1, in1 = input_gradients(0)
    in1 = Chain(in1 + [(mixture, g_attend, lambda s: s[CORE], half)], rows_of, "in_gradient", [zs[0], x_way, *zs[1:]])
    down.hop()
    back2, in2 = input_gradients(1)
    parts = [back1, back2]
    g_act1_theirs = []
    few = max(1, n // 2)
    for m in range(2):
        place = lambda i, s, m=m: ((1 - s[HALF]) * 2 + m) * few + i
        g_act1_theirs.append(core_swap(run(project_back, parts, weight_qkv, few, total // 4 // few, place)))
    in2 = Chain(in2, rows_of, "in_gradient", [x_way, *zs])
    up.hop()
    g_act1 = run(project_back, parts, weight_qkv, *own_half)
    result = give_back(run(add_branch, branch, branch_theirs, residual, down_bias[None, :], tl).reshape(-1, tl, d))
    down.hop()
    g_tokens, sums1 = run(attend_norm_back, g_act1, g_act1_theirs, full, g_residual, gain1, cond)
    gradient_tokens = give_back(g_tokens.reshape(-1, tl, d))
    in1.hop()

    once = jnp.where(core == 0, 1.0, 0.0)
    scales = 1.0 + cond
    up_sum = g_up_bias.reshape(nb, 1, fb)
    up_sum = jnp.concatenate(in_core_order(up_sum, jnp.zeros_like(up_sum)), axis=1).reshape(ff // d, d)
    level = jnp.where(lax.broadcasted_iota(jnp.int32, (1, d), 1) == 0, time // 256.0, time % 256.0)
    pack = jnp.concatenate(
        [
            sums1[0:1] * gain1,
            sums1[1:2],
            once * sums2[0:1] * gain2,
            once * sums2[1:2],
            once * level,
            sums1[0:1] * scales[0:1],
            once * sums2[0:1] * scales[2:3],
            once * sums2[2:3],
            once * g_down_bias[0:1],
            up_sum,
        ]
    )
    pack = order.after(pack + core_swap(pack))
    rows_each, sums = pack[:5].astype(BF), pack[5:]

    def pack_hop(rows_each, sums, swaps):
        sums = sums.astype(BF)
        packs = [swap(jnp.concatenate([rows_each, sums])) for swap in swaps]
        count = rows_each.shape[0]

        def arrive():
            rows = jnp.concatenate([rows_each] + [p[:count] for p in packs])
            return order.after((rows, sum([p[count:].astype(F32) for p in packs], sums.astype(F32))))

        return arrive

    packed = pack_hop(rows_each, sums, [x_swap])
    up.hop()
    in2.hop()
    packed = pack_hop(*packed(), [functools.partial(y_shift, k=k) for k in range(1, seq)])
    result = order.after(result())
    for _ in range(steps - 1):
        down.hop()
    packed = pack_hop(*packed(), [functools.partial(z_swap, j=0)])
    for _ in range(steps - 1):
        in1.hop()
    for _ in range(steps - 2):
        up.hop()
    down_mine = order.after((down.kept.astype(F32) + down.other().astype(F32)).astype(BF))
    down_all = jnp.stack([down_mine] + [y_shift(down_mine, k) for k in range(1, seq)])
    for j in range(1, steps):
        packed = pack_hop(*packed(), [functools.partial(z_swap, j=j)])

    def shared(chain):
        theirs, mine = chain.last()
        both = jnp.stack([mine, core_swap(theirs)])
        return [both] + [y_shift(both, k) for k in range(1, seq)]

    up_all, in1_all = shared(up), shared(in1)
    rows_each, sums = packed()
    for _ in range(steps - 1):
        in2.hop()
    gradient_tokens = order.after(gradient_tokens())
    in2_all = shared(in2)
    gradient_down = jnp.concatenate([pick(down_all, (y - n) % seq) for n in range(seq)], axis=1).astype(F32)
    (gradient_up,) = run(finish, [up_all], [(0, 0, n * fb, fb, 2 * n * fb, fb) for n in range(nb)], [ff])
    w = share * 2 * HD
    spots = [(0, n, t * w, w, (2 * t * 2 + n) * w, 2 * w) for t in range(3) for n in range(2)]
    gradient_in, gradient_out = run(
        finish, [in1_all, in2_all], spots + [(1, 0, 3 * w, half, 0, half)], [3 * d, d]
    )
    gathered = rows_each.reshape(-1, 5, d).astype(F32)
    g_cond = gathered[:, 0:4].reshape(-1, 4 * d)
    own_features = i * (d // dp) + jnp.arange(d // dp)
    times = gathered[:, 4, 0] * 256.0 + gathered[:, 4, 1]
    features = sinus_angles(times, own_features, d).astype(BF)
    gradient_time = lax.dot_general(
        features.astype(F32), g_cond, (((0,), (0,)), ((), ())), precision=lax.Precision.HIGHEST
    )
    g_time_bias = jnp.sum(g_cond, axis=0)
    part = lambda v: lax.dynamic_index_in_dim(v.reshape(dp, -1), i, 0, keepdims=False)
    return (
        result,
        gradient_tokens,
        gradient_time,
        part(g_time_bias),
        part(sums[0]),
        gradient_in,
        gradient_out,
        part(sums[2]),
        part(sums[1]),
        gradient_up,
        part(sums[4:]),
        gradient_down,
        part(sums[3]),
    )


def solution(mesh):
    whole = P()
    rows = P("dp", "seq", None)
    return jax.shard_map(
        functools.partial(body, mesh.shape["dp"], mesh.shape["seq"]),
        mesh=mesh,
        in_specs=(rows, P("dp"), P("dp"), *(whole,) * 11, rows),
        out_specs=(
            rows, rows, P("dp", None), P("dp"), P("dp"), P("dp", None), P("dp", None),
            P("dp"), P("dp"), P("dp", None), P("dp"), P("dp", None), P("dp"),
        ),
        check_vma=False,
    )
```

time: 542 us -> 364 us (0.67)
  Pallas kernels: 242 us -> 180 us
  starting transfers between devices: 96.5 us -> 40.6 us
  other arithmetic: 52.7 us -> 10.1 us
  waiting for transfers between devices: 98.9 us -> 77.3 us
  local copies, waits for them, and re-layouts: 33.4 us -> 41.2 us
    pallas_call x28 -> x40, Pallas kernels: 242 us -> 180 us  [call(): pl.pallas_call(kernel, name=name, grid_spec=pltpu.PrefetchScalarGridSpec(...]
    ppermute x32 -> x14, starting transfers between devices: 56.9 us -> 17.3 us  [the longest x10 11.1 us: z_swap(): return lax.ppermute(a, 'dp', [(n, n ^ 4 << j) for n in range(dp)])]
    unnamed x69 -> x173, local copies, waits for them, and re-layouts: 5.81 us -> 34.9 us
    ppermute x32 -> x14, waiting for transfers between devices: 78 us -> 59.7 us  [the longest x10 59.7 us: z_swap(): return lax.ppermute(a, 'dp', [(n, n ^ 4 << j) for n in range(dp)])]
    slice x10 -> x8, local copies, waits for them, and re-layouts: 11.7 us -> 0.12 us  [the longest x1 0.05 us: body(): g_cond = gathered[:, 0:4].reshape(-1, 4 * d)]
    concatenate x13 -> x7, other arithmetic: 11.1 us -> 0.11 us  [the longest x4 0.07 us: arrive(): rows = jnp.concatenate([rows_each] + [p[:count] for p in packs])]
    ppermute x11 -> x6, starting transfers between devices: 18.6 us -> 8.39 us  [y_shift(): return lax.ppermute(a, 'seq', [(n, (n + k) % seq) for n in range(seq)])]
    reduce_sum x6 -> x1, other arithmetic: 9.6 us -> 0.05 us  [body(): g_time_bias = jnp.sum(g_cond, axis=0)]
  transfers between devices with their start and end apart: 66 -> 41, of which waited for: 21 -> 11; matrix products, arithmetic and copies ran while one was open for 16% -> 6% of each run, Pallas kernels for 39% -> 42%
where the time goes in v2:
time: 364 us; the launch traced here: 359 us
  Pallas kernels  180 us (49%)
  waiting for transfers between devices  77.3 us (21%)
  local copies, waits for them, and re-layouts  41.2 us (11%)
  starting transfers between devices  40.6 us (11%)
  other arithmetic  10.1 us (3%)
  matrix products  5.99 us (2%)
  between operations  4.14 us (1%)
    pallas_call x40, Pallas kernels, call(): pl.pallas_call(kernel, name=name, grid_spec=pltpu.PrefetchScalarGridSpec(...  180 us
    ppermute x10, waiting for transfers between devices, z_swap(): return lax.ppermute(a, 'dp', [(n, n ^ 4 << j) for n in range(dp)])  59.7 us
    unnamed x173, local copies, waits for them, and re-layouts  34.9 us
    ppermute x10, starting transfers between devices, z_swap(): return lax.ppermute(a, 'dp', [(n, n ^ 4 << j) for n in range(dp)])  11.1 us
    ppermute x6, waiting for transfers between devices, y_shift(): return lax.ppermute(a, 'seq', [(n, (n + k) % seq) for n in range(seq)])  10.5 us
    ppermute x16, starting transfers between devices, body(): core_swap = lambda a: lax.ppermute(a, 'dp', [(n, n ^ 1) for n in range(dp)])  10.2 us
    ppermute x6, starting transfers between devices, y_shift(): return lax.ppermute(a, 'seq', [(n, (n + k) % seq) for n in range(seq)])  8.39 us
  transfers between devices with their start and end apart: 41, of which 11 were waited for; matrix products, arithmetic and copies ran while one was open for 6% of the time, Pallas kernels for 42%

profile of v2, /device:TPU:0, one launch (start us, length us, event | category | flops | bytes accessed | tf_op | source)
XLA Modules:
  0.0 359.1 jit_solution(17149835269282492305)
XLA Ops:
  1.9 4.7 %collective-permute-start.1 = (bf16[512,1024]{1,0:T(8,128)(2,1)}, bf16[512,1024]{1,0:T(8,128)(2,1)S(1)}, u32[]{:S(2)}, u32[]{:S(2)}) collective-permute-start(bf16[512,1024]{1,0:T(8,128)(2,1)} %bitcast.46), channel_id=1, source_target_pairs={{0,2},{2,0},{4,6},{6,4},{8,10},{10,8},{12,14},{14,12},{16,18},{18,... | collective-permute-start | bytes 3145736 | tf_op jit(solution)/shard_map/ppermute | solution.py:687
  8.6 5.0 %own_projection.1.w_ref.refs_6_ = bf16[1024,1536]{1,0:T(8,128)(2,1)} custom-call(s32[16]{0:T(128)} %compare_select_fusion.10.info_ref, bf16[1024,3072]{1,0:T(8,128)(2,1)} %v_ref.1, bf16[1024,3072]{1,0:T(8,128)(2,1)} %v_ref.1, bf16[1024,3072]{1,0:T(8,128)(2,1)} %v_ref.1), custom_call_target="tpu_custom_call" | custom-call | flops 1 | bytes 1 | tf_op jit(solution)/shard_map/own_projection/pallas_call | solution.py:52
  15.7 4.6 %fusion.31 = f32[1,4096]{1,0:T(1,128)S(1)} fusion(bf16[1024,1]{0,1:T(2,128)(2,1)S(1)} %reshape.164, bf16[1024,4096]{1,0:T(8,128)(2,1)} %param.18), kind=kOutput, calls=%fused_computation.99 | convolution fusion | flops 8388608 | bytes 8407040 | tf_op jit(solution)/shard_map/dot_general | solution.py:789
  21.3 1.9 copy-done
  25.7 3.1 project.2
  31.4 8.0 %own_units.1 = (bf16[1024,2048]{1,0:T(8,128)(2,1)}, bf16[2048,1024]{1,0:T(8,128)(2,1)}) custom-call(s32[16]{0:T(128)} %copy-done.57, bf16[1024,4096]{1,0:T(8,128)(2,1)} %refs_2_.1, bf16[4096,1024]{1,0:T(8,128)(2,1)} %refs_3_.1, bf16[1024,4096]{1,0:T(8,128)(2,1)} %refs_2_.1, bf16[4096,1024]{1,0:T(8,128)(2,1)} %refs_3_.1), custom_call_target="tpu_custom_call" | custom-call | flops 1 | bytes 1 | tf_op jit(solution)/shard_map/own_units/pallas_call | solution.py:52
  45.8 4.2 %project.3 = (bf16[1024,1024]{1,0:T(8,128)(2,1)S(1)}, bf16[1024,1024]{1,0:T(8,128)(2,1)S(1)}, bf16[1024,1536]{1,0:T(8,128)(2,1)S(1)}) custom-call(s32[16]{0:T(128)S(1)} %copy-done.58, bf16[512,1024]{1,0:T(8,128)(2,1)} %collective-permute-done.3.a_ref, ...), custom_call_target="tpu_custom_call", output_to_operand_aliasing={{0}: (6, {}), {1}: (7, {}), {2}: (8, {})} | custom-call | flops 1 | bytes 1 | tf_op jit(solution)/shard_map/project/pallas_call | solution.py:52
  52.6 7.4 %attend_forward.2 = (bf16[1024,256]{1,0:T(8,128)(2,1)}, f32[1024,128]{1,0:T(8,128)S(1)}) custom-call(s32[16]{0:T(128)S(1)} %copy-done.58, bf16[1024,1536]{1,0:T(8,128)(2,1)S(1)} %get-tuple-element.252.q_ref.k_ref.v_ref, bf16[1024,1536]{1,0:T(8,128)(2,1)S(1)} %get-tuple-element.252.q_ref.k_ref.v_ref, bf16[1024,1536]{1,0:T(8,128)(2,1)S(1)} %get-tuple-element.252.q_ref.k_ref.v_ref), custom_call_target="tpu_custom_call" | custom-call | flops 1 | bytes 1 | tf_op jit(solution)/shard_map/attend_forward/pallas_call | solution.py:52
  61.3 7.4 %attend_forward.3 = (bf16[1024,256]{1,0:T(8,128)(2,1)}, f32[1024,128]{1,0:T(8,128)S(1)}) custom-call(s32[16]{0:T(128)S(1)} %copy-done.58, bf16[1024,1536]{1,0:T(8,128)(2,1)S(1)} %get-tuple-element.252.q_ref.k_ref.v_ref, bf16[1024,1536]{1,0:T(8,128)(2,1)S(1)} %get-tuple-element.252.q_ref.k_ref.v_ref, bf16[1024,1536]{1,0:T(8,128)(2,1)S(1)} %get-tuple-element.252.q_ref.k_ref.v_ref), custom_call_target="tpu_custom_call" | custom-call | flops 1 | bytes 1 | tf_op jit(solution)/shard_map/attend_forward/pallas_call | solution.py:52
  69.9 4.0 %assemble.1 = (bf16[1024,1024]{1,0:T(8,128)(2,1)S(1)}, bf16[1024,1024]{1,0:T(8,128)(2,1)S(1)}, f32[8,1024]{1,0:T(8,128)S(1)}) custom-call(s32[16]{0:T(128)S(1)} %copy-done.58, bf16[512,1024]{1,0:T(8,128)(2,1)} %bitcast.5.n1_ref, bf16[512,1024]{1,0:T(8,128)(2,1)} %collective-permute-done.5.n2_ref, bf16[512,1024]{1,0:T(8,128)(2,1)} %collective-permute-done.2.f1_ref, ...), custom_call_target="tpu_custom_call" | custom-call | flops 1 | bytes 1 | tf_op jit(solution)/shard_map/assemble/pallas_call | solution.py:52
  74.0 6.4 %mix_out.1 = (bf16[1024,1024]{1,0:T(8,128)(2,1)S(1)}, bf16[1024,1024]{1,0:T(8,128)(2,1)S(1)}, bf16[1024,1024]{1,0:T(8,128)(2,1)S(1)}) custom-call(s32[16]{0:T(128)S(1)} %copy-done.58, bf16[1024,256]{1,0:T(8,128)(2,1)} %get-tuple-element.265.refs_0_.o_ref, bf16[1024,256]{1,0:T(8,128)(2,1)} %get-tuple-element.266.refs_1_.o_ref, ...), custom_call_target="tpu_custom_call" | custom-call | flops 1 | bytes 1 | tf_op jit(solution)/shard_map/mix_out/pallas_call | solution.py:52
  81.7 9.1 %raise_up.1 = (bf16[1024,2048]{1,0:T(8,128)(2,1)S(1)}, bf16[1024,2048]{1,0:T(8,128)(2,1)S(1)}) custom-call(s32[16]{0:T(128)S(1)} %copy-done.58, bf16[1024,1024]{1,0:T(8,128)(2,1)S(1)} %get-tuple-element.272.act_ref.refs_0_, bf16[1024,2048]{1,0:T(8,128)(2,1)S(1)} %copy-done.5, f32[1,2048]{1,0:T(1,128)S(1)} %bitcast.58), custom_call_target="tpu_custom_call" | custom-call | flops 1 | bytes 1 | tf_op jit(solution)/shard_map/raise_up/pallas_call | solution.py:52
  90.9 11.4 %down_gradient.1 = (bf16[2048,512]{1,0:T(8,128)(2,1)}, bf16[2048,512]{1,0:T(8,128)(2,1)S(1)}) custom-call(s32[16]{0:T(128)S(1)} %copy-done.58, bf16[1024,2048]{1,0:T(8,128)(2,1)S(1)} %get-tuple-element.277.refs_0_.lhs_ref, bf16[1024,1024]{1,0:T(8,128)(2,1)S(1)} %get-tuple-element.278.refs_1_.g_ref), custom_call_target="tpu_custom_call" | custom-call | flops 1 | bytes 1 | tf_op jit(solution)/shard_map/down_gradient/pallas_call | solution.py:52
  102.3 1.9 collective-permute-start.11
  104.2 6.7 %raise_back.1 = (bf16[1024,2048]{1,0:T(8,128)(2,1)S(1)}, f32[1,2048]{1,0:T(1,128)S(1)}) custom-call(s32[16]{0:T(128)S(1)} %copy-done.58, bf16[1024,1024]{1,0:T(8,128)(2,1)S(1)} %get-tuple-element.278.refs_1_.g_ref, bf16[2048,1024]{1,0:T(8,128)(2,1)S(1)} %copy-done.4, bf16[1024,2048]{1,0:T(8,128)(2,1)S(1)} %get-tuple-element.283.der_ref), custom_call_target="tpu_custom_call" | custom-call | flops 1 | bytes 1 | tf_op jit(solution)/shard_map/raise_back/pallas_call | solution.py:52
  110.9 8.5 %up_gradient.1 = (bf16[512,2048]{1,0:T(8,128)(2,1)}, bf16[512,2048]{1,0:T(8,128)(2,1)S(1)}) custom-call(s32[16]{0:T(128)S(1)} %copy-done.58, bf16[1024,1024]{1,0:T(8,128)(2,1)S(1)} %get-tuple-element.272.act_ref.refs_0_, bf16[1024,2048]{1,0:T(8,128)(2,1)S(1)} %get-tuple-element.287.refs_1_.lhs_ref), custom_call_target="tpu_custom_call" | custom-call | flops 1 | bytes 1 | tf_op jit(solution)/shard_map/up_gradient/pallas_call | solution.py:52
  120.7 3.1 raise_input_back.2.a1_ref
  123.9 3.1 raise_input_back.3.a2_ref
  129.1 3.9 %lower.2 = bf16[512,1024]{1,0:T(8,128)(2,1)} custom-call(s32[16]{0:T(128)S(1)} %copy-done.58, bf16[1024,2048]{1,0:T(8,128)(2,1)S(1)} %get-tuple-element.277.refs_0_.lhs_ref, bf16[2048,1024]{1,0:T(8,128)(2,1)S(1)} %copy-done.4), custom_call_target="tpu_custom_call" | custom-call | flops 1 | bytes 1 | tf_op jit(solution)/shard_map/lower/pallas_call | solution.py:52
  132.9 3.1 lower.3.a_ref
  137.0 6.8 %dense_norm_back.1 = (bf16[1024,1024]{1,0:T(8,128)(2,1)S(1)}, bf16[1024,1024]{1,0:T(8,128)(2,1)S(1)}, bf16[1024,512]{1,0:T(8,128)(2,1)S(1)}, f32[8,1024]{1,0:T(8,128)S(1)}) custom-call(s32[16]{0:T(128)S(1)} %copy-done.58, bf16[512,1024]{1,0:T(8,128)(2,1)S(1)} %raise_input_back.2.a1_ref, bf16[512,1024]{1,0:T(8,128)(2,1)S(1)} %raise_input_back.3.a2_ref, ...), custom_call_target="tpu_custom_call" | custom-call | flops 1 | bytes 1 | tf_op jit(solution)/shard_map/dense_norm_back/pallas_call | solution.py:52
  145.2 15.1 %attend_backward.2 = (bf16[1024,256]{1,0:T(8,128)(2,1)S(1)}, bf16[1024,256]{1,0:T(8,128)(2,1)S(1)}, bf16[1024,256]{1,0:T(8,128)(2,1)S(1)}) custom-call(s32[16]{0:T(128)S(1)} %copy-done.58, bf16[1024,1536]{1,0:T(8,128)(2,1)S(1)} %get-tuple-element.252.q_ref.k_ref.v_ref, bf16[1024,512]{1,0:T(8,128)(2,1)S(1)} %get-tuple-element.304.g_ref, ...), custom_call_target="tpu_custom_call" | custom-call | flops 1 | bytes 1 | tf_op jit(solution)/shard_map/attend_backward/pallas_call | solution.py:52
  160.4 7.6 %in_gradient.2 = (bf16[512,1280]{1,0:T(8,128)(2,1)}, bf16[512,1280]{1,0:T(8,128)(2,1)S(1)}) custom-call(s32[16]{0:T(128)S(1)} %copy-done.58, bf16[1024,1024]{1,0:T(8,128)(2,1)S(1)} %copy-done.14, bf16[1024,1024]{1,0:T(8,128)(2,1)S(1)} %copy-done.51, bf16[1024,256]{1,0:T(8,128)(2,1)S(1)} %get-tuple-element.312.refs_2_.refs_0_, ...), custom_call_target="tpu_custom_call" | custom-call | flops 1 | bytes 1 | tf_op jit(solution)/shard_map/in_gradient/pallas_call | solution.py:52
  168.0 1.9 add_split.12
  175.9 14.7 %attend_backward.3 = (bf16[1024,256]{1,0:T(8,128)(2,1)S(1)}, bf16[1024,256]{1,0:T(8,128)(2,1)S(1)}, bf16[1024,256]{1,0:T(8,128)(2,1)S(1)}) custom-call(s32[16]{0:T(128)S(1)} %copy-done.58, bf16[1024,1536]{1,0:T(8,128)(2,1)S(1)} %get-tuple-element.252.q_ref.k_ref.v_ref, bf16[1024,512]{1,0:T(8,128)(2,1)S(1)} %copy-done.43, ...), custom_call_target="tpu_custom_call" | custom-call | flops 1 | bytes 1 | tf_op jit(solution)/shard_map/attend_backward/pallas_call | solution.py:52
  190.7 2.3 project_back.3
  193.1 2.3 project_back.4
  195.4 5.8 %in_gradient.3 = (bf16[512,768]{1,0:T(8,128)(2,1)}, bf16[512,768]{1,0:T(8,128)(2,1)S(1)}) custom-call(s32[16]{0:T(128)S(1)} %copy-done.58, bf16[1024,1024]{1,0:T(8,128)(2,1)S(1)} %copy-done.15, bf16[1024,256]{1,0:T(8,128)(2,1)S(1)} %get-tuple-element.329.refs_1_, bf16[1024,256]{1,0:T(8,128)(2,1)S(1)} %get-tuple-element.330.refs_3_.refs_2_, ...), custom_call_target="tpu_custom_call" | custom-call | flops 1 | bytes 1 | tf_op jit(solution)/shard_map/in_gradient/pallas_call | solution.py:52
  202.1 3.6 add_split.13
  216.8 2.6 project_back.5.a_ref
  219.5 2.3 add_branch.1
  221.8 2.3 add_split.14
  224.2 1.8 collective-permute-start.14
  225.9 4.8 %attend_norm_back.1 = (bf16[512,1024]{1,0:T(8,128)(2,1)}, f32[8,1024]{1,0:T(8,128)S(1)}) custom-call(s32[16]{0:T(128)S(1)} %copy-done.59, bf16[512,1024]{1,0:T(8,128)(2,1)S(1)} %project_back.5.a_ref, bf16[256,1024]{1,0:T(8,128)(2,1)} %collective-permute-done.16.b1_ref, bf16[256,1024]{1,0:T(8,128)(2,1)} %collective-permute-done.17.b2_ref, ...), custom_call_target="tpu_custom_call" | custom-call | flops 1 | bytes 1 | tf_op jit(solution)/shard_map/attend_norm_back/pallas_call | solution.py:52
  237.1 2.1 add_split.15
  242.5 4.9 %collective-permute-done.21.b1_ref.b2_ref = bf16[256,2048]{1,0:T(8,128)(2,1)} collective-permute-done((bf16[256,2048]{1,0:T(8,128)(2,1)}, bf16[256,2048]{1,0:T(8,128)(2,1)}, u32[]{:S(2)}, u32[]{:S(2)}) %collective-permute-start.21) | collective-permute-done | bytes 1048608 | tf_op jit(solution)/shard_map/ppermute | solution.py:736
  247.3 2.0 add_split.16
  249.4 1.8 add_split.17
  253.0 2.6 collective-permute-start.25
  257.0 2.8 select_bitcast_fusion
  259.8 19.1 %collective-permute-done.25.b1_ref.b2_ref = bf16[512,512]{1,0:T(8,128)(2,1)S(1)} collective-permute-done((bf16[512,512]{1,0:T(8,128)(2,1)}, bf16[512,512]{1,0:T(8,128)(2,1)S(1)}, u32[]{:S(2)}, u32[]{:S(2)}) %collective-permute-start.25) | collective-permute-done | bytes 524320 | tf_op jit(solution)/shard_map/ppermute | solution.py:736
  280.5 3.3 collective-permute-start.30
  285.2 7.1 %collective-permute-done.27 = bf16[256,512]{1,0:T(8,128)(2,1)S(1)} collective-permute-done((bf16[256,512]{1,0:T(8,128)(2,1)S(1)}, bf16[256,512]{1,0:T(8,128)(2,1)S(1)}, u32[]{:S(2)}, u32[]{:S(2)}) %collective-permute-start.27) | collective-permute-done | bytes 262176 | tf_op jit(solution)/shard_map/ppermute | solution.py:688
  293.1 23.6 %collective-permute-done.30.b1_ref.b2_ref = bf16[128,2048]{1,0:T(8,128)(2,1)S(1)} collective-permute-done((bf16[128,2048]{1,0:T(8,128)(2,1)S(1)}, bf16[128,2048]{1,0:T(8,128)(2,1)S(1)}, u32[]{:S(2)}, u32[]{:S(2)}) %collective-permute-start.30) | collective-permute-done | bytes 524320 | tf_op jit(solution)/shard_map/ppermute | solution.py:736
  319.1 4.6 %collective-permute-done.31.b1_ref.b2_ref = bf16[128,1280]{1,0:T(8,128)(2,1)S(1)} collective-permute-done((bf16[128,1280]{1,0:T(8,128)(2,1)S(1)}, bf16[128,1280]{1,0:T(8,128)(2,1)S(1)}, u32[]{:S(2)}, u32[]{:S(2)}) %collective-permute-start.31) | collective-permute-done | bytes 327712 | tf_op jit(solution)/shard_map/ppermute | solution.py:736
  334.1 6.9 %collective-permute-done.33.b1_ref.b2_ref = bf16[128,768]{1,0:T(8,128)(2,1)S(1)} collective-permute-done((bf16[128,768]{1,0:T(8,128)(2,1)S(1)}, bf16[128,768]{1,0:T(8,128)(2,1)S(1)}, u32[]{:S(2)}, u32[]{:S(2)}) %collective-permute-start.33) | collective-permute-done | bytes 196640 | tf_op jit(solution)/shard_map/ppermute | solution.py:736
  348.9 5.4 %collective-permute-done.37.refs_1_ = bf16[2,64,1280]{2,1,0:T(8,128)(2,1)S(1)} collective-permute-done((bf16[2,64,1280]{2,1,0:T(8,128)(2,1)S(1)}, bf16[2,64,1280]{2,1,0:T(8,128)(2,1)S(1)}, u32[]{:S(2)}, u32[]{:S(2)}) %collective-permute-start.37) | collective-permute-done | bytes 327712 | tf_op jit(solution)/shard_map/ppermute | solution.py:691
  354.2 3.1 collective-permute-done.39.refs_3_
  (312 shorter events, 84.4 us)
Async XLA Ops:
  0.6 38.8 %collective-permute-start.3 = (bf16[512,1024]{1,0:T(8,128)(2,1)}, bf16[512,1024]{1,0:T(8,128)(2,1)}, u32[]{:S(2)}, u32[]{:S(2)}) collective-permute-start(bf16[512,1024]{1,0:T(8,128)(2,1)} %bitcast.45), channel_id=1, source_target_pairs={{2,1},{1,0},{6,5},{5,4},{10,9},{9,8},{14,13},{13,12},{18,17},{17,1... | collective-permute-start | bytes 3145736 | tf_op jit(solution)/shard_map/ppermute | solution.py:716
  1.9 18.4 %collective-permute-start.1 = (bf16[512,1024]{1,0:T(8,128)(2,1)}, bf16[512,1024]{1,0:T(8,128)(2,1)S(1)}, u32[]{:S(2)}, u32[]{:S(2)}) collective-permute-start(bf16[512,1024]{1,0:T(8,128)(2,1)} %bitcast.46), channel_id=1, source_target_pairs={{0,2},{2,0},{4,6},{6,4},{8,10},{10,8},{12,14},{14,12},{16,18},{18,... | collective-permute-start | bytes 3145736 | tf_op jit(solution)/shard_map/ppermute | solution.py:687
  8.0 5.6 %collective-permute-start = (s32[2]{0:T(128)S(1)}, s32[2]{0:T(128)S(1)}, u32[]{:S(2)}, u32[]{:S(2)}) collective-permute-start(s32[2]{0:T(128)S(1)} %pad_add_fusion), channel_id=1, source_target_pairs={{0,2},{2,0},{4,6},{6,4},{8,10},{10,8},{12,14},{14,12},{16,18},{18,... | collective-permute-start | bytes 32 | tf_op jit(solution)/shard_map/ppermute | solution.py:687
  39.5 3.1 collective-permute-start.4
  40.0 20.8 %collective-permute-start.2 = (bf16[512,1024]{1,0:T(8,128)(2,1)}, bf16[512,1024]{1,0:T(8,128)(2,1)}, u32[]{:S(2)}, u32[]{:S(2)}) collective-permute-start(bf16[512,1024]{1,0:T(8,128)(2,1)} %bitcast.5.n1_ref), channel_id=1, source_target_pairs={{2,1},{1,0},{6,5},{5,4},{10,9},{9,8},{14,13},{13,12},{18,17},{17,1... | collective-permute-start | bytes 3145736 | tf_op jit(solution)/shard_map/ppermute | solution.py:716
  41.5 28.4 %collective-permute-start.5 = (bf16[512,1024]{1,0:T(8,128)(2,1)}, bf16[512,1024]{1,0:T(8,128)(2,1)}, u32[]{:S(2)}, u32[]{:S(2)}) collective-permute-start(bf16[512,1024]{1,0:T(8,128)(2,1)} %bitcast.5.n1_ref), channel_id=1, source_target_pairs={{0,2},{2,0},{4,6},{6,4},{8,10},{10,8},{12,14},{14,12},{16,18},{18,... | collective-permute-start | bytes 3145736 | tf_op jit(solution)/shard_map/ppermute | solution.py:687
  60.8 9.1 %collective-permute-start.6 = (bf16[512,1024]{1,0:T(8,128)(2,1)}, bf16[512,1024]{1,0:T(8,128)(2,1)}, u32[]{:S(2)}, u32[]{:S(2)}) collective-permute-start(bf16[512,1024]{1,0:T(8,128)(2,1)} %collective-permute-done.2.f1_ref), channel_id=1, source_target_pairs={{0,2},{2,0},{4,6},{6,4},{8,10},{10,8},{12,14},{14,12},{16,18},{18,... | collective-permute-start | bytes 3145736 | tf_op jit(solution)/shard_map/ppermute | solution.py:687
  61.0 12.8 %collective-permute-start.7 = (bf16[1024,256]{1,0:T(8,128)(2,1)}, bf16[1024,256]{1,0:T(8,128)(2,1)}, u32[]{:S(2)}, u32[]{:S(2)}) collective-permute-start(bf16[1024,256]{1,0:T(8,128)(2,1)} %get-tuple-element.265.refs_0_.o_ref), channel_id=1, source_target_pairs={{0,2},{2,0},{4,6},{6,4},{8,10},{10,8},{12,14},{14,12},{16,18},{18,... | collective-permute-start | bytes 1572872 | tf_op jit(solution)/shard_map/ppermute | solution.py:687
  69.5 4.4 %collective-permute-start.8 = (bf16[1024,256]{1,0:T(8,128)(2,1)}, bf16[1024,256]{1,0:T(8,128)(2,1)}, u32[]{:S(2)}, u32[]{:S(2)}) collective-permute-start(bf16[1024,256]{1,0:T(8,128)(2,1)} %get-tuple-element.266.refs_1_.o_ref), channel_id=1, source_target_pairs={{0,2},{2,0},{4,6},{6,4},{8,10},{10,8},{12,14},{14,12},{16,18},{18,... | collective-permute-start | bytes 1572872 | tf_op jit(solution)/shard_map/ppermute | solution.py:687
  81.7 55.3 %copy-start.17 = (bf16[1024,1024]{1,0:T(8,128)(2,1)}, bf16[1024,1024]{1,0:T(8,128)(2,1)S(1)}, u32[]{:S(2)}) copy-start(bf16[1024,1024]{1,0:T(8,128)(2,1)S(1)} %get-tuple-element.297.res_ref) | copy-start | bytes 6291460
  102.3 65.7 %collective-permute-start.11 = (bf16[2048,512]{1,0:T(8,128)(2,1)}, bf16[2048,512]{1,0:T(8,128)(2,1)S(1)}, u32[]{:S(2)}, u32[]{:S(2)}) collective-permute-start(bf16[2048,512]{1,0:T(8,128)(2,1)} %get-tuple-element.320), channel_id=1, source_target_pairs={{0,1},{1,0},{2,3},{3,2},{4,5},{5,4},{6,7},{7,6},{8,9},{9,8},{10,11... | collective-permute-start | bytes 6291464 | tf_op jit(solution)/shard_map/ppermute | solution.py:691
  127.0 10.0 %collective-permute-start.10 = (bf16[512,1024]{1,0:T(8,128)(2,1)S(1)}, bf16[512,1024]{1,0:T(8,128)(2,1)S(1)}, u32[]{:S(2)}, u32[]{:S(2)}) collective-permute-start(bf16[512,1024]{1,0:T(8,128)(2,1)S(1)} %raise_input_back.3.a2_ref), channel_id=1, source_target_pairs={{0,2},{2,0},{4,6},{6,4},{8,10},{10,8},{12,14},{14,12},{16,18},{18,... | collective-permute-start | bytes 3145736 | tf_op jit(solution)/shard_map/ppermute | solution.py:687
  127.1 9.9 %collective-permute-start.9 = (bf16[512,1024]{1,0:T(8,128)(2,1)S(1)}, bf16[512,1024]{1,0:T(8,128)(2,1)S(1)}, u32[]{:S(2)}, u32[]{:S(2)}) collective-permute-start(bf16[512,1024]{1,0:T(8,128)(2,1)S(1)} %raise_input_back.2.a1_ref), channel_id=1, source_target_pairs={{0,2},{2,0},{4,6},{6,4},{8,10},{10,8},{12,14},{14,12},{16,18},{18,... | collective-permute-start | bytes 3145736 | tf_op jit(solution)/shard_map/ppermute | solution.py:687
  127.6 74.5 %collective-permute-start.12 = (bf16[512,2048]{1,0:T(8,128)(2,1)}, bf16[512,2048]{1,0:T(8,128)(2,1)}, u32[]{:S(2)}, u32[]{:S(2)}) collective-permute-start(bf16[512,2048]{1,0:T(8,128)(2,1)} %get-tuple-element.338), channel_id=1, source_target_pairs={{0,4},{2,6},{4,0},{6,2},{8,12},{10,14},{12,8},{14,10},{16,20},{18,... | collective-permute-start | bytes 6291464 | tf_op jit(solution)/shard_map/ppermute | solution.py:688
  137.0 70.1 %collective-permute-start.13 = (bf16[512,1024]{1,0:T(8,128)(2,1)}, bf16[512,1024]{1,0:T(8,128)(2,1)}, u32[]{:S(2)}, u32[]{:S(2)}) collective-permute-start(bf16[512,1024]{1,0:T(8,128)(2,1)} %lower.2), channel_id=1, source_target_pairs={{0,2},{2,0},{4,6},{6,4},{8,10},{10,8},{12,14},{14,12},{16,18},{18,... | collective-permute-start | bytes 3145736 | tf_op jit(solution)/shard_map/ppermute | solution.py:687
  145.2 15.2 %copy-start.42 = (bf16[1024,512]{1,0:T(8,128)(2,1)}, bf16[1024,512]{1,0:T(8,128)(2,1)S(1)}, u32[]{:S(2)}) copy-start(bf16[1024,512]{1,0:T(8,128)(2,1)S(1)} %get-tuple-element.304.g_ref) | copy-start | bytes 3145732
  145.2 15.2 %copy-start.70 = (f32[8,1024]{1,0:T(8,128)}, f32[8,1024]{1,0:T(8,128)S(1)}, u32[]{:S(2)}) copy-start(f32[8,1024]{1,0:T(8,128)S(1)} %get-tuple-element.359) | copy-start | bytes 98308
  145.2 15.2 %copy-start.14 = (bf16[1024,1024]{1,0:T(8,128)(2,1)S(1)}, bf16[1024,1024]{1,0:T(8,128)(2,1)}, u32[]{:S(2)}) copy-start(bf16[1024,1024]{1,0:T(8,128)(2,1)} %copy-done.13) | copy-start | bytes 6291460
  145.2 15.2 %copy-start.51 = (bf16[1024,1024]{1,0:T(8,128)(2,1)S(1)}, bf16[1024,1024]{1,0:T(8,128)(2,1)}, u32[]{:S(2)}) copy-start(bf16[1024,1024]{1,0:T(8,128)(2,1)} %copy-done.50) | copy-start | bytes 6291460
  170.9 36.8 %collective-permute-start.15 = (bf16[1024,512]{1,0:T(8,128)(2,1)}, bf16[1024,512]{1,0:T(8,128)(2,1)}, u32[]{:S(2)}, u32[]{:S(2)}) collective-permute-start(bf16[1024,512]{1,0:T(8,128)(2,1)} %get-tuple-element.348), channel_id=1, source_target_pairs={{0,8},{2,10},{4,12},{6,14},{8,0},{10,2},{12,4},{14,6},{16,24},{18,... | collective-permute-start | bytes 3145736 | tf_op jit(solution)/shard_map/ppermute | solution.py:736
  172.5 62.2 %collective-permute-start.19 = (bf16[512,1280]{1,0:T(8,128)(2,1)}, bf16[512,1280]{1,0:T(8,128)(2,1)}, u32[]{:S(2)}, u32[]{:S(2)}) collective-permute-start(bf16[512,1280]{1,0:T(8,128)(2,1)} %get-tuple-element.364), channel_id=1, source_target_pairs={{0,8},{2,10},{4,12},{6,14},{8,0},{10,2},{12,4},{14,6},{16,24},{18,... | collective-permute-start | bytes 3932168 | tf_op jit(solution)/shard_map/ppermute | solution.py:736
  206.6 17.5 %collective-permute-start.17 = (bf16[256,1024]{1,0:T(8,128)(2,1)}, bf16[256,1024]{1,0:T(8,128)(2,1)}, u32[]{:S(2)}, u32[]{:S(2)}) collective-permute-start(bf16[256,1024]{1,0:T(8,128)(2,1)} %project_back.4), channel_id=1, source_target_pairs={{0,2},{2,0},{4,6},{6,4},{8,10},{10,8},{12,14},{14,12},{16,18},{18,... | collective-permute-start | bytes 1572872 | tf_op jit(solution)/shard_map/ppermute | solution.py:687
  206.6 19.3 %collective-permute-start.16 = (bf16[256,1024]{1,0:T(8,128)(2,1)}, bf16[256,1024]{1,0:T(8,128)(2,1)}, u32[]{:S(2)}, u32[]{:S(2)}) collective-permute-start(bf16[256,1024]{1,0:T(8,128)(2,1)} %project_back.3), channel_id=1, source_target_pairs={{0,2},{2,0},{4,6},{6,4},{8,10},{10,8},{12,14},{14,12},{16,18},{18,... | collective-permute-start | bytes 1572872 | tf_op jit(solution)/shard_map/ppermute | solution.py:687
  207.1 42.2 %collective-permute-start.22 = (bf16[512,768]{1,0:T(8,128)(2,1)}, bf16[512,768]{1,0:T(8,128)(2,1)}, u32[]{:S(2)}, u32[]{:S(2)}) collective-permute-start(bf16[512,768]{1,0:T(8,128)(2,1)} %get-tuple-element.376), channel_id=1, source_target_pairs={{0,4},{2,6},{4,0},{6,2},{8,12},{10,14},{12,8},{14,10},{16,20},{18,... | collective-permute-start | bytes 2359304 | tf_op jit(solution)/shard_map/ppermute | solution.py:688
  207.7 39.7 %collective-permute-start.21 = (bf16[256,2048]{1,0:T(8,128)(2,1)}, bf16[256,2048]{1,0:T(8,128)(2,1)}, u32[]{:S(2)}, u32[]{:S(2)}) collective-permute-start(bf16[256,2048]{1,0:T(8,128)(2,1)} %get-tuple-element.371), channel_id=1, source_target_pairs={{0,8},{2,10},{4,12},{6,14},{8,0},{10,2},{12,4},{14,6},{16,24},{18,... | collective-permute-start | bytes 3145736 | tf_op jit(solution)/shard_map/ppermute | solution.py:736
  224.2 32.9 %collective-permute-start.14 = (bf16[512,1024]{1,0:T(8,128)(2,1)S(1)}, bf16[512,1024]{1,0:T(8,128)(2,1)}, u32[]{:S(2)}, u32[]{:S(2)}) collective-permute-start(bf16[512,1024]{1,0:T(8,128)(2,1)S(1)} %add_branch.1), channel_id=1, source_target_pairs={{2,1},{1,2},{6,5},{5,6},{10,9},{9,10},{14,13},{13,14},{18,17},{17,... | collective-permute-start | bytes 3145736 | tf_op jit(solution)/shard_map/ppermute | solution.py:728
  230.8 26.3 %collective-permute-start.23 = (bf16[512,1024]{1,0:T(8,128)(2,1)}, bf16[512,1024]{1,0:T(8,128)(2,1)}, u32[]{:S(2)}, u32[]{:S(2)}) collective-permute-start(bf16[512,1024]{1,0:T(8,128)(2,1)} %get-tuple-element.382), channel_id=1, source_target_pairs={{2,1},{1,2},{6,5},{5,6},{10,9},{9,10},{14,13},{13,14},{18,17},{17,... | collective-permute-start | bytes 3145736 | tf_op jit(solution)/shard_map/ppermute | solution.py:728
  234.7 4.6 %collective-permute-start.18 = (f32[13,1024]{1,0:T(8,128)}, f32[13,1024]{1,0:T(8,128)S(1)}, u32[]{:S(2)}, u32[]{:S(2)}) collective-permute-start(f32[13,1024]{1,0:T(8,128)} %concatenate.34), channel_id=1, source_target_pairs={{0,2},{2,0},{4,6},{6,4},{8,10},{10,8},{12,14},{14,12},{16,18},{18,... | collective-permute-start | bytes 159752 | tf_op jit(solution)/shard_map/ppermute | solution.py:687
  240.9 11.8 %collective-permute-start.20 = (bf16[13,1024]{1,0:T(8,128)(2,1)S(1)}, bf16[13,1024]{1,0:T(8,128)(2,1)S(1)}, u32[]{:S(2)}, u32[]{:S(2)}) collective-permute-start(bf16[13,1024]{1,0:T(8,128)(2,1)S(1)} %add.140), channel_id=1, source_target_pairs={{0,4},{2,6},{4,0},{6,2},{8,12},{10,14},{12,8},{14,10},{16,20},{18,... | collective-permute-start | bytes 79880 | tf_op jit(solution)/shard_map/ppermute | solution.py:688
  252.8 4.2 %collective-permute-start.24 = (bf16[18,1024]{1,0:T(8,128)(2,1)S(1)}, bf16[18,1024]{1,0:T(8,128)(2,1)S(1)}, u32[]{:S(2)}, u32[]{:S(2)}) collective-permute-start(bf16[18,1024]{1,0:T(8,128)(2,1)S(1)} %pad_maximum_fusion.7), channel_id=1, source_target_pairs={{0,1},{1,0},{2,3},{3,2},{4,5},{5,4},{6,7},{7,6},{8,9},{9,8},{10,11... | collective-permute-start | bytes 110600 | tf_op jit(solution)/shard_map/ppermute | solution.py:691
  253.0 25.8 %collective-permute-start.25 = (bf16[512,512]{1,0:T(8,128)(2,1)}, bf16[512,512]{1,0:T(8,128)(2,1)S(1)}, u32[]{:S(2)}, u32[]{:S(2)}) collective-permute-start(bf16[512,512]{1,0:T(8,128)(2,1)} %copy-done.74), channel_id=1, source_target_pairs={{0,16},{2,18},{4,20},{6,22},{8,24},{10,26},{12,28},{14,30},{16,0},... | collective-permute-start | bytes 1572872 | tf_op jit(solution)/shard_map/ppermute | solution.py:736
  255.6 28.2 %collective-permute-start.28 = (bf16[256,1280]{1,0:T(8,128)(2,1)}, bf16[256,1280]{1,0:T(8,128)(2,1)S(1)}, u32[]{:S(2)}, u32[]{:S(2)}) collective-permute-start(bf16[256,1280]{1,0:T(8,128)(2,1)} %copy-done.73), channel_id=1, source_target_pairs={{0,4},{2,6},{4,0},{6,2},{8,12},{10,14},{12,8},{14,10},{16,20},{18,... | collective-permute-start | bytes 1966088 | tf_op jit(solution)/shard_map/ppermute | solution.py:688
  257.0 21.9 %copy-start.61 = (s32[16]{0:T(128)S(1)}, s32[16]{0:T(128)}, u32[]{:S(2)}) copy-start(s32[16]{0:T(128)} %copy-done.57) | copy-start | bytes 196
  259.8 20.7 %copy-start.76 = (bf16[128,2048]{1,0:T(8,128)(2,1)S(1)}, bf16[128,2048]{1,0:T(8,128)(2,1)}, u32[]{:S(2)}) copy-start(bf16[128,2048]{1,0:T(8,128)(2,1)} %copy-done.75) | copy-start | bytes 1572868
  279.6 5.6 %collective-permute-start.26 = (bf16[28,1024]{1,0:T(8,128)(2,1)S(1)}, bf16[28,1024]{1,0:T(8,128)(2,1)S(1)}, u32[]{:S(2)}, u32[]{:S(2)}) collective-permute-start(bf16[28,1024]{1,0:T(8,128)(2,1)S(1)} %pad_maximum_fusion.6), channel_id=1, source_target_pairs={{0,8},{2,10},{4,12},{6,14},{8,0},{10,2},{12,4},{14,6},{16,24},{18,... | collective-permute-start | bytes 172040 | tf_op jit(solution)/shard_map/ppermute | solution.py:736
  280.5 36.2 %collective-permute-start.30 = (bf16[128,2048]{1,0:T(8,128)(2,1)S(1)}, bf16[128,2048]{1,0:T(8,128)(2,1)S(1)}, u32[]{:S(2)}, u32[]{:S(2)}) collective-permute-start(bf16[128,2048]{1,0:T(8,128)(2,1)S(1)} %copy-done.76), channel_id=1, source_target_pairs={{0,16},{2,18},{4,20},{6,22},{8,24},{10,26},{12,28},{14,30},{16,0},... | collective-permute-start | bytes 1572872 | tf_op jit(solution)/shard_map/ppermute | solution.py:736
  284.5 7.7 %collective-permute-start.27 = (bf16[256,512]{1,0:T(8,128)(2,1)S(1)}, bf16[256,512]{1,0:T(8,128)(2,1)S(1)}, u32[]{:S(2)}, u32[]{:S(2)}) collective-permute-start(bf16[256,512]{1,0:T(8,128)(2,1)S(1)} %get-tuple-element.394), channel_id=1, source_target_pairs={{0,4},{2,6},{4,0},{6,2},{8,12},{10,14},{12,8},{14,10},{16,20},{18,... | collective-permute-start | bytes 786440 | tf_op jit(solution)/shard_map/ppermute | solution.py:688
  285.1 38.6 %collective-permute-start.31 = (bf16[128,1280]{1,0:T(8,128)(2,1)S(1)}, bf16[128,1280]{1,0:T(8,128)(2,1)S(1)}, u32[]{:S(2)}, u32[]{:S(2)}) collective-permute-start(bf16[128,1280]{1,0:T(8,128)(2,1)S(1)} %get-tuple-element.411), channel_id=1, source_target_pairs={{0,16},{2,18},{4,20},{6,22},{8,24},{10,26},{12,28},{14,30},{16,0},... | collective-permute-start | bytes 983048 | tf_op jit(solution)/shard_map/ppermute | solution.py:736
  292.3 32.8 %collective-permute-start.29 = (bf16[48,1024]{1,0:T(8,128)(2,1)S(1)}, bf16[48,1024]{1,0:T(8,128)(2,1)S(1)}, u32[]{:S(2)}, u32[]{:S(2)}) collective-permute-start(bf16[48,1024]{1,0:T(8,128)(2,1)S(1)} %pad_maximum_fusion.4), channel_id=1, source_target_pairs={{0,16},{2,18},{4,20},{6,22},{8,24},{10,26},{12,28},{14,30},{16,0},... | collective-permute-start | bytes 294920 | tf_op jit(solution)/shard_map/ppermute | solution.py:736
  292.7 33.0 %collective-permute-start.32 = (bf16[256,768]{1,0:T(8,128)(2,1)S(1)}, bf16[256,768]{1,0:T(8,128)(2,1)S(1)}, u32[]{:S(2)}, u32[]{:S(2)}) collective-permute-start(bf16[256,768]{1,0:T(8,128)(2,1)S(1)} %copy-done.78), channel_id=1, source_target_pairs={{0,8},{2,10},{4,12},{6,14},{8,0},{10,2},{12,4},{14,6},{16,24},{18,... | collective-permute-start | bytes 1179656 | tf_op jit(solution)/shard_map/ppermute | solution.py:736
  317.4 14.0 %collective-permute-start.34 = (bf16[64,2048]{1,0:T(8,128)(2,1)S(1)}, bf16[64,2048]{1,0:T(8,128)(2,1)}, u32[]{:S(2)}, u32[]{:S(2)}) collective-permute-start(bf16[64,2048]{1,0:T(8,128)(2,1)S(1)} %get-tuple-element.431), channel_id=1, source_target_pairs={{0,2},{2,0},{4,6},{6,4},{8,10},{10,8},{12,14},{14,12},{16,18},{18,... | collective-permute-start | bytes 786440 | tf_op jit(solution)/shard_map/ppermute | solution.py:687
  317.4 27.2 %collective-permute-start.40 = (bf16[256,512]{1,0:T(8,128)(2,1)S(1)}, bf16[256,512]{1,0:T(8,128)(2,1)S(1)}, u32[]{:S(2)}, u32[]{:S(2)}) collective-permute-start(bf16[256,512]{1,0:T(8,128)(2,1)S(1)} %add_convert_fusion), channel_id=1, source_target_pairs={{0,1},{1,0},{2,3},{3,2},{4,5},{5,4},{6,7},{7,6},{8,9},{9,8},{10,11... | collective-permute-start | bytes 786440 | tf_op jit(solution)/shard_map/ppermute | solution.py:691
  324.3 17.4 %collective-permute-start.36 = (bf16[64,1280]{1,0:T(8,128)(2,1)S(1)}, bf16[64,1280]{1,0:T(8,128)(2,1)S(1)}, u32[]{:S(2)}, u32[]{:S(2)}) collective-permute-start(bf16[64,1280]{1,0:T(8,128)(2,1)S(1)} %get-tuple-element.434), channel_id=1, source_target_pairs={{0,2},{2,0},{4,6},{6,4},{8,10},{10,8},{12,14},{14,12},{16,18},{18,... | collective-permute-start | bytes 491528 | tf_op jit(solution)/shard_map/ppermute | solution.py:687
  329.3 11.7 %collective-permute-start.33 = (bf16[128,768]{1,0:T(8,128)(2,1)S(1)}, bf16[128,768]{1,0:T(8,128)(2,1)S(1)}, u32[]{:S(2)}, u32[]{:S(2)}) collective-permute-start(bf16[128,768]{1,0:T(8,128)(2,1)S(1)} %get-tuple-element.426), channel_id=1, source_target_pairs={{0,16},{2,18},{4,20},{6,22},{8,24},{10,26},{12,28},{14,30},{16,0},... | collective-permute-start | bytes 589832 | tf_op jit(solution)/shard_map/ppermute | solution.py:736
  332.4 14.8 %collective-permute-start.35 = (bf16[2,64,2048]{2,1,0:T(8,128)(2,1)S(1)}, bf16[2,64,2048]{2,1,0:T(8,128)(2,1)S(1)}, u32[]{:S(2)}, u32[]{:S(2)}) collective-permute-start(bf16[2,64,2048]{2,1,0:T(8,128)(2,1)S(1)} %pad_maximum_fusion.refs_0_), channel_id=1, source_target_pairs={{0,1},{1,0},{2,3},{3,2},{4,5},{5,4},{6,7},{7,6},{8,9},{9,8},{10,11... | collective-permute-start | bytes 1572872 | tf_op jit(solution)/shard_map/ppermute | solution.py:691
  341.6 1.8 collective-permute-start.38
  341.7 12.5 %collective-permute-start.37 = (bf16[2,64,1280]{2,1,0:T(8,128)(2,1)S(1)}, bf16[2,64,1280]{2,1,0:T(8,128)(2,1)S(1)}, u32[]{:S(2)}, u32[]{:S(2)}) collective-permute-start(bf16[2,64,1280]{2,1,0:T(8,128)(2,1)S(1)} %pad_maximum_fusion.1.refs_0_), channel_id=1, source_target_pairs={{0,1},{1,0},{2,3},{3,2},{4,5},{5,4},{6,7},{7,6},{8,9},{9,8},{10,11... | collective-permute-start | bytes 983048 | tf_op jit(solution)/shard_map/ppermute | solution.py:691
  343.4 13.9 %collective-permute-start.39 = (bf16[2,64,768]{2,1,0:T(8,128)(2,1)S(1)}, bf16[2,64,768]{2,1,0:T(8,128)(2,1)S(1)}, u32[]{:S(2)}, u32[]{:S(2)}) collective-permute-start(bf16[2,64,768]{2,1,0:T(8,128)(2,1)S(1)} %pad_maximum_fusion.2.refs_2_), channel_id=1, source_target_pairs={{0,1},{1,0},{2,3},{3,2},{4,5},{5,4},{6,7},{7,6},{8,9},{9,8},{10,11... | collective-permute-start | bytes 589832 | tf_op jit(solution)/shard_map/ppermute | solution.py:691
  (79 other events, 386.8 us)
